TPU v7x, 32 devices: a whole 2x2x4 slice. The times are simulated.
32 devices in a mesh: ctx: 8 (over z, y), kv: 4 (over x, core).
Axes of the slice: x: 2, y: 2, z: 4, core: 2. Of those that a mesh axis runs over, the one named last changes fastest.
Arguments:
- query: bfloat16 [2, 1024, 8192], P(None, 'ctx', 'kv')
- kv_rows: bfloat16 [2, 1024, 2048], P(None, 'ctx', 'kv')
- keep: int32 [2, 8, 8, 512], P(None, 'ctx', 'kv'), may hold values from 0 to 639, as said below
- dest: int32 [8192, 1], P('ctx'), may hold values from 0 to 31; in each aligned block of 1024 rows (0 to 1023, 1024 to 2047, ...) at most 64 rows name the same one
- offsets: int32 [2], replicated, may hold values from 0 to 6, as said below
Outputs:
- attention: bfloat16 [2, 1024, 8192], P(None, 'ctx', 'kv')
- row_scores: float32 [2, 8, 5120], P(None, 'kv', 'ctx')
- owner_cache: bfloat16 [16384, 2048], P(('ctx', 'kv'))
Inputs may be any that keep to these rules, and one draw needn't show every extreme that they name: `keep`: each list holds 512 distinct indices in increasing order; an index below 512 names a cache slot, an index k of 512 or more names span row k - 512. `dest`: among the 1024 rows of one context shard no owner is named more than 64 times; owner o is the device at position o in the ctx-major order of ctx and kv. `offsets`: one prompt starts at the first shard and another prompt at the second-to-last shard.
All inputs are finite; a program needn't handle non-finite values.
Results may differ from a plain program's by a relative error of at most 0.0049.
Values may be sent and summed in bfloat16 or wider, within the bound.
No kernel may reach another device: no remote copies, remote signals or barrier semaphores. Data moves between devices by JAX's collectives and lax.ppermute only.
A program may use at most 192 MiB of HBM per device.

v0:
```python
import functools
import math

import jax
import jax.numpy as jnp
from jax import lax
from jax.experimental import pallas as pl
from jax.experimental.pallas import tpu as pltpu
from jax.sharding import PartitionSpec as P

HEAD = 128
WIDTH = 2 * HEAD
LANES = 128
VMEM_BYTES = 56 * 1024 * 1024
PLANE_BYTES = 28 * 1024 * 1024
NOTES = 16
BANDS = 4


def look_up(state, keep, fresh):
    tiles = state.shape[1] // LANES
    parts = []
    for tile in range(tiles):
        wanted = keep[:, tile * LANES : (tile + 1) * LANES]
        high = wanted >> 7
        low = wanted & 127
        found = jnp.where(high >= tiles, fresh + wanted - state.shape[1], 0)
        for source in range(tiles):
            held = state[:, source * LANES : (source + 1) * LANES]
            moved = jnp.take_along_axis(held, low, axis=1, mode="promise_in_bounds")
            found = jnp.where(high == source, moved, found)
        parts.append(found)
    return jnp.concatenate(parts, axis=1)


def split(state):
    both = jnp.concatenate([state >> 7, state & 127], axis=0)
    return both.astype(jnp.float32).astype(jnp.bfloat16)


def index_kernel(
    where_ref, keep_early_ref, keep_late_ref, dest_ref, slot_ref, row_ref, column_ref, coded
):
    shards, heads, cache = keep_early_ref.shape
    cap = slot_ref.shape[0] // shards
    span = LANES
    early, mine, me = where_ref[0], where_ref[1], where_ref[2]
    empty = jnp.minimum(keep_early_ref[0], 0)

    def follow(shard, carry):
        state, own = carry
        own = jnp.where(shard == mine, state, own)
        state = look_up(state, keep_early_ref[shard], shard * span + 1)
        coded[shard] = split(state)
        return state, own

    _, own_early = lax.fori_loop(0, shards, follow, (empty, empty), unroll=shards <= 8)
    base = shards * span + 1
    late_first = look_up(empty, keep_late_ref[0], base)
    late_second = look_up(late_first, keep_late_ref[1], base + span)
    own_late = jnp.where(mine == shards - 1, late_first, 0)
    for index, own in enumerate((own_early, own_late)):
        row_ref[index] = own
        column_ref[index] = jnp.transpose(own.astype(jnp.float32)).astype(jnp.int32)

    named = (dest_ref[...] == me).astype(jnp.float32)
    chunks = named.shape[1] // LANES
    upper = (
        lax.broadcasted_iota(jnp.int32, (LANES, LANES), 0)
        <= lax.broadcasted_iota(jnp.int32, (LANES, LANES), 1)
    ).astype(jnp.float32).astype(jnp.bfloat16)
    total = jnp.zeros((shards, 1), jnp.float32)
    ranks = []
    for chunk in range(chunks):
        part = named[:, chunk * LANES : (chunk + 1) * LANES]
        upto = jnp.dot(part.astype(jnp.bfloat16), upper, preferred_element_type=jnp.float32)
        ranks.append(jnp.where(part > 0, upto + total, 0.0))
        total = total + upto[:, LANES - 1 :]
    low_half = jnp.concatenate(ranks[: chunks // 2], axis=1)
    high_half = jnp.concatenate(ranks[chunks // 2 :], axis=1)
    rank_early = jnp.where(early == 0, low_half, high_half)
    rank_late = jnp.where(early == 0, high_half, low_half)
    place = lax.broadcasted_iota(jnp.int32, (cap, cache), 0).astype(jnp.float32) + 1.0
    contract = (((1,), (1,)), ((), ()))
    for shard in range(shards):
        pick = (rank_early[shard : shard + 1] == place).astype(jnp.float32).astype(jnp.bfloat16)
        found = lax.dot_general(pick, coded[shard], contract, preferred_element_type=jnp.float32)
        if shard >= shards - 2:
            state = late_first if shard == shards - 2 else late_second
            pick = (rank_late[shard : shard + 1] == place).astype(jnp.float32).astype(jnp.bfloat16)
            found += lax.dot_general(
                pick, split(state), contract, preferred_element_type=jnp.float32
            )
        tokens = found[:, :heads] * 128.0 + found[:, heads:]
        slot_ref[shard * cap : (shard + 1) * cap, :] = tokens.astype(jnp.int32)


def column_of(table, head):
    lane = lax.broadcasted_iota(jnp.int32, table.shape, 1)
    return jnp.sum(
        jnp.where(lane == head, table, 0).astype(jnp.float32), axis=1, keepdims=True
    ).astype(jnp.int32)


def picked(column, first, tokens):
    number = lax.broadcasted_iota(jnp.int32, (column.shape[0], tokens.shape[0]), 1) + first
    table = (column == number).astype(jnp.float32).astype(jnp.bfloat16)
    return jnp.dot(table, tokens, preferred_element_type=jnp.float32)


def attend(q_ref, prompt, keys, values, seen, out_ref, score_ref, head):
    span = q_ref.shape[1]
    cache = seen.shape[1]
    group = q_ref.shape[2] // HEAD
    causal = lax.broadcasted_iota(jnp.int32, (span, span), 1) <= lax.broadcasted_iota(
        jnp.int32, (span, span), 0
    )
    bias = jnp.concatenate(
        [
            jnp.broadcast_to(jnp.where(seen > 0, 0.0, -1e30), (span, cache)),
            jnp.where(causal, 0.0, -1e30),
        ],
        axis=1,
    )
    scale = math.log2(math.e) / math.sqrt(HEAD)
    mass = jnp.zeros((1, cache + span), jnp.float32)
    for member in range(group):
        query = q_ref[prompt, :, member * HEAD : (member + 1) * HEAD]
        scores = lax.dot_general(
            query, keys, (((1,), (1,)), ((), ())), preferred_element_type=jnp.float32
        )
        scores = scores + bias
        peak = jnp.max(scores, axis=1, keepdims=True)
        expo = jnp.exp2((scores - peak) * scale)
        weights = expo * (1.0 / jnp.sum(expo, axis=1, keepdims=True))
        mass = mass + jnp.sum(weights, axis=0, keepdims=True)
        mixed = jnp.dot(weights.astype(jnp.bfloat16), values, preferred_element_type=jnp.float32)
        out_ref[prompt, :, member * HEAD : (member + 1) * HEAD] = mixed.astype(jnp.bfloat16)
    score_ref[prompt, pl.ds(head, 1), :] = mass


def attention_kernel(
    where_ref, q_ref, span_ref, early_ref, late_ref, row_ref, column_ref, out_ref, score_ref
):
    early, mine, column, shards = where_ref[0], where_ref[1], where_ref[3], early_ref.shape[0]
    span = q_ref.shape[1]
    late = 1 - early
    local_head = pl.program_id(0)
    head = column * pl.num_programs(0) + local_head

    def run(which, prompt, tokens, first):
        chosen = column_of(column_ref[which], head)
        cached = picked(chosen, first, tokens).astype(jnp.bfloat16)
        rows = jnp.concatenate([cached, span_ref[prompt]], axis=0)
        seen = row_ref[which, pl.ds(head, 1), :]
        attend(
            q_ref, prompt, rows[:, :HEAD], rows[:, HEAD:], seen, out_ref, score_ref, local_head
        )

    run(0, early, early_ref[:, 0].reshape(shards * span, WIDTH), 1)

    @pl.when(mine >= shards - 2)
    def _():
        run(1, late, late_ref[0, 0], shards * span + 1)

    @pl.when(mine < shards - 2)
    def _():
        out_ref[late] = jnp.zeros(out_ref.shape[1:], out_ref.dtype)
        score_ref[late, pl.ds(local_head, 1), :] = jnp.zeros((1, score_ref.shape[2]), jnp.float32)


def owner_kernel(slot_ref, early_ref, late_ref, out_ref):
    shards, _, span, width = early_ref.shape
    rows = out_ref.shape[0]
    chosen = column_of(slot_ref[...], pl.program_id(0))
    bands = 4
    band = rows // bands
    reach = shards * span // bands
    tokens = early_ref[:, 0].reshape(shards * span, width)
    for index in range(bands):
        part = chosen[index * band : (index + 1) * band]
        found = picked(part, 1, tokens[: (index + 1) * reach])
        if index == bands - 1:
            found += picked(part, shards * span + 1, late_ref[:, 0].reshape(2 * span, width))
        out_ref[index * band : (index + 1) * band, :] = found.astype(jnp.bfloat16)


def local(query, kv_rows, keep, dest, offsets):
    prompts, span, qwidth = query.shape
    shards, columns = lax.axis_size("ctx"), lax.axis_size("kv")
    width = kv_rows.shape[2]
    heads_dev = width // WIDTH
    heads = heads_dev * columns
    cache = keep.shape[3]
    owners = shards * columns
    cap = 2 * prompts * cache // owners
    mine, column = lax.axis_index("ctx"), lax.axis_index("kv")
    early = jnp.where(offsets[0] < offsets[1], 0, 1).astype(jnp.int32)
    facts = jnp.stack([early, mine, mine * columns + column, column]).astype(jnp.int32)

    swap = early == 1
    ordered_kv = jnp.where(swap, kv_rows[::-1], kv_rows)
    ordered_keep = jnp.where(swap, keep[::-1, 0], keep[:, 0])
    digits = jnp.stack([ordered_keep >> 7, ordered_keep & 127], axis=1)
    share = dest.shape[0] // columns
    own_dest = lax.dynamic_slice_in_dim(dest[:, 0], column * share, share)
    facts_rows = jnp.concatenate([digits.reshape(-1), own_dest]).astype(jnp.bfloat16)
    used = facts_rows.shape[0]
    room = 16 * width
    facts_rows = jnp.concatenate([facts_rows, jnp.zeros((room - used,), jnp.bfloat16)])
    payload = jnp.concatenate(
        [ordered_kv.reshape(prompts * span, width), facts_rows.reshape(16, width)], axis=0
    )
    whole = lax.all_gather(payload, ("ctx", "kv")).reshape(
        shards, columns, prompts * span + 16, width
    )

    told = whole[:, :, prompts * span :, :].reshape(shards, columns, room).astype(jnp.int32)
    kept = told[:, :, : prompts * 2 * heads_dev * cache].reshape(
        shards, columns, prompts, 2, heads_dev, cache
    )
    kept = kept[:, :, :, 0] * 128 + kept[:, :, :, 1]
    kept = jnp.transpose(kept, (2, 0, 1, 3, 4)).reshape(prompts, shards, heads, cache)
    whole_dest = told[:, :, used - share : used].reshape(shards, columns * share)

    vmem = pl.BlockSpec(memory_space=pltpu.VMEM)
    smem = pl.BlockSpec(memory_space=pltpu.SMEM)
    params = pltpu.CompilerParams(vmem_limit_bytes=VMEM_BYTES)
    slots, rows, cols = pl.pallas_call(
        index_kernel,
        out_shape=(
            jax.ShapeDtypeStruct((shards * cap, heads), jnp.int32),
            jax.ShapeDtypeStruct((2, heads, cache), jnp.int32),
            jax.ShapeDtypeStruct((2, cache, heads), jnp.int32),
        ),
        in_specs=[smem, vmem, vmem, vmem],
        out_specs=(vmem, vmem, vmem),
        scratch_shapes=[pltpu.VMEM((shards, 2 * heads, cache), jnp.bfloat16)],
        compiler_params=params,
    )(facts, kept[0], kept[1, shards - 2 :], whole_dest)

    group_width = qwidth // heads_dev
    attention, row_scores = pl.pallas_call(
        attention_kernel,
        grid_spec=pltpu.PrefetchScalarGridSpec(
            num_scalar_prefetch=1,
            grid=(heads_dev,),
            in_specs=[
                pl.BlockSpec((prompts, span, group_width), lambda h, w: (0, 0, h)),
                pl.BlockSpec((prompts, span, WIDTH), lambda h, w: (0, 0, h)),
                pl.BlockSpec((shards, 1, span, WIDTH), lambda h, w: (0, w[3], 0, h)),
                pl.BlockSpec((1, 1, span, WIDTH), lambda h, w: (shards - 2, w[3], 1, h)),
                pl.BlockSpec((2, heads, cache), lambda h, w: (0, 0, 0)),
                pl.BlockSpec((2, cache, heads), lambda h, w: (0, 0, 0)),
            ],
            out_specs=(
                pl.BlockSpec((prompts, span, group_width), lambda h, w: (0, 0, h)),
                pl.BlockSpec((prompts, heads_dev, cache + span), lambda h, w: (0, 0, 0)),
            ),
        ),
        out_shape=(
            jax.ShapeDtypeStruct((prompts, span, qwidth), jnp.bfloat16),
            jax.ShapeDtypeStruct((prompts, heads_dev, cache + span), jnp.float32),
        ),
        compiler_params=params,
    )(facts, query, kv_rows, whole, whole, rows, cols)

    owner_cache = pl.pallas_call(
        owner_kernel,
        grid=(heads,),
        in_specs=[
            pl.BlockSpec((shards * cap, heads), lambda g: (0, 0)),
            pl.BlockSpec(
                (shards, 1, span, WIDTH), lambda g: (0, g // heads_dev, 0, g % heads_dev)
            ),
            pl.BlockSpec(
                (2, 1, span, WIDTH),
                lambda g: (shards // 2 - 1, g // heads_dev, 1, g % heads_dev),
            ),
        ],
        out_specs=pl.BlockSpec((shards * cap, WIDTH), lambda g: (0, g)),
        out_shape=jax.ShapeDtypeStruct((shards * cap, heads * WIDTH), jnp.bfloat16),
        compiler_params=params,
    )(slots, whole, whole)
    return (attention, row_scores, owner_cache)


def dot(a, b, dims=((1,), (0,))):
    return lax.dot_general(a, b, (dims, ((), ())), preferred_element_type=jnp.float32)


def marks(table):
    return table.astype(jnp.float32).astype(jnp.bfloat16)


def early_of(offsets_ref):
    return jnp.where(offsets_ref[0] < offsets_ref[1], 0, 1)


def prepare_kernel(
    offsets_ref, kv_ref, keep_ref, dest_ref, both_ref, single_ref, keep, dest, sems
):
    span = kv_ref.shape[1]
    heads, cache = keep_ref.shape[2], keep_ref.shape[3]
    early = early_of(offsets_ref)
    copies = [
        (keep_ref, keep),
        (dest_ref, dest),
        (kv_ref.at[early], single_ref.at[:span]),
        (kv_ref.at[early], both_ref.at[:span]),
        (kv_ref.at[1 - early], both_ref.at[span : 2 * span]),
    ]
    copies = [
        pltpu.make_async_copy(source, target, sems.at[index])
        for index, (source, target) in enumerate(copies)
    ]
    for copy in copies:
        copy.start()
    for copy in copies[:2]:
        copy.wait()
    lane = lax.broadcasted_iota(jnp.int32, (heads, cache), 1)
    rows = [
        keep[early, 0] - lane,
        dest[:, :cache],
        dest[:, cache:],
        keep[1 - early, 0] - lane,
        jnp.zeros((NOTES - 2 * heads - 2, cache), jnp.int32),
    ]
    rows = jnp.concatenate([row.astype(jnp.float32) for row in rows], axis=0)
    rows = rows.astype(jnp.bfloat16)
    single_ref[span:, :] = rows
    both_ref[2 * span :, :] = rows
    for copy in copies[2:]:
        copy.wait()


def two_notes(first, first_row, second, second_row):
    half = NOTES // 2
    return jnp.concatenate(
        [
            first[first_row : first_row + NOTES, :].astype(jnp.float32)[:half],
            second[second_row : second_row + NOTES, :].astype(jnp.float32)[:half],
        ],
        axis=0,
    ).astype(jnp.bfloat16)


def going_kernel(both, y_own, x_own, d_own, going_ref):
    span = both.shape[0] // 2 - NOTES // 2
    going_ref[:span, :] = both[:span, :]
    going_ref[span : 2 * span, :] = y_own[:span, :]
    going_ref[2 * span : 2 * span + NOTES, :] = two_notes(both, 2 * span, y_own, 2 * span)
    going_ref[2 * span + NOTES :, :] = two_notes(x_own, span, d_own, span)


def beside_kernel(below, above, both, _, beside_ref, relay_ref):
    span = relay_ref.shape[0]
    beside_ref[:span, :] = below[:span, :]
    beside_ref[span : 2 * span, :] = above[:span, :]
    beside_ref[2 * span :, :] = two_notes(below, 2 * span, above, span)
    level = lax.axis_index("ctx") // 2

    @pl.when(level == 0)
    def _():
        relay_ref[...] = below[span : 2 * span, :]

    @pl.when(level > 0)
    def _():
        relay_ref[...] = both[span : 2 * span, :]


def join_second_kernel(beyond, relay, relayed, *rest):
    out_ref, late_ref = rest[-2:]
    span = relay.shape[0]
    level = lax.axis_index("ctx") // 2
    out_ref[: 2 * span, :] = beyond[: 2 * span, :]
    for ref, chosen in ((relay, (level == 0) | (level == 3)), (relayed, (level == 1) | (level == 2))):

        @pl.when(chosen)
        def _(ref=ref):
            out_ref[2 * span :, :] = ref[...]
            late_ref[...] = ref[...]


def place_of(turn, flip, shards):
    mine = lax.axis_index("ctx")
    place = lax.rem(mine - 2 * turn + shards, shards)
    return place + 1 - 2 * lax.rem(mine, 2) if flip else place


def sort_tokens(pieces, tokens, span):
    shards = tokens.shape[0] // span
    for ref, base, turn, flip in pieces:
        place = place_of(turn, flip, shards)
        tokens[pl.ds(pl.multiple_of(place * span, span), span), :] = ref[base : base + span, :]


def sort_late(pieces, late_tokens):
    span = late_tokens.shape[0] // 2
    side = lax.rem(lax.axis_index("ctx"), 2)
    for flip, ref_base in enumerate(pieces):
        ref, base = ref_base
        place = side + flip - 2 * side * flip
        late_tokens[pl.ds(pl.multiple_of(place * span, span), span), :] = ref[
            base : base + span, :
        ]


def read_notes(ref, base, part, heads):
    half = NOTES // 2
    rows = ref[base : base + NOTES, :].astype(jnp.float32).astype(jnp.int32)
    rows = rows[part * half : (part + 1) * half]
    lane = lax.broadcasted_iota(jnp.int32, (heads, rows.shape[1]), 1)
    return rows[:heads] + lane, rows[heads + 2 : 2 * heads + 2] + lane, rows[heads : heads + 2]


def sort_notes(notes, keeps, dests):
    shards, heads = keeps.shape[0], keeps.shape[1] // 4
    for ref, base, part, turn, flip in notes:
        place = place_of(turn, flip, shards)
        early, late, dest = read_notes(ref, base, part, heads)
        keeps[place, :heads, :] = early
        keeps[place, heads : 2 * heads, :] = late
        dests[place, :, :] = dest


def follow_lists(keeps, coded, span):
    shards, rows, cache = keeps.shape
    heads = rows // 4
    row = lax.broadcasted_iota(jnp.int32, (rows, cache), 0)
    is_early = row < heads
    state = jnp.where(row < 0, keeps[0], 0)
    own = state
    mine = lax.axis_index("ctx")
    for shard in range(shards):
        own = jnp.where(mine == shard, state, own)
        late_first = (shards + shard - (shards - 2)) * span + 1
        fresh = jnp.where(is_early[:, :LANES], shard * span + 1, late_first)
        state = look_up(state, keeps[shard], fresh)
        if shard < shards - 2:
            state = jnp.where(is_early, state, 0)
        coded[shard] = split(state)
    return own


def find_slots(early, dests, coded, owner, slots):
    shards, halves, cache = dests.shape
    heads = coded.shape[1] // 8
    cap = slots.shape[0] // shards
    upper = marks(
        lax.broadcasted_iota(jnp.int32, (LANES, LANES), 0)
        <= lax.broadcasted_iota(jnp.int32, (LANES, LANES), 1)
    )
    place = lax.broadcasted_iota(jnp.int32, (cap, cache), 0).astype(jnp.float32) + 1.0
    total = jnp.zeros((shards, 1), jnp.float32)
    ranks = []
    for half in range(halves):
        named = (dests[:, half, :] == owner).astype(jnp.float32)
        parts = []
        for chunk in range(cache // LANES):
            part = named[:, chunk * LANES : (chunk + 1) * LANES]
            upto = dot(part.astype(jnp.bfloat16), upper)
            parts.append(jnp.where(part > 0, upto + total, 0.0))
            total = total + upto[:, LANES - 1 :]
        ranks.append(jnp.concatenate(parts, axis=1))
    rank_early = jnp.where(early == 0, ranks[0], ranks[1])
    rank_late = jnp.where(early == 0, ranks[1], ranks[0])
    across = ((1,), (1,))
    for shard in range(shards):
        found = dot(marks(rank_early[shard : shard + 1] == place), coded[shard], across)
        tokens = found[:, :heads] * 128.0 + found[:, 4 * heads : 5 * heads]
        if shard >= shards - 2:
            found = dot(marks(rank_late[shard : shard + 1] == place), coded[shard], across)
            tokens += found[:, heads : 2 * heads] * 128.0 + found[:, 5 * heads : 6 * heads]
        slots[shard * cap : (shard + 1) * cap, :] = tokens.astype(jnp.int32)


def place_bands(slots, tokens, out_ref, bands, total_bands):
    rows, heads = slots.shape
    reach = tokens.shape[0]
    band = rows // total_bands
    for head in range(heads):
        lanes = slice(head * WIDTH, (head + 1) * WIDTH)
        for order, index in enumerate(bands):
            part = slots[index * band : (index + 1) * band, head : head + 1]
            found = picked(part, 1, tokens[: (index + 1) * reach // total_bands, lanes])
            out_ref[order * band : (order + 1) * band, lanes] = found.astype(jnp.bfloat16)


def add_late(slots, first, late_tokens, out_ref, base):
    band, heads = slots.shape
    for head in range(heads):
        lanes = slice(head * WIDTH, (head + 1) * WIDTH)
        found = picked(slots[:, head : head + 1], first, late_tokens[:, lanes])
        out_ref[base : base + band, lanes] += found.astype(jnp.bfloat16)


def attend_columns(q_ref, head, rows, seen, out_ref, score_ref):
    span = q_ref.shape[1]
    total = rows.shape[0]
    cache = total - span
    group = q_ref.shape[2] // (score_ref.shape[1] * HEAD)
    keys, values = rows[:, :HEAD], rows[:, HEAD:]
    flat = jnp.transpose(values.astype(jnp.float32)).astype(jnp.bfloat16)
    lane = lax.broadcasted_iota(jnp.int32, (total, HEAD), 1)
    hidden = jnp.where(seen > 0, 0.0, -1e30)
    hidden = jnp.concatenate([hidden, jnp.zeros((span, 1), jnp.float32)], axis=0)
    hidden = jnp.where(lane == 0, hidden, 0.0).astype(jnp.bfloat16)
    keys = jnp.concatenate([keys, hidden], axis=1)
    ones = jnp.ones((2 * span, HEAD), jnp.bfloat16)
    causal = lax.broadcasted_iota(jnp.int32, (span, 2 * span), 0) <= lax.rem(
        lax.broadcasted_iota(jnp.int32, (span, 2 * span), 1), span
    )
    bias = jnp.where(causal, 0.0, -1e30)
    scale = math.log2(math.e) / math.sqrt(HEAD)
    mass = None
    for pair in range(group // 2):
        first = (head * group + 2 * pair) * HEAD
        query = jnp.concatenate(
            [
                q_ref[0, :, first : first + HEAD],
                q_ref[0, :, first + HEAD : first + 2 * HEAD],
            ],
            axis=0,
        )
        scores = dot(keys, jnp.concatenate([query, ones], axis=1), ((1,), (1,)))
        near = scores[cache:] + bias
        scores = jnp.concatenate([scores[:cache], near], axis=0) * scale
        peak = jnp.max(scores, axis=0, keepdims=True)
        expo = jnp.exp2(scores - peak)
        weights = expo * (1.0 / jnp.sum(expo, axis=0, keepdims=True))
        both = weights[:, :span] + weights[:, span:]
        mass = both if mass is None else mass + both
        mixed = jnp.transpose(dot(flat, weights.astype(jnp.bfloat16)))
        for member in range(2):
            lanes = slice(first + member * HEAD, first + (member + 1) * HEAD)
            out_ref[0, :, lanes] = mixed[member * span : (member + 1) * span].astype(
                jnp.bfloat16
            )
    score_ref[0, head : head + 1, :] = jnp.sum(jnp.transpose(mass), axis=0, keepdims=True)


def late_kernel(offsets_ref, q_ref, both_ref, beside_ref, out_ref, score_ref, done_ref):
    mine, shards = lax.axis_index("ctx"), lax.axis_size("ctx")
    heads, cache = score_ref.shape[1], score_ref.shape[2] - q_ref.shape[1]
    span = q_ref.shape[1]
    done_ref[...] = jnp.zeros(done_ref.shape, jnp.float32)

    @pl.when(mine >= shards - 2)
    def _():
        _, keep, _ = read_notes(beside_ref, 2 * span, 0, heads)
        state = jnp.where(keep >= cache, keep - cache + 1, 0)
        state = jnp.where(mine == shards - 1, state, 0).astype(jnp.float32)
        state = jnp.concatenate([state, jnp.zeros((8 - heads, cache), jnp.float32)], axis=0)
        columns = jnp.transpose(state).astype(jnp.int32)
        for head in range(heads):
            lanes = slice(head * WIDTH, (head + 1) * WIDTH)
            column = columns[:, head : head + 1]
            cached = picked(column, 1, beside_ref[span : 2 * span, lanes])
            rows = jnp.concatenate(
                [cached.astype(jnp.bfloat16), both_ref[span : 2 * span, lanes]], axis=0
            )
            attend_columns(q_ref, head, rows, column, out_ref, score_ref)

    @pl.when(mine < shards - 2)
    def _():
        out_ref[...] = jnp.zeros(out_ref.shape, out_ref.dtype)
        score_ref[...] = jnp.zeros(score_ref.shape, jnp.float32)


def output_part(cache_ref, row, rows, column):
    width = cache_ref.shape[1] // lax.axis_size("kv")
    return cache_ref.at[
        pl.ds(row, rows), pl.ds(pl.multiple_of(column * width, width), width)
    ]


def fill_slots(offsets_ref, notes, keeps, dests, coded, slots_ref):
    me = lax.axis_index("ctx") * lax.axis_size("kv") + lax.axis_index("kv")
    sort_notes(notes, keeps, dests)
    own = follow_lists(keeps, coded, LANES)
    for flip in range(2):
        find_slots(early_of(offsets_ref), dests, coded, me ^ flip, slots_ref.at[flip])
    return own


def early_kernel(offsets_ref, q_ref, *rest):
    both, beside, beyond, y_own, y_beside = rest[:5]
    out_ref, score_ref, done_ref, cache_ref, top_sent, low_ref, slots_ref = rest[8:15]
    tokens, top, sem, keeps, dests, coded = rest[15:]
    done_ref[...] = jnp.zeros(done_ref.shape, jnp.float32)
    span = both.shape[0] // 2 - NOTES // 2
    column = lax.axis_index("kv")
    at = 2 * span
    notes = [(both, at, 0, 0, 0), (beside, at, 0, 1, 0), (beside, at, 1, 3, 0)]
    notes += [(beyond, at, 0, 2, 0), (beyond, at, 1, 2, 1), (y_own, at, 0, 0, 1)]
    notes += [(y_beside, at, 0, 1, 1), (y_beside, at, 1, 3, 1)]
    own = fill_slots(offsets_ref, notes, keeps, dests, coded, slots_ref)
    own = jnp.transpose(own.astype(jnp.float32)).astype(jnp.int32)
    pieces = [(both, 0, 0, 0), (beside, 0, 1, 0), (beside, span, 3, 0), (beyond, 0, 2, 0)]
    pieces += [(beyond, span, 2, 1), (y_own, 0, 0, 1), (y_beside, 0, 1, 1), (y_beside, span, 3, 1)]
    sort_tokens(pieces, tokens, span)
    bands = tuple(range(BANDS - 1))
    place_bands(slots_ref.at[0], tokens, top, bands, BANDS)
    copy = pltpu.make_async_copy(top, output_part(cache_ref, 0, top.shape[0], column), sem)
    copy.start()
    place_bands(slots_ref.at[1], tokens, top_sent, bands, BANDS)
    for flip in range(2):
        place_bands(slots_ref.at[flip], tokens, low_ref.at[flip], (BANDS - 1,), BANDS)
    for head in range(score_ref.shape[1]):
        lanes = slice(head * WIDTH, (head + 1) * WIDTH)
        chosen = own[:, head : head + 1]
        cached = picked(chosen, 1, tokens[:, lanes]).astype(jnp.bfloat16)
        rows = jnp.concatenate([cached, both[:span, lanes]], axis=0)
        attend_columns(q_ref, head, rows, chosen, out_ref, score_ref)
    copy.wait()


def far_index_kernel(offsets_ref, x_own, x_beside, d_own, d_beside, beyond, _, *rest):
    slots_ref, keeps, dests, coded = rest
    span = x_own.shape[0] - NOTES
    at = 2 * span
    notes = [(x_own, span, 0, 0, 0), (d_own, span, 0, 0, 1), (x_beside, at, 0, 1, 0)]
    notes += [(x_beside, at, 1, 3, 0), (d_beside, at, 0, 1, 1), (d_beside, at, 1, 3, 1)]
    notes += [(beyond, at + NOTES, 0, 2, 0), (beyond, at + NOTES, 1, 2, 1)]
    fill_slots(offsets_ref, notes, keeps, dests, coded, slots_ref)


def far_rows(flip, refs, far_ref, low, tokens, near_late, far_late):
    x_own, x_beside, x_end, d_own, d_beside, d_late, late, y_late, low_ref = refs[:9]
    near_slots, far_slots = refs[9:]
    span = late.shape[0]
    rows = far_slots.shape[1]
    band = rows // BANDS
    first = tokens.shape[0] + 1
    last = pl.ds(rows - band, band)
    sort_late([(late, 0), (y_late, 0)], near_late)
    sort_late([(x_end, 2 * span), (d_late, 0)], far_late)
    low[...] = low_ref[flip]
    add_late(near_slots.at[flip, last], first, near_late, low, 0)
    pieces = [(x_own, 0, 0, 0), (x_beside, 0, 1, 0), (x_beside, span, 3, 0), (x_end, 0, 2, 0)]
    pieces += [(x_end, span, 2, 1), (d_own, 0, 0, 1), (d_beside, 0, 1, 1), (d_beside, span, 3, 1)]
    sort_tokens(pieces, tokens, span)
    place_bands(far_slots.at[flip], tokens, far_ref, tuple(range(BANDS)), BANDS)
    add_late(far_slots.at[flip, last], first, far_late, far_ref, rows - band)


def far_sent_kernel(*refs):
    top_ref, sent_ref = refs[11:13]
    rows = refs[10].shape[1]
    upper = rows + top_ref.shape[0]
    sent_ref[rows:upper, :] = top_ref[...]
    far_rows(1, refs[:11], sent_ref.at[:rows], sent_ref.at[upper:], *refs[13:])


def far_kept_kernel(*refs):
    cache_ref, far, low, tokens, near_late, far_late, sems = refs[12:]
    column = lax.axis_index("kv")
    rows, band = far.shape[0], low.shape[0]
    far_rows(0, refs[:11], far, low, tokens, near_late, far_late)
    copies = [
        pltpu.make_async_copy(far, output_part(cache_ref, 0, rows, column ^ 2), sems.at[0]),
        pltpu.make_async_copy(
            low, output_part(cache_ref, rows - band, band, column), sems.at[1]
        ),
    ]
    for copy in copies:
        copy.start()
    for copy in copies:
        copy.wait()


def last_kernel(sent_ref, _, cache_ref, sems):
    column = lax.axis_index("kv")
    rows = cache_ref.shape[0]
    copies = [
        pltpu.make_async_copy(
            sent_ref.at[index * rows : (index + 1) * rows],
            output_part(cache_ref, 0, rows, column ^ place),
            sems.at[index],
        )
        for index, place in enumerate((3, 1))
    ]
    for copy in copies:
        copy.start()
    for copy in copies:
        copy.wait()


def send(value, axis, pairs):
    return lax.ppermute(value, axis, pairs)


def local_in_planes(query, kv_rows, keep, dest, offsets):
    prompts, span, qwidth = query.shape
    shards, columns = lax.axis_size("ctx"), lax.axis_size("kv")
    width = kv_rows.shape[2]
    heads = width // WIDTH
    cache = keep.shape[3]
    rows = 2 * prompts * cache // columns
    band = rows // BANDS
    vmem = pl.BlockSpec(memory_space=pltpu.VMEM)
    smem = pl.BlockSpec(memory_space=pltpu.SMEM)
    anywhere = pl.BlockSpec(memory_space=pl.ANY)
    hbm = pl.BlockSpec(memory_space=pltpu.HBM)
    params = pltpu.CompilerParams(vmem_limit_bytes=PLANE_BYTES)

    def cost(flops, moved):
        return pl.CostEstimate(flops=flops, bytes_accessed=moved, transcendentals=0)

    def piece(count):
        return jax.ShapeDtypeStruct((count, width), jnp.bfloat16)

    def along_z(value, turn):
        return send(value, "ctx", [(i, (i + 2 * turn) % shards) for i in range(shards)])

    def across_y(value):
        return send(value, "ctx", [(i, i ^ 1) for i in range(shards)])

    def across_x(value):
        return send(value, "kv", [(i, i ^ 2) for i in range(columns)])

    def across_both(value):
        pairs = [(i, i ^ columns ^ 2) for i in range(shards * columns)]
        return send(value, ("ctx", "kv"), pairs)

    def across_core(value):
        return send(value, "kv", [(i, i ^ 1) for i in range(columns)])

    both, single = pl.pallas_call(
        prepare_kernel,
        out_shape=(piece(2 * span + NOTES), piece(span + NOTES)),
        in_specs=[smem] + [hbm] * 3,
        out_specs=(vmem, vmem),
        scratch_shapes=[
            pltpu.VMEM(keep.shape, jnp.int32),
            pltpu.VMEM((1, prompts * cache), jnp.int32),
            pltpu.SemaphoreType.DMA((5,)),
        ],
        compiler_params=pltpu.CompilerParams(vmem_limit_bytes=60 * 1024 * 1024),
        cost_estimate=cost(10**9, 1),
    )(offsets, kv_rows, keep, jnp.transpose(dest))

    below, above = along_z(both, 1), along_z(single, 3)
    y_own, x_own, d_own = across_y(both), across_x(single), across_both(single)
    going = pl.pallas_call(
        going_kernel,
        out_shape=piece(2 * span + 2 * NOTES),
        in_specs=[vmem] * 4,
        out_specs=vmem,
        compiler_params=params,
        cost_estimate=cost(0, 10**6),
    )(both, y_own, x_own, d_own)
    beyond = along_z(going, 2)
    beside, relay = pl.pallas_call(
        beside_kernel,
        out_shape=(piece(2 * span + NOTES), piece(span)),
        in_specs=[vmem] * 3 + [anywhere],
        out_specs=(vmem,) * 2,
        compiler_params=params,
        cost_estimate=cost(0, 10**6),
    )(below, above, both, going)
    relayed = send(relay, "ctx", [(0, 2), (1, 3), (6, 4), (7, 5)])
    y_beside, x_beside = across_y(beside), across_x(beside)
    d_beside = across_y(x_beside)

    attention_shape = jax.ShapeDtypeStruct((prompts, span, qwidth), jnp.bfloat16)
    score_shape = jax.ShapeDtypeStruct((prompts, heads, cache + span), jnp.float32)

    def prompt_specs(late):
        def block(_, offsets_ref):
            early = early_of(offsets_ref)
            return (1 - early if late else early, 0, 0)

        return (
            pl.BlockSpec((1, span, qwidth), block),
            pl.BlockSpec((1, heads, cache + span), block),
        )

    attention, row_scores, late_done = pl.pallas_call(
        late_kernel,
        grid_spec=pltpu.PrefetchScalarGridSpec(
            num_scalar_prefetch=1,
            grid=(1,),
            in_specs=[prompt_specs(True)[0], vmem, vmem],
            out_specs=prompt_specs(True) + (vmem,),
        ),
        out_shape=(attention_shape, score_shape, jax.ShapeDtypeStruct((8, LANES), jnp.float32)),
        compiler_params=params,
        cost_estimate=cost(10**6, 1),
    )(offsets, query, both, y_own)

    end, late = pl.pallas_call(
        join_second_kernel,
        out_shape=(piece(3 * span), piece(span)),
        in_specs=[vmem] * 3 + [anywhere] * 3,
        out_specs=(vmem, vmem),
        compiler_params=params,
        cost_estimate=cost(10**6, 1),
    )(beyond, relay, relayed, y_beside, x_beside, late_done)
    d_late, y_late, x_end = across_both(late), across_y(late), across_x(end)

    tokens = pltpu.VMEM((shards * span, width), jnp.bfloat16)
    late_tokens = pltpu.VMEM((2 * span, width), jnp.bfloat16)
    cache_shape = jax.ShapeDtypeStruct((rows, columns * width), jnp.bfloat16)
    slots_shape = jax.ShapeDtypeStruct((2, rows, heads), jnp.int32)
    done_shape = jax.ShapeDtypeStruct((8, LANES), jnp.float32)
    tables = [
        pltpu.VMEM((shards, 4 * heads, cache), jnp.int32),
        pltpu.VMEM((shards, prompts, cache), jnp.int32),
        pltpu.VMEM((shards, 8 * heads, cache), jnp.bfloat16),
    ]
    attention, row_scores, early_done, owner_cache, top, low, near_slots = pl.pallas_call(
        early_kernel,
        grid_spec=pltpu.PrefetchScalarGridSpec(
            num_scalar_prefetch=1,
            grid=(1,),
            in_specs=[prompt_specs(False)[0]] + [vmem] * 5 + [anywhere] * 3,
            out_specs=prompt_specs(False) + (vmem, hbm, vmem, vmem, vmem),
            scratch_shapes=[
                tokens,
                pltpu.VMEM((rows - band, width), jnp.bfloat16),
                pltpu.SemaphoreType.DMA,
            ]
            + tables,
        ),
        out_shape=(
            attention_shape,
            score_shape,
            done_shape,
            cache_shape,
            piece(rows - band),
            jax.ShapeDtypeStruct((2, band, width), jnp.bfloat16),
            slots_shape,
        ),
        input_output_aliases={8: 0, 9: 1},
        compiler_params=params,
        cost_estimate=cost(10**10, 10**7),
    )(offsets, query, both, beside, beyond, y_own, y_beside, late, attention, row_scores)
    far_slots = pl.pallas_call(
        far_index_kernel,
        out_shape=slots_shape,
        in_specs=[smem] + [vmem] * 5 + [anywhere],
        out_specs=vmem,
        scratch_shapes=tables,
        compiler_params=params,
        cost_estimate=cost(10**6, 1),
    )(offsets, x_own, x_beside, d_own, d_beside, beyond, early_done)
    far = (x_own, x_beside, x_end, d_own, d_beside, d_late, late, y_late, low)
    far += (near_slots, far_slots)
    sent = pl.pallas_call(
        far_sent_kernel,
        out_shape=piece(2 * rows),
        in_specs=[vmem] * 12,
        out_specs=vmem,
        scratch_shapes=[tokens, late_tokens, late_tokens],
        compiler_params=params,
        cost_estimate=cost(2 * 10**9, 4 * 10**6),
    )(*far, top)
    received = across_core(sent)
    owner_cache = pl.pallas_call(
        far_kept_kernel,
        out_shape=cache_shape,
        in_specs=[vmem] * 11 + [hbm],
        out_specs=hbm,
        scratch_shapes=[
            pltpu.VMEM((rows, width), jnp.bfloat16),
            pltpu.VMEM((band, width), jnp.bfloat16),
            tokens,
            late_tokens,
            late_tokens,
            pltpu.SemaphoreType.DMA((2,)),
        ],
        input_output_aliases={11: 0},
        compiler_params=params,
        cost_estimate=cost(2 * 10**9, 4 * 10**6),
    )(*far, owner_cache)
    owner_cache = pl.pallas_call(
        last_kernel,
        out_shape=cache_shape,
        in_specs=[anywhere, hbm],
        out_specs=hbm,
        scratch_shapes=[pltpu.SemaphoreType.DMA((2,))],
        input_output_aliases={1: 0},
        compiler_params=params,
        cost_estimate=cost(0, 10**6),
    )(received, owner_cache)
    return (attention, row_scores, owner_cache)


def solution(mesh):
    placed = (
        P(None, "ctx", "kv"),
        P(None, "ctx", "kv"),
        P(None, "ctx", "kv", None),
        P("ctx", None),
        P(),
    )
    in_planes = mesh.shape["ctx"] == 8 and mesh.shape["kv"] == 4
    return jax.shard_map(
        local_in_planes if in_planes else local,
        mesh=mesh,
        in_specs=placed,
        out_specs=(P(None, "ctx", "kv"), P(None, "kv", "ctx"), P(("ctx", "kv"), None)),
        check_vma=False,
    )
```

profile of v0, /device:TPU:0, one launch (start us, length us, event | category | flops | bytes accessed | tf_op | source)
XLA Modules:
  0.0 51.5 jit_solution(7331216342601604198)
XLA Ops:
  0.7 2.7 %shard_map.76 = (bf16[272,512]{1,0:T(8,128)(2,1)}, bf16[144,512]{1,0:T(8,128)(2,1)}) custom-call(s32[2]{0:T(128)} %offsets_ref.7, bf16[2,128,512]{2,1,0:T(8,128)(2,1)} %kv_ref.1, s32[2,1,2,512]{3,2,1,0:T(2,128)} %keep_ref.1, s32[1,1024]{1,0:T(1,128)} %bitcast.1), custom_call_target="tpu_custom_call" | custom-call | flops 1000000000 | bytes 1 | tf_op jit(solution)/shard_map/pallas_call | solution.py:730
  3.3 3.0 %collective-permute-start.2 = (bf16[272,512]{1,0:T(8,128)(2,1)}, bf16[272,512]{1,0:T(8,128)(2,1)S(1)}, u32[]{:S(2)}, u32[]{:S(2)}) collective-permute-start(bf16[272,512]{1,0:T(8,128)(2,1)} %get-tuple-element.19.both.both_ref.rest_0_), channel_id=1, source_target_pairs={{0,4},{4,0},{8,12},{12,8},{16,20},{20,16},{24,28},{28,24},{1,5},{5... | collective-permute-start | bytes 835592 | tf_op jit(solution)/shard_map/ppermute | solution.py:691
  6.3 1.6 %collective-permute-start = (bf16[272,512]{1,0:T(8,128)(2,1)}, bf16[272,512]{1,0:T(8,128)(2,1)S(1)}, u32[]{:S(2)}, u32[]{:S(2)}) collective-permute-start(bf16[272,512]{1,0:T(8,128)(2,1)} %get-tuple-element.19.both.both_ref.rest_0_), channel_id=1, source_target_pairs={{0,8},{4,12},{8,16},{12,20},{16,24},{20,28},{24,0},{28,4},{1,9},{5... | collective-permute-start | bytes 835592 | tf_op jit(solution)/shard_map/ppermute | solution.py:691
  7.9 1.4 %collective-permute-start.4 = (bf16[144,512]{1,0:T(8,128)(2,1)}, bf16[144,512]{1,0:T(8,128)(2,1)S(1)}, u32[]{:S(2)}, u32[]{:S(2)}) collective-permute-start(bf16[144,512]{1,0:T(8,128)(2,1)} %get-tuple-element.20), channel_id=1, source_target_pairs={{0,6},{1,7},{2,4},{3,5},{4,2},{5,3},{6,0},{7,1},{8,14},{9,15},{10,... | collective-permute-start | bytes 442376 | tf_op jit(solution)/shard_map/ppermute | solution.py:691
  9.4 0.5 %collective-permute-start.3 = (bf16[144,512]{1,0:T(8,128)(2,1)}, bf16[144,512]{1,0:T(8,128)(2,1)S(1)}, u32[]{:S(2)}, u32[]{:S(2)}) collective-permute-start(bf16[144,512]{1,0:T(8,128)(2,1)} %get-tuple-element.20), channel_id=1, source_target_pairs={{0,2},{1,3},{2,0},{3,1},{4,6},{5,7},{6,4},{7,5},{8,10},{9,11},{10,... | collective-permute-start | bytes 442376 | tf_op jit(solution)/shard_map/ppermute | solution.py:691
  9.9 2.0 %collective-permute-start.1 = (bf16[144,512]{1,0:T(8,128)(2,1)}, bf16[144,512]{1,0:T(8,128)(2,1)S(1)}, u32[]{:S(2)}, u32[]{:S(2)}) collective-permute-start(bf16[144,512]{1,0:T(8,128)(2,1)} %get-tuple-element.20), channel_id=1, source_target_pairs={{0,24},{4,28},{8,0},{12,4},{16,8},{20,12},{24,16},{28,20},{1,25},{... | collective-permute-start | bytes 442376 | tf_op jit(solution)/shard_map/ppermute | solution.py:691
  11.9 3.8 %collective-permute-done.4.d_own.refs_3_ = bf16[144,512]{1,0:T(8,128)(2,1)S(1)} collective-permute-done((bf16[144,512]{1,0:T(8,128)(2,1)}, bf16[144,512]{1,0:T(8,128)(2,1)S(1)}, u32[]{:S(2)}, u32[]{:S(2)}) %collective-permute-start.4) | collective-permute-done | bytes 147488 | tf_op jit(solution)/shard_map/ppermute | solution.py:691
  15.7 0.6 %collective-permute-done.3.x_own.refs_0_ = bf16[144,512]{1,0:T(8,128)(2,1)S(1)} collective-permute-done((bf16[144,512]{1,0:T(8,128)(2,1)}, bf16[144,512]{1,0:T(8,128)(2,1)S(1)}, u32[]{:S(2)}, u32[]{:S(2)}) %collective-permute-start.3) | collective-permute-done | bytes 147488 | tf_op jit(solution)/shard_map/ppermute | solution.py:691
  16.3 0.1 collective-permute-done.2.y_own.beside_ref.rest_3_
  16.4 1.0 %copy-done = bf16[272,512]{1,0:T(8,128)(2,1)S(1)} copy-done((bf16[272,512]{1,0:T(8,128)(2,1)S(1)}, bf16[272,512]{1,0:T(8,128)(2,1)}, u32[]{:S(2)}) %copy-start) | copy-done | bytes 278552
  17.4 2.9 %collective-permute-start.5 = (bf16[288,512]{1,0:T(8,128)(2,1)S(1)}, bf16[288,512]{1,0:T(8,128)(2,1)S(1)}, u32[]{:S(2)}, u32[]{:S(2)}) collective-permute-start(bf16[288,512]{1,0:T(8,128)(2,1)S(1)} %shard_map.77._), channel_id=1, source_target_pairs={{0,16},{4,20},{8,24},{12,28},{16,0},{20,4},{24,8},{28,12},{1,17},{... | collective-permute-start | bytes 884744 | tf_op jit(solution)/shard_map/ppermute | solution.py:691
  20.3 1.6 %collective-permute-start.8 = (bf16[272,512]{1,0:T(8,128)(2,1)S(1)}, bf16[272,512]{1,0:T(8,128)(2,1)S(1)}, u32[]{:S(2)}, u32[]{:S(2)}) collective-permute-start(bf16[272,512]{1,0:T(8,128)(2,1)S(1)} %get-tuple-element.21.rest_1_), channel_id=1, source_target_pairs={{0,2},{1,3},{2,0},{3,1},{4,6},{5,7},{6,4},{7,5},{8,10},{9,11},{10,... | collective-permute-start | bytes 835592 | tf_op jit(solution)/shard_map/ppermute | solution.py:691
  21.8 1.5 %collective-permute-start.6 = (bf16[272,512]{1,0:T(8,128)(2,1)S(1)}, bf16[272,512]{1,0:T(8,128)(2,1)S(1)}, u32[]{:S(2)}, u32[]{:S(2)}) collective-permute-start(bf16[272,512]{1,0:T(8,128)(2,1)S(1)} %get-tuple-element.21.rest_1_), channel_id=1, source_target_pairs={{0,4},{4,0},{8,12},{12,8},{16,20},{20,16},{24,28},{28,24},{1,5},{5... | collective-permute-start | bytes 835592 | tf_op jit(solution)/shard_map/ppermute | solution.py:691
  23.4 3.5 %collective-permute-start.7 = (bf16[128,512]{1,0:T(8,128)(2,1)S(1)}, bf16[128,512]{1,0:T(8,128)(2,1)S(1)}, u32[]{:S(2)}, u32[]{:S(2)}) collective-permute-start(bf16[128,512]{1,0:T(8,128)(2,1)S(1)} %get-tuple-element.22.relay), channel_id=1, source_target_pairs={{0,8},{4,12},{24,16},{28,20},{1,9},{5,13},{25,17},{29,21},{2,10},{... | collective-permute-start | bytes 393224 | tf_op jit(solution)/shard_map/ppermute | solution.py:691
  26.9 1.4 %shard_map.79 = (bf16[2,128,2048]{2,1,0:T(8,128)(2,1)}, f32[2,2,640]{2,1,0:T(2,128)}, f32[8,128]{1,0:T(8,128)S(1)}) custom-call(s32[2]{0:T(128)S(1)} %copy-done.3, bf16[2,128,2048]{2,1,0:T(8,128)(2,1)S(1)} %copy-done.2, bf16[272,512]{1,0:T(8,128)(2,1)S(1)} %copy-done.1, bf16[272,512]{1,0:T(8,128)(2,1)S(1)} %collective-permute-done.2.y_own.beside_ref.rest_3_), custom_call_target="tpu_custom_call" | custom-call | flops 1000000 | bytes 1 | tf_op jit(solution)/shard_map/pallas_call | solution.py:780
  28.3 0.1 collective-permute-done.8.rest_1_.x_beside.refs_1_
  28.4 0.8 %collective-permute-start.10 = (bf16[272,512]{1,0:T(8,128)(2,1)S(1)}, bf16[272,512]{1,0:T(8,128)(2,1)S(1)}, u32[]{:S(2)}, u32[]{:S(2)}) collective-permute-start(bf16[272,512]{1,0:T(8,128)(2,1)S(1)} %collective-permute-done.8.rest_1_.x_beside.refs_1_), channel_id=1, source_target_pairs={{0,4},{4,0},{8,12},{12,8},{16,20},{20,16},{24,28},{28,24},{1,5},{5... | collective-permute-start | bytes 835592 | tf_op jit(solution)/shard_map/ppermute | solution.py:691
  29.1 0.2 collective-permute-done.7.relayed
  29.3 0.3 collective-permute-done.6.rest_0_.rest_4_
  29.6 3.0 %collective-permute-done.5.beyond.rest_2_ = bf16[288,512]{1,0:T(8,128)(2,1)S(1)} collective-permute-done((bf16[288,512]{1,0:T(8,128)(2,1)S(1)}, bf16[288,512]{1,0:T(8,128)(2,1)S(1)}, u32[]{:S(2)}, u32[]{:S(2)}) %collective-permute-start.5) | collective-permute-done | bytes 294944 | tf_op jit(solution)/shard_map/ppermute | solution.py:691
  32.5 0.2 shard_map.80
  32.8 1.8 %collective-permute-start.12 = (bf16[128,512]{1,0:T(8,128)(2,1)S(1)}, bf16[128,512]{1,0:T(8,128)(2,1)S(1)}, u32[]{:S(2)}, u32[]{:S(2)}) collective-permute-start(bf16[128,512]{1,0:T(8,128)(2,1)S(1)} %get-tuple-element.24.rest_5_.refs_6_), channel_id=1, source_target_pairs={{0,4},{4,0},{8,12},{12,8},{16,20},{20,16},{24,28},{28,24},{1,5},{5... | collective-permute-start | bytes 393224 | tf_op jit(solution)/shard_map/ppermute | solution.py:691
  34.5 1.1 %collective-permute-start.11 = (bf16[128,512]{1,0:T(8,128)(2,1)S(1)}, bf16[128,512]{1,0:T(8,128)(2,1)S(1)}, u32[]{:S(2)}, u32[]{:S(2)}) collective-permute-start(bf16[128,512]{1,0:T(8,128)(2,1)S(1)} %get-tuple-element.24.rest_5_.refs_6_), channel_id=1, source_target_pairs={{0,6},{1,7},{2,4},{3,5},{4,2},{5,3},{6,0},{7,1},{8,14},{9,15},{10,... | collective-permute-start | bytes 393224 | tf_op jit(solution)/shard_map/ppermute | solution.py:691
  35.6 0.7 %collective-permute-start.9 = (bf16[384,512]{1,0:T(8,128)(2,1)S(1)}, bf16[384,512]{1,0:T(8,128)(2,1)S(1)}, u32[]{:S(2)}, u32[]{:S(2)}) collective-permute-start(bf16[384,512]{1,0:T(8,128)(2,1)S(1)} %get-tuple-element.29), channel_id=1, source_target_pairs={{0,2},{1,3},{2,0},{3,1},{4,6},{5,7},{6,4},{7,5},{8,10},{9,11},{10,... | collective-permute-start | bytes 1179656 | tf_op jit(solution)/shard_map/ppermute | solution.py:691
  36.3 8.3 %shard_map.81 = (bf16[2,128,2048]{2,1,0:T(8,128)(2,1)}, f32[2,2,640]{2,1,0:T(2,128)}, f32[8,128]{1,0:T(8,128)S(1)}, bf16[512,2048]{1,0:T(8,128)(2,1)}, bf16[384,...) custom-call(s32[2]{0:T(128)S(1)} %copy-done.3, ...), custom_call_target="tpu_custom_call", output_to_operand_aliasing={{0}: (8, {}), {1}: (9, {})} | custom-call | flops 10000000000 | bytes 10000000 | tf_op jit(solution)/shard_map/pallas_call | solution.py:813
  44.6 2.0 %shard_map.82.refs_10_ = s32[2,512,2]{2,1,0:T(8,128)S(1)} custom-call(s32[2]{0:T(128)S(1)} %copy-done.3, bf16[144,512]{1,0:T(8,128)(2,1)S(1)} %collective-permute-done.3.x_own.refs_0_, bf16[272,512]{1,0:T(8,128)(2,1)S(1)} %collective-permute-done.8.rest_1_.x_beside.refs_1_, bf16[144,512]{1,0:T(8,128)(2,1)S(1)} %collective-permute-done.4.d_own.refs_3_, ...), custom_call_target="tpu_custom_call" | custom-call | flops 1000000 | bytes 1 | tf_op jit(solution)/shard_map/pallas_call | solution.py:840
  46.7 0.2 collective-permute-done.9.refs_2_
  46.9 0.7 %shard_map.83 = bf16[1024,512]{1,0:T(8,128)(2,1)S(1)} custom-call(bf16[144,512]{1,0:T(8,128)(2,1)S(1)} %collective-permute-done.3.x_own.refs_0_, bf16[272,512]{1,0:T(8,128)(2,1)S(1)} %collective-permute-done.8.rest_1_.x_beside.refs_1_, bf16[384,512]{1,0:T(8,128)(2,1)S(1)} %collective-permute-done.9.refs_2_, ...), custom_call_target="tpu_custom_call" | custom-call | flops 2000000000 | bytes 4000000 | tf_op jit(solution)/shard_map/pallas_call | solution.py:851
  47.6 0.1 collective-permute-start.13
  47.7 1.5 %shard_map.84._ = bf16[512,2048]{1,0:T(8,128)(2,1)} custom-call(bf16[144,512]{1,0:T(8,128)(2,1)S(1)} %collective-permute-done.3.x_own.refs_0_, bf16[272,512]{1,0:T(8,128)(2,1)S(1)} %collective-permute-done.8.rest_1_.x_beside.refs_1_, bf16[384,512]{1,0:T(8,128)(2,1)S(1)} %collective-permute-done.9.refs_2_, ...), custom_call_target="tpu_custom_call", output_to_operand_aliasing={{}: (11, {})} | custom-call | flops 2000000000 | bytes 4000000 | tf_op jit(solution)/shard_map/pallas_call | solution.py:861
  49.2 1.1 %collective-permute-done.13.sent_ref = bf16[1024,512]{1,0:T(8,128)(2,1)S(1)} collective-permute-done((bf16[1024,512]{1,0:T(8,128)(2,1)S(1)}, bf16[1024,512]{1,0:T(8,128)(2,1)S(1)}, u32[]{:S(2)}, u32[]{:S(2)}) %collective-permute-start.13) | collective-permute-done | bytes 1048608 | tf_op jit(solution)/shard_map/ppermute | solution.py:691
  50.3 1.0 %shard_map.85 = bf16[512,2048]{1,0:T(8,128)(2,1)} custom-call(bf16[1024,512]{1,0:T(8,128)(2,1)S(1)} %collective-permute-done.13.sent_ref, bf16[512,2048]{1,0:T(8,128)(2,1)} %shard_map.84._), custom_call_target="tpu_custom_call", output_to_operand_aliasing={{}: (1, {})} | custom-call | bytes 1000000 | tf_op jit(solution)/shard_map/pallas_call | solution.py:878
  (14 shorter events, 0.1 us)
Async XLA Ops:
  0.6 26.2 %copy-start.2 = (bf16[2,128,2048]{2,1,0:T(8,128)(2,1)S(1)}, bf16[2,128,2048]{2,1,0:T(8,128)(2,1)}, u32[]{:S(2)}) copy-start(bf16[2,128,2048]{2,1,0:T(8,128)(2,1)} %q_ref.3) | copy-start | bytes 3145732
  0.6 26.2 %copy-start.3 = (s32[2]{0:T(128)S(1)}, s32[2]{0:T(128)}, u32[]{:S(2)}) copy-start(s32[2]{0:T(128)} %offsets_ref.7) | copy-start | bytes 28
  3.3 13.1 %collective-permute-start.2 = (bf16[272,512]{1,0:T(8,128)(2,1)}, bf16[272,512]{1,0:T(8,128)(2,1)S(1)}, u32[]{:S(2)}, u32[]{:S(2)}) collective-permute-start(bf16[272,512]{1,0:T(8,128)(2,1)} %get-tuple-element.19.both.both_ref.rest_0_), channel_id=1, source_target_pairs={{0,4},{4,0},{8,12},{12,8},{16,20},{20,16},{24,28},{28,24},{1,5},{5... | collective-permute-start | bytes 835592 | tf_op jit(solution)/shard_map/ppermute | solution.py:691
  6.3 13.9 %collective-permute-start = (bf16[272,512]{1,0:T(8,128)(2,1)}, bf16[272,512]{1,0:T(8,128)(2,1)S(1)}, u32[]{:S(2)}, u32[]{:S(2)}) collective-permute-start(bf16[272,512]{1,0:T(8,128)(2,1)} %get-tuple-element.19.both.both_ref.rest_0_), channel_id=1, source_target_pairs={{0,8},{4,12},{8,16},{12,20},{16,24},{20,28},{24,0},{28,4},{1,9},{5... | collective-permute-start | bytes 835592 | tf_op jit(solution)/shard_map/ppermute | solution.py:691
  7.9 7.8 %collective-permute-start.4 = (bf16[144,512]{1,0:T(8,128)(2,1)}, bf16[144,512]{1,0:T(8,128)(2,1)S(1)}, u32[]{:S(2)}, u32[]{:S(2)}) collective-permute-start(bf16[144,512]{1,0:T(8,128)(2,1)} %get-tuple-element.20), channel_id=1, source_target_pairs={{0,6},{1,7},{2,4},{3,5},{4,2},{5,3},{6,0},{7,1},{8,14},{9,15},{10,... | collective-permute-start | bytes 442376 | tf_op jit(solution)/shard_map/ppermute | solution.py:691
  9.4 7.0 %collective-permute-start.3 = (bf16[144,512]{1,0:T(8,128)(2,1)}, bf16[144,512]{1,0:T(8,128)(2,1)S(1)}, u32[]{:S(2)}, u32[]{:S(2)}) collective-permute-start(bf16[144,512]{1,0:T(8,128)(2,1)} %get-tuple-element.20), channel_id=1, source_target_pairs={{0,2},{1,3},{2,0},{3,1},{4,6},{5,7},{6,4},{7,5},{8,10},{9,11},{10,... | collective-permute-start | bytes 442376 | tf_op jit(solution)/shard_map/ppermute | solution.py:691
  9.9 10.3 %collective-permute-start.1 = (bf16[144,512]{1,0:T(8,128)(2,1)}, bf16[144,512]{1,0:T(8,128)(2,1)S(1)}, u32[]{:S(2)}, u32[]{:S(2)}) collective-permute-start(bf16[144,512]{1,0:T(8,128)(2,1)} %get-tuple-element.20), channel_id=1, source_target_pairs={{0,24},{4,28},{8,0},{12,4},{16,8},{20,12},{24,16},{28,20},{1,25},{... | collective-permute-start | bytes 442376 | tf_op jit(solution)/shard_map/ppermute | solution.py:691
  16.4 1.0 %copy-start = (bf16[272,512]{1,0:T(8,128)(2,1)S(1)}, bf16[272,512]{1,0:T(8,128)(2,1)}, u32[]{:S(2)}) copy-start(bf16[272,512]{1,0:T(8,128)(2,1)} %get-tuple-element.19.both.both_ref.rest_0_) | copy-start | bytes 835588
  17.3 9.5 %copy-start.1 = (bf16[272,512]{1,0:T(8,128)(2,1)S(1)}, bf16[272,512]{1,0:T(8,128)(2,1)}, u32[]{:S(2)}) copy-start(bf16[272,512]{1,0:T(8,128)(2,1)} %get-tuple-element.19.both.both_ref.rest_0_) | copy-start | bytes 835588
  17.4 15.2 %collective-permute-start.5 = (bf16[288,512]{1,0:T(8,128)(2,1)S(1)}, bf16[288,512]{1,0:T(8,128)(2,1)S(1)}, u32[]{:S(2)}, u32[]{:S(2)}) collective-permute-start(bf16[288,512]{1,0:T(8,128)(2,1)S(1)} %shard_map.77._), channel_id=1, source_target_pairs={{0,16},{4,20},{8,24},{12,28},{16,0},{20,4},{24,8},{28,12},{1,17},{... | collective-permute-start | bytes 884744 | tf_op jit(solution)/shard_map/ppermute | solution.py:691
  20.3 8.1 %collective-permute-start.8 = (bf16[272,512]{1,0:T(8,128)(2,1)S(1)}, bf16[272,512]{1,0:T(8,128)(2,1)S(1)}, u32[]{:S(2)}, u32[]{:S(2)}) collective-permute-start(bf16[272,512]{1,0:T(8,128)(2,1)S(1)} %get-tuple-element.21.rest_1_), channel_id=1, source_target_pairs={{0,2},{1,3},{2,0},{3,1},{4,6},{5,7},{6,4},{7,5},{8,10},{9,11},{10,... | collective-permute-start | bytes 835592 | tf_op jit(solution)/shard_map/ppermute | solution.py:691
  21.8 7.8 %collective-permute-start.6 = (bf16[272,512]{1,0:T(8,128)(2,1)S(1)}, bf16[272,512]{1,0:T(8,128)(2,1)S(1)}, u32[]{:S(2)}, u32[]{:S(2)}) collective-permute-start(bf16[272,512]{1,0:T(8,128)(2,1)S(1)} %get-tuple-element.21.rest_1_), channel_id=1, source_target_pairs={{0,4},{4,0},{8,12},{12,8},{16,20},{20,16},{24,28},{28,24},{1,5},{5... | collective-permute-start | bytes 835592 | tf_op jit(solution)/shard_map/ppermute | solution.py:691
  23.4 6.0 %collective-permute-start.7 = (bf16[128,512]{1,0:T(8,128)(2,1)S(1)}, bf16[128,512]{1,0:T(8,128)(2,1)S(1)}, u32[]{:S(2)}, u32[]{:S(2)}) collective-permute-start(bf16[128,512]{1,0:T(8,128)(2,1)S(1)} %get-tuple-element.22.relay), channel_id=1, source_target_pairs={{0,8},{4,12},{24,16},{28,20},{1,9},{5,13},{25,17},{29,21},{2,10},{... | collective-permute-start | bytes 393224 | tf_op jit(solution)/shard_map/ppermute | solution.py:691
  28.4 16.3 %collective-permute-start.10 = (bf16[272,512]{1,0:T(8,128)(2,1)S(1)}, bf16[272,512]{1,0:T(8,128)(2,1)S(1)}, u32[]{:S(2)}, u32[]{:S(2)}) collective-permute-start(bf16[272,512]{1,0:T(8,128)(2,1)S(1)} %collective-permute-done.8.rest_1_.x_beside.refs_1_), channel_id=1, source_target_pairs={{0,4},{4,0},{8,12},{12,8},{16,20},{20,16},{24,28},{28,24},{1,5},{5... | collective-permute-start | bytes 835592 | tf_op jit(solution)/shard_map/ppermute | solution.py:691
  32.8 13.9 %collective-permute-start.12 = (bf16[128,512]{1,0:T(8,128)(2,1)S(1)}, bf16[128,512]{1,0:T(8,128)(2,1)S(1)}, u32[]{:S(2)}, u32[]{:S(2)}) collective-permute-start(bf16[128,512]{1,0:T(8,128)(2,1)S(1)} %get-tuple-element.24.rest_5_.refs_6_), channel_id=1, source_target_pairs={{0,4},{4,0},{8,12},{12,8},{16,20},{20,16},{24,28},{28,24},{1,5},{5... | collective-permute-start | bytes 393224 | tf_op jit(solution)/shard_map/ppermute | solution.py:691
  34.5 12.2 %collective-permute-start.11 = (bf16[128,512]{1,0:T(8,128)(2,1)S(1)}, bf16[128,512]{1,0:T(8,128)(2,1)S(1)}, u32[]{:S(2)}, u32[]{:S(2)}) collective-permute-start(bf16[128,512]{1,0:T(8,128)(2,1)S(1)} %get-tuple-element.24.rest_5_.refs_6_), channel_id=1, source_target_pairs={{0,6},{1,7},{2,4},{3,5},{4,2},{5,3},{6,0},{7,1},{8,14},{9,15},{10,... | collective-permute-start | bytes 393224 | tf_op jit(solution)/shard_map/ppermute | solution.py:691
  35.6 11.3 %collective-permute-start.9 = (bf16[384,512]{1,0:T(8,128)(2,1)S(1)}, bf16[384,512]{1,0:T(8,128)(2,1)S(1)}, u32[]{:S(2)}, u32[]{:S(2)}) collective-permute-start(bf16[384,512]{1,0:T(8,128)(2,1)S(1)} %get-tuple-element.29), channel_id=1, source_target_pairs={{0,2},{1,3},{2,0},{3,1},{4,6},{5,7},{6,4},{7,5},{8,10},{9,11},{10,... | collective-permute-start | bytes 1179656 | tf_op jit(solution)/shard_map/ppermute | solution.py:691
  47.6 2.7 %collective-permute-start.13 = (bf16[1024,512]{1,0:T(8,128)(2,1)S(1)}, bf16[1024,512]{1,0:T(8,128)(2,1)S(1)}, u32[]{:S(2)}, u32[]{:S(2)}) collective-permute-start(bf16[1024,512]{1,0:T(8,128)(2,1)S(1)} %shard_map.83), channel_id=1, source_target_pairs={{0,1},{1,0},{2,3},{3,2},{4,5},{5,4},{6,7},{7,6},{8,9},{9,8},{10,11... | collective-permute-start | bytes 3145736 | tf_op jit(solution)/shard_map/ppermute | solution.py:691
where the time goes:
time: 51.7 us; the launch traced here: 51.5 us
  starting transfers between devices  22.4 us (43%)
  Pallas kernels  17.9 us (35%)
  waiting for transfers between devices  9.27 us (18%)
  local copies, waits for them, and re-layouts  0.97 us (2%)
  between operations  0.94 us (2%)
    ppermute x14, starting transfers between devices, send(): return lax.ppermute(value, axis, pairs)  22.4 us
    ppermute x14, waiting for transfers between devices, send(): return lax.ppermute(value, axis, pairs)  9.27 us
    pallas_call x1, Pallas kernels, local_in_planes(): pl.pallas_call(early_kernel, grid_spec=pltpu.PrefetchScalarGridSpec(num_s...  8.29 us
    pallas_call x1, Pallas kernels, local_in_planes(): pl.pallas_call(prepare_kernel, out_shape=(piece(2 * span + NOTES), piece(...  2.65 us
    pallas_call x1, Pallas kernels, local_in_planes(): pl.pallas_call(far_index_kernel, out_shape=slots_shape, in_specs=[smem] +...  2.04 us
    pallas_call x1, Pallas kernels, local_in_planes(): pl.pallas_call(far_kept_kernel, out_shape=cache_shape, in_specs=[vmem] *...  1.53 us
    pallas_call x1, Pallas kernels, local_in_planes(): pl.pallas_call(late_kernel, grid_spec=pltpu.PrefetchScalarGridSpec(num_sc...  1.39 us
  transfers between devices with their start and end apart: 14, of which 9 were waited for; matrix products, arithmetic and copies ran while one was open for 0% of the time, Pallas kernels for 26%

commit v1 on v0

--- a/solution.py
+++ b/solution.py
@@ -15,6 +15,7 @@
 PLANE_BYTES = 28 * 1024 * 1024
 NOTES = 16
 BANDS = 4
+GROUP = 8
 
 
 def look_up(state, keep, fresh):
@@ -345,14 +346,6 @@
     ).astype(jnp.bfloat16)
 
 
-def going_kernel(both, y_own, x_own, d_own, going_ref):
-    span = both.shape[0] // 2 - NOTES // 2
-    going_ref[:span, :] = both[:span, :]
-    going_ref[span : 2 * span, :] = y_own[:span, :]
-    going_ref[2 * span : 2 * span + NOTES, :] = two_notes(both, 2 * span, y_own, 2 * span)
-    going_ref[2 * span + NOTES :, :] = two_notes(x_own, span, d_own, span)
-
-
 def beside_kernel(below, above, both, _, beside_ref, relay_ref):
     span = relay_ref.shape[0]
     beside_ref[:span, :] = below[:span, :]
@@ -369,17 +362,17 @@
         relay_ref[...] = both[span : 2 * span, :]
 
 
-def join_second_kernel(beyond, relay, relayed, *rest):
-    out_ref, late_ref = rest[-2:]
+def beyond_kernel(far_level, relay, relayed, *rest):
+    out_ref = rest[-1]
     span = relay.shape[0]
     level = lax.axis_index("ctx") // 2
-    out_ref[: 2 * span, :] = beyond[: 2 * span, :]
+    out_ref[:span, :] = far_level[:span, :]
+    out_ref[2 * span :, :] = far_level[span:, :]
     for ref, chosen in ((relay, (level == 0) | (level == 3)), (relayed, (level == 1) | (level == 2))):
 
         @pl.when(chosen)
         def _(ref=ref):
-            out_ref[2 * span :, :] = ref[...]
-            late_ref[...] = ref[...]
+            out_ref[span : 2 * span, :] = ref[...]
 
 
 def place_of(turn, flip, shards):
@@ -475,31 +468,25 @@
         slots[shard * cap : (shard + 1) * cap, :] = tokens.astype(jnp.int32)
 
 
-def place_bands(slots, tokens, out_ref, bands, total_bands):
+def place_bands(slots, tokens, late_tokens, out_ref):
     rows, heads = slots.shape
     reach = tokens.shape[0]
-    band = rows // total_bands
+    band = rows // BANDS
     for head in range(heads):
         lanes = slice(head * WIDTH, (head + 1) * WIDTH)
-        for order, index in enumerate(bands):
+        for index in range(BANDS):
             part = slots[index * band : (index + 1) * band, head : head + 1]
-            found = picked(part, 1, tokens[: (index + 1) * reach // total_bands, lanes])
-            out_ref[order * band : (order + 1) * band, lanes] = found.astype(jnp.bfloat16)
-
-
-def add_late(slots, first, late_tokens, out_ref, base):
-    band, heads = slots.shape
-    for head in range(heads):
-        lanes = slice(head * WIDTH, (head + 1) * WIDTH)
-        found = picked(slots[:, head : head + 1], first, late_tokens[:, lanes])
-        out_ref[base : base + band, lanes] += found.astype(jnp.bfloat16)
-
-
-def attend_columns(q_ref, head, rows, seen, out_ref, score_ref):
+            found = picked(part, 1, tokens[: (index + 1) * reach // BANDS, lanes])
+            if index == BANDS - 1:
+                found += picked(part, reach + 1, late_tokens[:, lanes])
+            out_ref[index * band : (index + 1) * band, lanes] = found.astype(jnp.bfloat16)
+
+
+def attend_columns(q_ref, base, rows, seen, out_ref):
     span = q_ref.shape[1]
     total = rows.shape[0]
     cache = total - span
-    group = q_ref.shape[2] // (score_ref.shape[1] * HEAD)
+    group = GROUP
     keys, values = rows[:, :HEAD], rows[:, HEAD:]
     flat = jnp.transpose(values.astype(jnp.float32)).astype(jnp.bfloat16)
     lane = lax.broadcasted_iota(jnp.int32, (total, HEAD), 1)
@@ -515,7 +502,7 @@
     scale = math.log2(math.e) / math.sqrt(HEAD)
     mass = None
     for pair in range(group // 2):
-        first = (head * group + 2 * pair) * HEAD
+        first = base + 2 * pair * HEAD
         query = jnp.concatenate(
             [
                 q_ref[0, :, first : first + HEAD],
@@ -537,14 +524,16 @@
             out_ref[0, :, lanes] = mixed[member * span : (member + 1) * span].astype(
                 jnp.bfloat16
             )
-    score_ref[0, head : head + 1, :] = jnp.sum(jnp.transpose(mass), axis=0, keepdims=True)
-
-
-def late_kernel(offsets_ref, q_ref, both_ref, beside_ref, out_ref, score_ref, done_ref):
+    return jnp.sum(jnp.transpose(mass), axis=0, keepdims=True)
+
+
+def late_kernel(head, offsets_ref, q_ref, both_ref, beside_ref, *rest):
+    out_ref, score_ref = rest[-2:]
     mine, shards = lax.axis_index("ctx"), lax.axis_size("ctx")
-    heads, cache = score_ref.shape[1], score_ref.shape[2] - q_ref.shape[1]
     span = q_ref.shape[1]
-    done_ref[...] = jnp.zeros(done_ref.shape, jnp.float32)
+    cache = score_ref.shape[1] - span
+    heads = both_ref.shape[1] // WIDTH
+    lanes = slice(head * WIDTH, (head + 1) * WIDTH)
 
     @pl.when(mine >= shards - 2)
     def _():
@@ -552,15 +541,12 @@
         state = jnp.where(keep >= cache, keep - cache + 1, 0)
         state = jnp.where(mine == shards - 1, state, 0).astype(jnp.float32)
         state = jnp.concatenate([state, jnp.zeros((8 - heads, cache), jnp.float32)], axis=0)
-        columns = jnp.transpose(state).astype(jnp.int32)
-        for head in range(heads):
-            lanes = slice(head * WIDTH, (head + 1) * WIDTH)
-            column = columns[:, head : head + 1]
-            cached = picked(column, 1, beside_ref[span : 2 * span, lanes])
-            rows = jnp.concatenate(
-                [cached.astype(jnp.bfloat16), both_ref[span : 2 * span, lanes]], axis=0
-            )
-            attend_columns(q_ref, head, rows, column, out_ref, score_ref)
+        column = jnp.transpose(state).astype(jnp.int32)[:, head : head + 1]
+        cached = picked(column, 1, beside_ref[span : 2 * span, lanes])
+        rows = jnp.concatenate(
+            [cached.astype(jnp.bfloat16), both_ref[span : 2 * span, lanes]], axis=0
+        )
+        score_ref[...] = attend_columns(q_ref, 0, rows, column, out_ref)
 
     @pl.when(mine < shards - 2)
     def _():
@@ -585,89 +571,73 @@
 
 
 def early_kernel(offsets_ref, q_ref, *rest):
-    both, beside, beyond, y_own, y_beside = rest[:5]
-    out_ref, score_ref, done_ref, cache_ref, top_sent, low_ref, slots_ref = rest[8:15]
-    tokens, top, sem, keeps, dests, coded = rest[15:]
+    both, beside, beyond, y_own, y_beside, y_beyond = rest[:6]
+    late_scores = rest[6:8]
+    out_ref, score_ref, done_ref, cache_ref, sent_ref, *rest = rest[9:]
+    tokens, late_tokens, kept, slots, keeps, dests, coded, sem = rest
     done_ref[...] = jnp.zeros(done_ref.shape, jnp.float32)
-    span = both.shape[0] // 2 - NOTES // 2
-    column = lax.axis_index("kv")
+    span = q_ref.shape[1]
+    early = early_of(offsets_ref)
     at = 2 * span
     notes = [(both, at, 0, 0, 0), (beside, at, 0, 1, 0), (beside, at, 1, 3, 0)]
-    notes += [(beyond, at, 0, 2, 0), (beyond, at, 1, 2, 1), (y_own, at, 0, 0, 1)]
-    notes += [(y_beside, at, 0, 1, 1), (y_beside, at, 1, 3, 1)]
-    own = fill_slots(offsets_ref, notes, keeps, dests, coded, slots_ref)
+    notes += [(beyond, at, 0, 2, 0), (y_own, at, 0, 0, 1), (y_beside, at, 0, 1, 1)]
+    notes += [(y_beside, at, 1, 3, 1), (y_beyond, at, 0, 2, 1)]
+    own = fill_slots(offsets_ref, notes, keeps, dests, coded, slots)
     own = jnp.transpose(own.astype(jnp.float32)).astype(jnp.int32)
     pieces = [(both, 0, 0, 0), (beside, 0, 1, 0), (beside, span, 3, 0), (beyond, 0, 2, 0)]
-    pieces += [(beyond, span, 2, 1), (y_own, 0, 0, 1), (y_beside, 0, 1, 1), (y_beside, span, 3, 1)]
+    pieces += [(y_own, 0, 0, 1), (y_beside, 0, 1, 1), (y_beside, span, 3, 1), (y_beyond, 0, 2, 1)]
     sort_tokens(pieces, tokens, span)
-    bands = tuple(range(BANDS - 1))
-    place_bands(slots_ref.at[0], tokens, top, bands, BANDS)
-    copy = pltpu.make_async_copy(top, output_part(cache_ref, 0, top.shape[0], column), sem)
+    sort_late([(beyond, span), (y_beyond, span)], late_tokens)
+    place_bands(slots.at[0], tokens, late_tokens, kept)
+    column = lax.axis_index("kv")
+    copy = pltpu.make_async_copy(kept, output_part(cache_ref, 0, kept.shape[0], column), sem)
     copy.start()
-    place_bands(slots_ref.at[1], tokens, top_sent, bands, BANDS)
-    for flip in range(2):
-        place_bands(slots_ref.at[flip], tokens, low_ref.at[flip], (BANDS - 1,), BANDS)
+    place_bands(slots.at[1], tokens, late_tokens, sent_ref)
     for head in range(score_ref.shape[1]):
         lanes = slice(head * WIDTH, (head + 1) * WIDTH)
         chosen = own[:, head : head + 1]
         cached = picked(chosen, 1, tokens[:, lanes]).astype(jnp.bfloat16)
         rows = jnp.concatenate([cached, both[:span, lanes]], axis=0)
-        attend_columns(q_ref, head, rows, chosen, out_ref, score_ref)
+        mass = attend_columns(q_ref, head * GROUP * HEAD, rows, chosen, out_ref)
+        score_ref[early, head : head + 1, :] = mass
+        score_ref[1 - early, head : head + 1, :] = late_scores[head][...]
     copy.wait()
 
 
-def far_index_kernel(offsets_ref, x_own, x_beside, d_own, d_beside, beyond, _, *rest):
+def far_index_kernel(offsets_ref, x_own, x_beside, x_beyond, d_own, d_beside, d_beyond, _, *rest):
     slots_ref, keeps, dests, coded = rest
     span = x_own.shape[0] - NOTES
     at = 2 * span
     notes = [(x_own, span, 0, 0, 0), (d_own, span, 0, 0, 1), (x_beside, at, 0, 1, 0)]
     notes += [(x_beside, at, 1, 3, 0), (d_beside, at, 0, 1, 1), (d_beside, at, 1, 3, 1)]
-    notes += [(beyond, at + NOTES, 0, 2, 0), (beyond, at + NOTES, 1, 2, 1)]
+    notes += [(x_beyond, at, 0, 2, 0), (d_beyond, at, 0, 2, 1)]
     fill_slots(offsets_ref, notes, keeps, dests, coded, slots_ref)
 
 
-def far_rows(flip, refs, far_ref, low, tokens, near_late, far_late):
-    x_own, x_beside, x_end, d_own, d_beside, d_late, late, y_late, low_ref = refs[:9]
-    near_slots, far_slots = refs[9:]
-    span = late.shape[0]
-    rows = far_slots.shape[1]
-    band = rows // BANDS
-    first = tokens.shape[0] + 1
-    last = pl.ds(rows - band, band)
-    sort_late([(late, 0), (y_late, 0)], near_late)
-    sort_late([(x_end, 2 * span), (d_late, 0)], far_late)
-    low[...] = low_ref[flip]
-    add_late(near_slots.at[flip, last], first, near_late, low, 0)
-    pieces = [(x_own, 0, 0, 0), (x_beside, 0, 1, 0), (x_beside, span, 3, 0), (x_end, 0, 2, 0)]
-    pieces += [(x_end, span, 2, 1), (d_own, 0, 0, 1), (d_beside, 0, 1, 1), (d_beside, span, 3, 1)]
+def far_rows(flip, refs, far_ref, tokens, late_tokens):
+    x_own, x_beside, x_beyond, d_own, d_beside, d_beyond, slots = refs
+    span = x_own.shape[0] - NOTES
+    pieces = [(x_own, 0, 0, 0), (x_beside, 0, 1, 0), (x_beside, span, 3, 0), (x_beyond, 0, 2, 0)]
+    pieces += [(d_own, 0, 0, 1), (d_beside, 0, 1, 1), (d_beside, span, 3, 1), (d_beyond, 0, 2, 1)]
     sort_tokens(pieces, tokens, span)
-    place_bands(far_slots.at[flip], tokens, far_ref, tuple(range(BANDS)), BANDS)
-    add_late(far_slots.at[flip, last], first, far_late, far_ref, rows - band)
+    sort_late([(x_beyond, span), (d_beyond, span)], late_tokens)
+    place_bands(slots.at[flip], tokens, late_tokens, far_ref)
 
 
 def far_sent_kernel(*refs):
-    top_ref, sent_ref = refs[11:13]
-    rows = refs[10].shape[1]
-    upper = rows + top_ref.shape[0]
-    sent_ref[rows:upper, :] = top_ref[...]
-    far_rows(1, refs[:11], sent_ref.at[:rows], sent_ref.at[upper:], *refs[13:])
+    near_ref, sent_ref, tokens, late_tokens = refs[7:]
+    rows = near_ref.shape[0]
+    sent_ref[rows:, :] = near_ref[...]
+    far_rows(1, refs[:7], sent_ref.at[:rows], tokens, late_tokens)
 
 
 def far_kept_kernel(*refs):
-    cache_ref, far, low, tokens, near_late, far_late, sems = refs[12:]
+    cache_ref, far, tokens, late_tokens, sem = refs[8:]
+    far_rows(0, refs[:7], far, tokens, late_tokens)
     column = lax.axis_index("kv")
-    rows, band = far.shape[0], low.shape[0]
-    far_rows(0, refs[:11], far, low, tokens, near_late, far_late)
-    copies = [
-        pltpu.make_async_copy(far, output_part(cache_ref, 0, rows, column ^ 2), sems.at[0]),
-        pltpu.make_async_copy(
-            low, output_part(cache_ref, rows - band, band, column), sems.at[1]
-        ),
-    ]
-    for copy in copies:
-        copy.start()
-    for copy in copies:
-        copy.wait()
+    copy = pltpu.make_async_copy(far, output_part(cache_ref, 0, far.shape[0], column ^ 2), sem)
+    copy.start()
+    copy.wait()
 
 
 def last_kernel(sent_ref, _, cache_ref, sems):
@@ -741,17 +711,9 @@
         cost_estimate=cost(10**9, 1),
     )(offsets, kv_rows, keep, jnp.transpose(dest))
 
-    below, above = along_z(both, 1), along_z(single, 3)
-    y_own, x_own, d_own = across_y(both), across_x(single), across_both(single)
-    going = pl.pallas_call(
-        going_kernel,
-        out_shape=piece(2 * span + 2 * NOTES),
-        in_specs=[vmem] * 4,
-        out_specs=vmem,
-        compiler_params=params,
-        cost_estimate=cost(0, 10**6),
-    )(both, y_own, x_own, d_own)
-    beyond = along_z(going, 2)
+    below, above, far_level = along_z(both, 1), along_z(single, 3), along_z(single, 2)
+    y_own, x_own = across_y(both), across_x(single)
+    d_own = across_y(x_own)
     beside, relay = pl.pallas_call(
         beside_kernel,
         out_shape=(piece(2 * span + NOTES), piece(span)),
@@ -759,122 +721,124 @@
         out_specs=(vmem,) * 2,
         compiler_params=params,
         cost_estimate=cost(0, 10**6),
-    )(below, above, both, going)
+    )(below, above, both, x_own)
     relayed = send(relay, "ctx", [(0, 2), (1, 3), (6, 4), (7, 5)])
     y_beside, x_beside = across_y(beside), across_x(beside)
     d_beside = across_y(x_beside)
 
     attention_shape = jax.ShapeDtypeStruct((prompts, span, qwidth), jnp.bfloat16)
-    score_shape = jax.ShapeDtypeStruct((prompts, heads, cache + span), jnp.float32)
-
-    def prompt_specs(late):
+    half = qwidth // heads
+
+    def late_attention(head, *after):
         def block(_, offsets_ref):
-            early = early_of(offsets_ref)
-            return (1 - early if late else early, 0, 0)
-
-        return (
-            pl.BlockSpec((1, span, qwidth), block),
-            pl.BlockSpec((1, heads, cache + span), block),
-        )
-
-    attention, row_scores, late_done = pl.pallas_call(
-        late_kernel,
-        grid_spec=pltpu.PrefetchScalarGridSpec(
-            num_scalar_prefetch=1,
-            grid=(1,),
-            in_specs=[prompt_specs(True)[0], vmem, vmem],
-            out_specs=prompt_specs(True) + (vmem,),
-        ),
-        out_shape=(attention_shape, score_shape, jax.ShapeDtypeStruct((8, LANES), jnp.float32)),
-        compiler_params=params,
-        cost_estimate=cost(10**6, 1),
-    )(offsets, query, both, y_own)
-
-    end, late = pl.pallas_call(
-        join_second_kernel,
-        out_shape=(piece(3 * span), piece(span)),
+            return (1 - early_of(offsets_ref), 0, head)
+
+        spec = pl.BlockSpec((1, span, half), block)
+        return pl.pallas_call(
+            functools.partial(late_kernel, head),
+            grid_spec=pltpu.PrefetchScalarGridSpec(
+                num_scalar_prefetch=1,
+                grid=(1,),
+                in_specs=[spec, vmem, vmem] + [anywhere] * len(after),
+                out_specs=(spec, vmem),
+            ),
+            out_shape=(attention_shape, jax.ShapeDtypeStruct((1, cache + span), jnp.float32)),
+            input_output_aliases={4: 0} if head else {},
+            compiler_params=params,
+            cost_estimate=cost(5 * 10**9, 10**7),
+        )(offsets, query, both, y_own, *after)
+
+    attention, late_first = late_attention(0, far_level)
+    beyond = pl.pallas_call(
+        beyond_kernel,
+        out_shape=piece(2 * span + NOTES),
         in_specs=[vmem] * 3 + [anywhere] * 3,
-        out_specs=(vmem, vmem),
-        compiler_params=params,
-        cost_estimate=cost(10**6, 1),
-    )(beyond, relay, relayed, y_beside, x_beside, late_done)
-    d_late, y_late, x_end = across_both(late), across_y(late), across_x(end)
+        out_specs=vmem,
+        compiler_params=params,
+        cost_estimate=cost(0, 10**6),
+    )(far_level, relay, relayed, y_beside, x_beside, late_first)
+    y_beyond, x_beyond = across_y(beyond), across_x(beyond)
+    attention, late_second = late_attention(1, attention, beyond)
+    d_beyond = across_x(y_beyond)
 
     tokens = pltpu.VMEM((shards * span, width), jnp.bfloat16)
     late_tokens = pltpu.VMEM((2 * span, width), jnp.bfloat16)
+    block_rows = pltpu.VMEM((rows, width), jnp.bfloat16)
     cache_shape = jax.ShapeDtypeStruct((rows, columns * width), jnp.bfloat16)
     slots_shape = jax.ShapeDtypeStruct((2, rows, heads), jnp.int32)
-    done_shape = jax.ShapeDtypeStruct((8, LANES), jnp.float32)
     tables = [
         pltpu.VMEM((shards, 4 * heads, cache), jnp.int32),
         pltpu.VMEM((shards, prompts, cache), jnp.int32),
         pltpu.VMEM((shards, 8 * heads, cache), jnp.bfloat16),
     ]
-    attention, row_scores, early_done, owner_cache, top, low, near_slots = pl.pallas_call(
+    early_spec = pl.BlockSpec(
+        (1, span, qwidth), lambda _, offsets_ref: (early_of(offsets_ref), 0, 0)
+    )
+    attention, row_scores, early_done, owner_cache, near_sent = pl.pallas_call(
         early_kernel,
         grid_spec=pltpu.PrefetchScalarGridSpec(
             num_scalar_prefetch=1,
             grid=(1,),
-            in_specs=[prompt_specs(False)[0]] + [vmem] * 5 + [anywhere] * 3,
-            out_specs=prompt_specs(False) + (vmem, hbm, vmem, vmem, vmem),
-            scratch_shapes=[
-                tokens,
-                pltpu.VMEM((rows - band, width), jnp.bfloat16),
-                pltpu.SemaphoreType.DMA,
-            ]
-            + tables,
+            in_specs=[early_spec] + [vmem] * 8 + [anywhere],
+            out_specs=(early_spec, vmem, vmem, hbm, vmem),
+            scratch_shapes=[tokens, late_tokens, block_rows]
+            + [pltpu.VMEM(slots_shape.shape, jnp.int32)]
+            + tables
+            + [pltpu.SemaphoreType.DMA],
         ),
         out_shape=(
             attention_shape,
-            score_shape,
-            done_shape,
+            jax.ShapeDtypeStruct((prompts, heads, cache + span), jnp.float32),
+            jax.ShapeDtypeStruct((8, LANES), jnp.float32),
             cache_shape,
-            piece(rows - band),
-            jax.ShapeDtypeStruct((2, band, width), jnp.bfloat16),
-            slots_shape,
+            piece(rows),
         ),
-        input_output_aliases={8: 0, 9: 1},
+        input_output_aliases={10: 0},
         compiler_params=params,
         cost_estimate=cost(10**10, 10**7),
-    )(offsets, query, both, beside, beyond, y_own, y_beside, late, attention, row_scores)
+    )(
+        offsets,
+        query,
+        both,
+        beside,
+        beyond,
+        y_own,
+        y_beside,
+        y_beyond,
+        late_first,
+        late_second,
+        attention,
+    )
+    far = (x_own, x_beside, x_beyond, d_own, d_beside, d_beyond)
     far_slots = pl.pallas_call(
         far_index_kernel,
         out_shape=slots_shape,
-        in_specs=[smem] + [vmem] * 5 + [anywhere],
+        in_specs=[smem] + [vmem] * 6 + [anywhere],
         out_specs=vmem,
         scratch_shapes=tables,
         compiler_params=params,
         cost_estimate=cost(10**6, 1),
-    )(offsets, x_own, x_beside, d_own, d_beside, beyond, early_done)
-    far = (x_own, x_beside, x_end, d_own, d_beside, d_late, late, y_late, low)
-    far += (near_slots, far_slots)
+    )(offsets, *far, early_done)
     sent = pl.pallas_call(
         far_sent_kernel,
         out_shape=piece(2 * rows),
-        in_specs=[vmem] * 12,
+        in_specs=[vmem] * 8,
         out_specs=vmem,
-        scratch_shapes=[tokens, late_tokens, late_tokens],
+        scratch_shapes=[tokens, late_tokens],
         compiler_params=params,
         cost_estimate=cost(2 * 10**9, 4 * 10**6),
-    )(*far, top)
+    )(*far, far_slots, near_sent)
     received = across_core(sent)
     owner_cache = pl.pallas_call(
         far_kept_kernel,
         out_shape=cache_shape,
-        in_specs=[vmem] * 11 + [hbm],
+        in_specs=[vmem] * 7 + [hbm],
         out_specs=hbm,
-        scratch_shapes=[
-            pltpu.VMEM((rows, width), jnp.bfloat16),
-            pltpu.VMEM((band, width), jnp.bfloat16),
-            tokens,
-            late_tokens,
-            late_tokens,
-            pltpu.SemaphoreType.DMA((2,)),
-        ],
-        input_output_aliases={11: 0},
+        scratch_shapes=[block_rows, tokens, late_tokens, pltpu.SemaphoreType.DMA],
+        input_output_aliases={7: 0},
         compiler_params=params,
         cost_estimate=cost(2 * 10**9, 4 * 10**6),
-    )(*far, owner_cache)
+    )(*far, far_slots, owner_cache)
     owner_cache = pl.pallas_call(
         last_kernel,
         out_shape=cache_shape,

time: 51.7 us -> 56.1 us (1.085)
  waiting for transfers between devices: 9.27 us -> 14.7 us
  starting transfers between devices: 22.4 us -> 18.9 us
  Pallas kernels: 17.9 us -> 19 us
  local copies, waits for them, and re-layouts: 0.97 us -> 1.92 us
    ppermute x14, waiting for transfers between devices: 9.27 us -> 14.7 us  [send(): return lax.ppermute(value, axis, pairs)]
    ppermute x14, starting transfers between devices: 22.4 us -> 18.9 us  [send(): return lax.ppermute(value, axis, pairs)]
    pallas_call x3, Pallas kernels: 1.63 us -> 2.79 us  [the longest x2 2.76 us: late_attention(): pl.pallas_call(functools.partial(late_kernel, head), grid_spec=pltpu.Pref...]
    unnamed x8 -> x10, local copies, waits for them, and re-layouts: 0.97 us -> 1.92 us
  transfers between devices with their start and end apart: 14 -> 14, of which waited for: 9 -> 6; matrix products, arithmetic and copies ran while one was open for 0% -> 0% of each run, Pallas kernels for 26% -> 23%
where the time goes in v1:
time: 56.1 us; the launch traced here: 55.4 us
  Pallas kernels  19 us (34%)
  starting transfers between devices  18.9 us (34%)
  waiting for transfers between devices  14.7 us (26%)
  local copies, waits for them, and re-layouts  1.92 us (3%)
  between operations  0.95 us (2%)
    ppermute x14, starting transfers between devices, send(): return lax.ppermute(value, axis, pairs)  18.9 us
    ppermute x14, waiting for transfers between devices, send(): return lax.ppermute(value, axis, pairs)  14.7 us
    pallas_call x1, Pallas kernels, local_in_planes(): pl.pallas_call(early_kernel, grid_spec=pltpu.PrefetchScalarGridSpec(num_s...  8.33 us
    pallas_call x2, Pallas kernels, late_attention(): pl.pallas_call(functools.partial(late_kernel, head), grid_spec=pltpu.Pref...  2.76 us
    pallas_call x1, Pallas kernels, local_in_planes(): pl.pallas_call(prepare_kernel, out_shape=(piece(2 * span + NOTES), piece(...  2.65 us
    pallas_call x1, Pallas kernels, local_in_planes(): pl.pallas_call(far_index_kernel, out_shape=slots_shape, in_specs=[smem] +...  2.04 us
    unnamed x10, local copies, waits for them, and re-layouts  1.92 us
    pallas_call x1, Pallas kernels, local_in_planes(): pl.pallas_call(far_kept_kernel, out_shape=cache_shape, in_specs=[vmem] *...  1.45 us
  transfers between devices with their start and end apart: 14, of which 6 were waited for; matrix products, arithmetic and copies ran while one was open for 0% of the time, Pallas kernels for 23%

profile of v1, /device:TPU:0, one launch (start us, length us, event | category | flops | bytes accessed | tf_op | source)
XLA Modules:
  0.0 55.4 jit_solution(13848617583421471206)
XLA Ops:
  0.7 2.7 %shard_map.76 = (bf16[272,512]{1,0:T(8,128)(2,1)}, bf16[144,512]{1,0:T(8,128)(2,1)}) custom-call(s32[2]{0:T(128)} %offsets_ref.9, bf16[2,128,512]{2,1,0:T(8,128)(2,1)} %kv_ref.1, s32[2,1,2,512]{3,2,1,0:T(2,128)} %keep_ref.1, s32[1,1024]{1,0:T(1,128)} %bitcast.1), custom_call_target="tpu_custom_call" | custom-call | flops 1000000000 | bytes 1 | tf_op jit(solution)/shard_map/pallas_call | solution.py:700
  3.3 3.1 %collective-permute-start = (bf16[272,512]{1,0:T(8,128)(2,1)}, bf16[272,512]{1,0:T(8,128)(2,1)S(1)}, u32[]{:S(2)}, u32[]{:S(2)}) collective-permute-start(bf16[272,512]{1,0:T(8,128)(2,1)} %get-tuple-element.16.both.both_ref.rest_0_), channel_id=1, source_target_pairs={{0,8},{4,12},{8,16},{12,20},{16,24},{20,28},{24,0},{28,4},{1,9},{5... | collective-permute-start | bytes 835592 | tf_op jit(solution)/shard_map/ppermute | solution.py:661
  6.4 1.5 %collective-permute-start.7 = (bf16[272,512]{1,0:T(8,128)(2,1)}, bf16[272,512]{1,0:T(8,128)(2,1)S(1)}, u32[]{:S(2)}, u32[]{:S(2)}) collective-permute-start(bf16[272,512]{1,0:T(8,128)(2,1)} %get-tuple-element.16.both.both_ref.rest_0_), channel_id=1, source_target_pairs={{0,4},{4,0},{8,12},{12,8},{16,20},{20,16},{24,28},{28,24},{1,5},{5... | collective-permute-start | bytes 835592 | tf_op jit(solution)/shard_map/ppermute | solution.py:661
  7.9 1.5 %collective-permute-start.2 = (bf16[144,512]{1,0:T(8,128)(2,1)}, bf16[144,512]{1,0:T(8,128)(2,1)S(1)}, u32[]{:S(2)}, u32[]{:S(2)}) collective-permute-start(bf16[144,512]{1,0:T(8,128)(2,1)} %get-tuple-element.17), channel_id=1, source_target_pairs={{0,2},{1,3},{2,0},{3,1},{4,6},{5,7},{6,4},{7,5},{8,10},{9,11},{10,... | collective-permute-start | bytes 442376 | tf_op jit(solution)/shard_map/ppermute | solution.py:661
  9.4 2.2 %collective-permute-start.1 = (bf16[144,512]{1,0:T(8,128)(2,1)}, bf16[144,512]{1,0:T(8,128)(2,1)S(1)}, u32[]{:S(2)}, u32[]{:S(2)}) collective-permute-start(bf16[144,512]{1,0:T(8,128)(2,1)} %get-tuple-element.17), channel_id=1, source_target_pairs={{0,24},{4,28},{8,0},{12,4},{16,8},{20,12},{24,16},{28,20},{1,25},{... | collective-permute-start | bytes 442376 | tf_op jit(solution)/shard_map/ppermute | solution.py:661
  11.6 0.8 %collective-permute-start.3 = (bf16[144,512]{1,0:T(8,128)(2,1)}, bf16[144,512]{1,0:T(8,128)(2,1)S(1)}, u32[]{:S(2)}, u32[]{:S(2)}) collective-permute-start(bf16[144,512]{1,0:T(8,128)(2,1)} %get-tuple-element.17), channel_id=1, source_target_pairs={{0,16},{4,20},{8,24},{12,28},{16,0},{20,4},{24,8},{28,12},{1,17},{... | collective-permute-start | bytes 442376 | tf_op jit(solution)/shard_map/ppermute | solution.py:661
  12.4 0.8 %collective-permute-done.2._.x_own.refs_0_ = bf16[144,512]{1,0:T(8,128)(2,1)S(1)} collective-permute-done((bf16[144,512]{1,0:T(8,128)(2,1)}, bf16[144,512]{1,0:T(8,128)(2,1)S(1)}, u32[]{:S(2)}, u32[]{:S(2)}) %collective-permute-start.2) | collective-permute-done | bytes 147488 | tf_op jit(solution)/shard_map/ppermute | solution.py:661
  13.3 0.5 collective-permute-start.10
  13.8 4.7 %collective-permute-done.1.above = bf16[144,512]{1,0:T(8,128)(2,1)S(1)} collective-permute-done((bf16[144,512]{1,0:T(8,128)(2,1)}, bf16[144,512]{1,0:T(8,128)(2,1)S(1)}, u32[]{:S(2)}, u32[]{:S(2)}) %collective-permute-start.1) | collective-permute-done | bytes 147488 | tf_op jit(solution)/shard_map/ppermute | solution.py:661
  18.4 0.0 collective-permute-done.below
  18.4 1.0 %copy-done = bf16[272,512]{1,0:T(8,128)(2,1)S(1)} copy-done((bf16[272,512]{1,0:T(8,128)(2,1)S(1)}, bf16[272,512]{1,0:T(8,128)(2,1)}, u32[]{:S(2)}) %copy-start) | copy-done | bytes 278552
  19.4 1.6 %collective-permute-start.6 = (bf16[272,512]{1,0:T(8,128)(2,1)S(1)}, bf16[272,512]{1,0:T(8,128)(2,1)S(1)}, u32[]{:S(2)}, u32[]{:S(2)}) collective-permute-start(bf16[272,512]{1,0:T(8,128)(2,1)S(1)} %get-tuple-element.18.rest_1_), channel_id=1, source_target_pairs={{0,2},{1,3},{2,0},{3,1},{4,6},{5,7},{6,4},{7,5},{8,10},{9,11},{10,... | collective-permute-start | bytes 835592 | tf_op jit(solution)/shard_map/ppermute | solution.py:661
  21.0 1.4 %collective-permute-start.5 = (bf16[272,512]{1,0:T(8,128)(2,1)S(1)}, bf16[272,512]{1,0:T(8,128)(2,1)S(1)}, u32[]{:S(2)}, u32[]{:S(2)}) collective-permute-start(bf16[272,512]{1,0:T(8,128)(2,1)S(1)} %get-tuple-element.18.rest_1_), channel_id=1, source_target_pairs={{0,4},{4,0},{8,12},{12,8},{16,20},{20,16},{24,28},{28,24},{1,5},{5... | collective-permute-start | bytes 835592 | tf_op jit(solution)/shard_map/ppermute | solution.py:661
  22.4 2.3 %collective-permute-done.3.rest_0_.far_level = bf16[144,512]{1,0:T(8,128)(2,1)S(1)} collective-permute-done((bf16[144,512]{1,0:T(8,128)(2,1)}, bf16[144,512]{1,0:T(8,128)(2,1)S(1)}, u32[]{:S(2)}, u32[]{:S(2)}) %collective-permute-start.3) | collective-permute-done | bytes 147488 | tf_op jit(solution)/shard_map/ppermute | solution.py:661
  24.8 2.9 %collective-permute-start.4 = (bf16[128,512]{1,0:T(8,128)(2,1)S(1)}, bf16[128,512]{1,0:T(8,128)(2,1)S(1)}, u32[]{:S(2)}, u32[]{:S(2)}) collective-permute-start(bf16[128,512]{1,0:T(8,128)(2,1)S(1)} %get-tuple-element.19.relay), channel_id=1, source_target_pairs={{0,8},{4,12},{24,16},{28,20},{1,9},{5,13},{25,17},{29,21},{2,10},{... | collective-permute-start | bytes 393224 | tf_op jit(solution)/shard_map/ppermute | solution.py:661
  27.7 0.0 copy-start.1
  27.7 0.9 %copy-done.1 = bf16[272,512]{1,0:T(8,128)(2,1)S(1)} copy-done((bf16[272,512]{1,0:T(8,128)(2,1)S(1)}, bf16[272,512]{1,0:T(8,128)(2,1)}, u32[]{:S(2)}) %copy-start.1) | copy-done | bytes 278552
  28.6 1.3 %shard_map.78 = (bf16[2,128,2048]{2,1,0:T(8,128)(2,1)}, f32[1,640]{1,0:T(1,128)S(1)}) custom-call(s32[2]{0:T(128)S(1)} %copy-done.3, bf16[2,128,2048]{2,1,0:T(8,128)(2,1)S(1)} %copy-done.4, bf16[272,512]{1,0:T(8,128)(2,1)S(1)} %copy-done.1, bf16[272,512]{1,0:T(8,128)(2,1)S(1)} %collective-permute-done.7.beside_ref.rest_3_, ...), custom_call_target="tpu_custom_call" | custom-call | flops 5000000000 | bytes 10000000 | tf_op jit(solution)/shard_map/pallas_call | solution.py:737
  29.9 0.2 collective-permute-done.4.relayed
  30.2 0.7 %collective-permute-start.8 = (bf16[272,512]{1,0:T(8,128)(2,1)S(1)}, bf16[272,512]{1,0:T(8,128)(2,1)S(1)}, u32[]{:S(2)}, u32[]{:S(2)}) collective-permute-start(bf16[272,512]{1,0:T(8,128)(2,1)S(1)} %shard_map.79.rest_1_.rest_2_), channel_id=1, source_target_pairs={{0,4},{4,0},{8,12},{12,8},{16,20},{20,16},{24,28},{28,24},{1,5},{5... | collective-permute-start | bytes 835592 | tf_op jit(solution)/shard_map/ppermute | solution.py:661
  30.9 1.5 %collective-permute-start.9 = (bf16[272,512]{1,0:T(8,128)(2,1)S(1)}, bf16[272,512]{1,0:T(8,128)(2,1)S(1)}, u32[]{:S(2)}, u32[]{:S(2)}) collective-permute-start(bf16[272,512]{1,0:T(8,128)(2,1)S(1)} %shard_map.79.rest_1_.rest_2_), channel_id=1, source_target_pairs={{0,2},{1,3},{2,0},{3,1},{4,6},{5,7},{6,4},{7,5},{8,10},{9,11},{10,... | collective-permute-start | bytes 835592 | tf_op jit(solution)/shard_map/ppermute | solution.py:661
  32.4 0.5 collective-permute-start.11
  32.9 1.5 %shard_map.80 = (bf16[2,128,2048]{2,1,0:T(8,128)(2,1)}, f32[1,640]{1,0:T(1,128)S(1)}) custom-call(s32[2]{0:T(128)S(1)} %copy-done.3, bf16[2,128,2048]{2,1,0:T(8,128)(2,1)S(1)} %copy-done.4, bf16[272,512]{1,0:T(8,128)(2,1)S(1)} %copy-done.2, bf16[272,512]{1,0:T(8,128)(2,1)S(1)} %collective-permute-done.7.beside_ref.rest_3_, ...), custom_call_target="tpu_custom_call", output_to_operand_aliasing={{0}: (4, {})} | custom-call | flops 5000000000 | bytes 10000000 | tf_op jit(solution)/shard_map/pallas_call | solution.py:737
  34.3 5.5 %collective-permute-done.8.rest_5_ = bf16[272,512]{1,0:T(8,128)(2,1)S(1)} collective-permute-done((bf16[272,512]{1,0:T(8,128)(2,1)S(1)}, bf16[272,512]{1,0:T(8,128)(2,1)S(1)}, u32[]{:S(2)}, u32[]{:S(2)}) %collective-permute-start.8) | collective-permute-done | bytes 278560 | tf_op jit(solution)/shard_map/ppermute | solution.py:661
  39.8 0.6 %collective-permute-start.12 = (bf16[272,512]{1,0:T(8,128)(2,1)S(1)}, bf16[272,512]{1,0:T(8,128)(2,1)S(1)}, u32[]{:S(2)}, u32[]{:S(2)}) collective-permute-start(bf16[272,512]{1,0:T(8,128)(2,1)S(1)} %collective-permute-done.8.rest_5_), channel_id=1, source_target_pairs={{0,2},{1,3},{2,0},{3,1},{4,6},{5,7},{6,4},{7,5},{8,10},{9,11},{10,... | collective-permute-start | bytes 835592 | tf_op jit(solution)/shard_map/ppermute | solution.py:661
  40.4 8.3 %shard_map.81 = (bf16[2,128,2048]{2,1,0:T(8,128)(2,1)}, f32[2,2,640]{2,1,0:T(2,128)}, f32[8,128]{1,0:T(8,128)S(1)}, bf16[512,2048]{1,0:T(8,128)(2,1)}, bf16[512,512]{1,0:T(8,128)(2,1)S(1)}) custom-call(s32[2]{0:T(128)S(1)} %copy-done.3, bf16[2,128,2048]{2,1,0:T(8,128)(2,1)S(1)} %copy-done.4, ...), custom_call_target="tpu_custom_call", output_to_operand_aliasing={{0}: (10, {})} | custom-call | flops 10000000000 | bytes 10000000 | tf_op jit(solution)/shard_map/pallas_call | solution.py:777
  48.8 2.0 %shard_map.82.refs_6_ = s32[2,512,2]{2,1,0:T(8,128)S(1)} custom-call(s32[2]{0:T(128)S(1)} %copy-done.3, bf16[144,512]{1,0:T(8,128)(2,1)S(1)} %collective-permute-done.2._.x_own.refs_0_, bf16[272,512]{1,0:T(8,128)(2,1)S(1)} %collective-permute-done.6.rest_1_.x_beside.refs_1_, bf16[272,512]{1,0:T(8,128)(2,1)S(1)} %collective-permute-done.9.x_beyond.refs_2_, ...), custom_call_target="tpu_custom_call" | custom-call | flops 1000000 | bytes 1 | tf_op jit(solution)/shard_map/pallas_call | solution.py:813
  50.9 0.7 %shard_map.83 = bf16[1024,512]{1,0:T(8,128)(2,1)S(1)} custom-call(bf16[144,512]{1,0:T(8,128)(2,1)S(1)} %collective-permute-done.2._.x_own.refs_0_, bf16[272,512]{1,0:T(8,128)(2,1)S(1)} %collective-permute-done.6.rest_1_.x_beside.refs_1_, bf16[272,512]{1,0:T(8,128)(2,1)S(1)} %collective-permute-done.9.x_beyond.refs_2_, ...), custom_call_target="tpu_custom_call" | custom-call | flops 2000000000 | bytes 4000000 | tf_op jit(solution)/shard_map/pallas_call | solution.py:822
  51.6 0.1 collective-permute-start.13
  51.7 1.5 %shard_map.84._ = bf16[512,2048]{1,0:T(8,128)(2,1)} custom-call(bf16[144,512]{1,0:T(8,128)(2,1)S(1)} %collective-permute-done.2._.x_own.refs_0_, bf16[272,512]{1,0:T(8,128)(2,1)S(1)} %collective-permute-done.6.rest_1_.x_beside.refs_1_, bf16[272,512]{1,0:T(8,128)(2,1)S(1)} %collective-permute-done.9.x_beyond.refs_2_, ...), custom_call_target="tpu_custom_call", output_to_operand_aliasing={{}: (7, {})} | custom-call | flops 2000000000 | bytes 4000000 | tf_op jit(solution)/shard_map/pallas_call | solution.py:832
  53.1 1.2 %collective-permute-done.13.sent_ref = bf16[1024,512]{1,0:T(8,128)(2,1)S(1)} collective-permute-done((bf16[1024,512]{1,0:T(8,128)(2,1)S(1)}, bf16[1024,512]{1,0:T(8,128)(2,1)S(1)}, u32[]{:S(2)}, u32[]{:S(2)}) %collective-permute-start.13) | collective-permute-done | bytes 1048608 | tf_op jit(solution)/shard_map/ppermute | solution.py:661
  54.3 1.0 %shard_map.85 = bf16[512,2048]{1,0:T(8,128)(2,1)} custom-call(bf16[1024,512]{1,0:T(8,128)(2,1)S(1)} %collective-permute-done.13.sent_ref, bf16[512,2048]{1,0:T(8,128)(2,1)} %shard_map.84._), custom_call_target="tpu_custom_call", output_to_operand_aliasing={{}: (1, {})} | custom-call | bytes 1000000 | tf_op jit(solution)/shard_map/pallas_call | solution.py:842
  (16 shorter events, 0.1 us)
Async XLA Ops:
  0.6 27.0 %copy-start.3 = (s32[2]{0:T(128)S(1)}, s32[2]{0:T(128)}, u32[]{:S(2)}) copy-start(s32[2]{0:T(128)} %offsets_ref.9) | copy-start | bytes 28
  0.6 27.0 %copy-start.4 = (bf16[2,128,2048]{2,1,0:T(8,128)(2,1)S(1)}, bf16[2,128,2048]{2,1,0:T(8,128)(2,1)}, u32[]{:S(2)}) copy-start(bf16[2,128,2048]{2,1,0:T(8,128)(2,1)} %q_ref.5) | copy-start | bytes 3145732
  3.3 15.1 %collective-permute-start = (bf16[272,512]{1,0:T(8,128)(2,1)}, bf16[272,512]{1,0:T(8,128)(2,1)S(1)}, u32[]{:S(2)}, u32[]{:S(2)}) collective-permute-start(bf16[272,512]{1,0:T(8,128)(2,1)} %get-tuple-element.16.both.both_ref.rest_0_), channel_id=1, source_target_pairs={{0,8},{4,12},{8,16},{12,20},{16,24},{20,28},{24,0},{28,4},{1,9},{5... | collective-permute-start | bytes 835592 | tf_op jit(solution)/shard_map/ppermute | solution.py:661
  6.4 21.3 %collective-permute-start.7 = (bf16[272,512]{1,0:T(8,128)(2,1)}, bf16[272,512]{1,0:T(8,128)(2,1)S(1)}, u32[]{:S(2)}, u32[]{:S(2)}) collective-permute-start(bf16[272,512]{1,0:T(8,128)(2,1)} %get-tuple-element.16.both.both_ref.rest_0_), channel_id=1, source_target_pairs={{0,4},{4,0},{8,12},{12,8},{16,20},{20,16},{24,28},{28,24},{1,5},{5... | collective-permute-start | bytes 835592 | tf_op jit(solution)/shard_map/ppermute | solution.py:661
  7.9 5.4 %collective-permute-start.2 = (bf16[144,512]{1,0:T(8,128)(2,1)}, bf16[144,512]{1,0:T(8,128)(2,1)S(1)}, u32[]{:S(2)}, u32[]{:S(2)}) collective-permute-start(bf16[144,512]{1,0:T(8,128)(2,1)} %get-tuple-element.17), channel_id=1, source_target_pairs={{0,2},{1,3},{2,0},{3,1},{4,6},{5,7},{6,4},{7,5},{8,10},{9,11},{10,... | collective-permute-start | bytes 442376 | tf_op jit(solution)/shard_map/ppermute | solution.py:661
  9.4 9.0 %collective-permute-start.1 = (bf16[144,512]{1,0:T(8,128)(2,1)}, bf16[144,512]{1,0:T(8,128)(2,1)S(1)}, u32[]{:S(2)}, u32[]{:S(2)}) collective-permute-start(bf16[144,512]{1,0:T(8,128)(2,1)} %get-tuple-element.17), channel_id=1, source_target_pairs={{0,24},{4,28},{8,0},{12,4},{16,8},{20,12},{24,16},{28,20},{1,25},{... | collective-permute-start | bytes 442376 | tf_op jit(solution)/shard_map/ppermute | solution.py:661
  11.6 13.1 %collective-permute-start.3 = (bf16[144,512]{1,0:T(8,128)(2,1)}, bf16[144,512]{1,0:T(8,128)(2,1)S(1)}, u32[]{:S(2)}, u32[]{:S(2)}) collective-permute-start(bf16[144,512]{1,0:T(8,128)(2,1)} %get-tuple-element.17), channel_id=1, source_target_pairs={{0,16},{4,20},{8,24},{12,28},{16,0},{20,4},{24,8},{28,12},{1,17},{... | collective-permute-start | bytes 442376 | tf_op jit(solution)/shard_map/ppermute | solution.py:661
  13.3 35.5 %collective-permute-start.10 = (bf16[144,512]{1,0:T(8,128)(2,1)S(1)}, bf16[144,512]{1,0:T(8,128)(2,1)S(1)}, u32[]{:S(2)}, u32[]{:S(2)}) collective-permute-start(bf16[144,512]{1,0:T(8,128)(2,1)S(1)} %collective-permute-done.2._.x_own.refs_0_), channel_id=1, source_target_pairs={{0,4},{4,0},{8,12},{12,8},{16,20},{20,16},{24,28},{28,24},{1,5},{5... | collective-permute-start | bytes 442376 | tf_op jit(solution)/shard_map/ppermute | solution.py:661
  18.4 1.0 %copy-start = (bf16[272,512]{1,0:T(8,128)(2,1)S(1)}, bf16[272,512]{1,0:T(8,128)(2,1)}, u32[]{:S(2)}) copy-start(bf16[272,512]{1,0:T(8,128)(2,1)} %get-tuple-element.16.both.both_ref.rest_0_) | copy-start | bytes 835588
  19.4 10.7 %collective-permute-start.6 = (bf16[272,512]{1,0:T(8,128)(2,1)S(1)}, bf16[272,512]{1,0:T(8,128)(2,1)S(1)}, u32[]{:S(2)}, u32[]{:S(2)}) collective-permute-start(bf16[272,512]{1,0:T(8,128)(2,1)S(1)} %get-tuple-element.18.rest_1_), channel_id=1, source_target_pairs={{0,2},{1,3},{2,0},{3,1},{4,6},{5,7},{6,4},{7,5},{8,10},{9,11},{10,... | collective-permute-start | bytes 835592 | tf_op jit(solution)/shard_map/ppermute | solution.py:661
  21.0 9.2 %collective-permute-start.5 = (bf16[272,512]{1,0:T(8,128)(2,1)S(1)}, bf16[272,512]{1,0:T(8,128)(2,1)S(1)}, u32[]{:S(2)}, u32[]{:S(2)}) collective-permute-start(bf16[272,512]{1,0:T(8,128)(2,1)S(1)} %get-tuple-element.18.rest_1_), channel_id=1, source_target_pairs={{0,4},{4,0},{8,12},{12,8},{16,20},{20,16},{24,28},{28,24},{1,5},{5... | collective-permute-start | bytes 835592 | tf_op jit(solution)/shard_map/ppermute | solution.py:661
  24.8 5.4 %collective-permute-start.4 = (bf16[128,512]{1,0:T(8,128)(2,1)S(1)}, bf16[128,512]{1,0:T(8,128)(2,1)S(1)}, u32[]{:S(2)}, u32[]{:S(2)}) collective-permute-start(bf16[128,512]{1,0:T(8,128)(2,1)S(1)} %get-tuple-element.19.relay), channel_id=1, source_target_pairs={{0,8},{4,12},{24,16},{28,20},{1,9},{5,13},{25,17},{29,21},{2,10},{... | collective-permute-start | bytes 393224 | tf_op jit(solution)/shard_map/ppermute | solution.py:661
  27.7 1.0 %copy-start.1 = (bf16[272,512]{1,0:T(8,128)(2,1)S(1)}, bf16[272,512]{1,0:T(8,128)(2,1)}, u32[]{:S(2)}) copy-start(bf16[272,512]{1,0:T(8,128)(2,1)} %get-tuple-element.16.both.both_ref.rest_0_) | copy-start | bytes 835588
  28.6 4.2 %copy-start.2 = (bf16[272,512]{1,0:T(8,128)(2,1)S(1)}, bf16[272,512]{1,0:T(8,128)(2,1)}, u32[]{:S(2)}) copy-start(bf16[272,512]{1,0:T(8,128)(2,1)} %get-tuple-element.16.both.both_ref.rest_0_) | copy-start | bytes 835588
  30.2 9.7 %collective-permute-start.8 = (bf16[272,512]{1,0:T(8,128)(2,1)S(1)}, bf16[272,512]{1,0:T(8,128)(2,1)S(1)}, u32[]{:S(2)}, u32[]{:S(2)}) collective-permute-start(bf16[272,512]{1,0:T(8,128)(2,1)S(1)} %shard_map.79.rest_1_.rest_2_), channel_id=1, source_target_pairs={{0,4},{4,0},{8,12},{12,8},{16,20},{20,16},{24,28},{28,24},{1,5},{5... | collective-permute-start | bytes 835592 | tf_op jit(solution)/shard_map/ppermute | solution.py:661
  30.9 17.9 %collective-permute-start.9 = (bf16[272,512]{1,0:T(8,128)(2,1)S(1)}, bf16[272,512]{1,0:T(8,128)(2,1)S(1)}, u32[]{:S(2)}, u32[]{:S(2)}) collective-permute-start(bf16[272,512]{1,0:T(8,128)(2,1)S(1)} %shard_map.79.rest_1_.rest_2_), channel_id=1, source_target_pairs={{0,2},{1,3},{2,0},{3,1},{4,6},{5,7},{6,4},{7,5},{8,10},{9,11},{10,... | collective-permute-start | bytes 835592 | tf_op jit(solution)/shard_map/ppermute | solution.py:661
  32.4 16.4 %collective-permute-start.11 = (bf16[272,512]{1,0:T(8,128)(2,1)S(1)}, bf16[272,512]{1,0:T(8,128)(2,1)S(1)}, u32[]{:S(2)}, u32[]{:S(2)}) collective-permute-start(bf16[272,512]{1,0:T(8,128)(2,1)S(1)} %collective-permute-done.6.rest_1_.x_beside.refs_1_), channel_id=1, source_target_pairs={{0,4},{4,0},{8,12},{12,8},{16,20},{20,16},{24,28},{28,24},{1,5},{5... | collective-permute-start | bytes 835592 | tf_op jit(solution)/shard_map/ppermute | solution.py:661
  39.8 9.0 %collective-permute-start.12 = (bf16[272,512]{1,0:T(8,128)(2,1)S(1)}, bf16[272,512]{1,0:T(8,128)(2,1)S(1)}, u32[]{:S(2)}, u32[]{:S(2)}) collective-permute-start(bf16[272,512]{1,0:T(8,128)(2,1)S(1)} %collective-permute-done.8.rest_5_), channel_id=1, source_target_pairs={{0,2},{1,3},{2,0},{3,1},{4,6},{5,7},{6,4},{7,5},{8,10},{9,11},{10,... | collective-permute-start | bytes 835592 | tf_op jit(solution)/shard_map/ppermute | solution.py:661
  51.6 2.7 %collective-permute-start.13 = (bf16[1024,512]{1,0:T(8,128)(2,1)S(1)}, bf16[1024,512]{1,0:T(8,128)(2,1)S(1)}, u32[]{:S(2)}, u32[]{:S(2)}) collective-permute-start(bf16[1024,512]{1,0:T(8,128)(2,1)S(1)} %shard_map.83), channel_id=1, source_target_pairs={{0,1},{1,0},{2,3},{3,2},{4,5},{5,4},{6,7},{7,6},{8,9},{9,8},{10,11... | collective-permute-start | bytes 3145736 | tf_op jit(solution)/shard_map/ppermute | solution.py:661

commit v2 on v1

--- a/solution.py
+++ b/solution.py
@@ -346,6 +346,15 @@
     ).astype(jnp.bfloat16)
 
 
+def going_kernel(both, y_own, x_own, d_own, going_ref, notes_ref):
+    span = both.shape[0] // 2 - NOTES // 2
+    going_ref[:span, :] = both[:span, :]
+    going_ref[span : 2 * span, :] = y_own[:span, :]
+    going_ref[2 * span :, :] = jnp.zeros((going_ref.shape[0] - 2 * span, going_ref.shape[1]), going_ref.dtype)
+    notes_ref[:NOTES, :] = two_notes(both, 2 * span, y_own, 2 * span)
+    notes_ref[NOTES:, :] = two_notes(x_own, span, d_own, span)
+
+
 def beside_kernel(below, above, both, _, beside_ref, relay_ref):
     span = relay_ref.shape[0]
     beside_ref[:span, :] = below[:span, :]
@@ -362,17 +371,17 @@
         relay_ref[...] = both[span : 2 * span, :]
 
 
-def beyond_kernel(far_level, relay, relayed, *rest):
-    out_ref = rest[-1]
-    span = relay.shape[0]
+def pick_late_kernel(relay, relayed, _, out_ref):
     level = lax.axis_index("ctx") // 2
-    out_ref[:span, :] = far_level[:span, :]
-    out_ref[2 * span :, :] = far_level[span:, :]
     for ref, chosen in ((relay, (level == 0) | (level == 3)), (relayed, (level == 1) | (level == 2))):
 
         @pl.when(chosen)
         def _(ref=ref):
-            out_ref[span : 2 * span, :] = ref[...]
+            out_ref[...] = ref[...]
+
+
+def end_kernel(beyond, _, out_ref):
+    out_ref[...] = beyond[: out_ref.shape[0], :]
 
 
 def place_of(turn, flip, shards):
@@ -527,13 +536,10 @@
     return jnp.sum(jnp.transpose(mass), axis=0, keepdims=True)
 
 
-def late_kernel(head, offsets_ref, q_ref, both_ref, beside_ref, *rest):
-    out_ref, score_ref = rest[-2:]
+def late_kernel(offsets_ref, q_ref, both_ref, beside_ref, out_ref, score_ref):
     mine, shards = lax.axis_index("ctx"), lax.axis_size("ctx")
     span = q_ref.shape[1]
-    cache = score_ref.shape[1] - span
-    heads = both_ref.shape[1] // WIDTH
-    lanes = slice(head * WIDTH, (head + 1) * WIDTH)
+    heads, cache = score_ref.shape[0], score_ref.shape[1] - span
 
     @pl.when(mine >= shards - 2)
     def _():
@@ -541,12 +547,16 @@
         state = jnp.where(keep >= cache, keep - cache + 1, 0)
         state = jnp.where(mine == shards - 1, state, 0).astype(jnp.float32)
         state = jnp.concatenate([state, jnp.zeros((8 - heads, cache), jnp.float32)], axis=0)
-        column = jnp.transpose(state).astype(jnp.int32)[:, head : head + 1]
-        cached = picked(column, 1, beside_ref[span : 2 * span, lanes])
-        rows = jnp.concatenate(
-            [cached.astype(jnp.bfloat16), both_ref[span : 2 * span, lanes]], axis=0
-        )
-        score_ref[...] = attend_columns(q_ref, 0, rows, column, out_ref)
+        columns = jnp.transpose(state).astype(jnp.int32)
+        for head in range(heads):
+            lanes = slice(head * WIDTH, (head + 1) * WIDTH)
+            column = columns[:, head : head + 1]
+            cached = picked(column, 1, beside_ref[span : 2 * span, lanes])
+            rows = jnp.concatenate(
+                [cached.astype(jnp.bfloat16), both_ref[span : 2 * span, lanes]], axis=0
+            )
+            mass = attend_columns(q_ref, head * GROUP * HEAD, rows, column, out_ref)
+            score_ref[head : head + 1, :] = mass
 
     @pl.when(mine < shards - 2)
     def _():
@@ -570,29 +580,40 @@
     return own
 
 
+def index_kernel_in_planes(offsets_ref, *refs):
+    both, beside, y_own, y_beside, x_own, x_beside, d_own, d_beside, far_notes = refs[:9]
+    own_ref, near_slots, far_slots = refs[9:12]
+    near_tables, far_tables = refs[12:15], refs[15:]
+    span = x_own.shape[0] - NOTES
+    at = 2 * span
+    notes = [(both, at, 0, 0, 0), (beside, at, 0, 1, 0), (beside, at, 1, 3, 0)]
+    notes += [(far_notes, 0, 0, 2, 0), (far_notes, 0, 1, 2, 1), (y_own, at, 0, 0, 1)]
+    notes += [(y_beside, at, 0, 1, 1), (y_beside, at, 1, 3, 1)]
+    own = fill_slots(offsets_ref, notes, *near_tables, near_slots)
+    own_ref[...] = jnp.transpose(own.astype(jnp.float32)).astype(jnp.int32)
+    notes = [(x_own, span, 0, 0, 0), (d_own, span, 0, 0, 1), (x_beside, at, 0, 1, 0)]
+    notes += [(x_beside, at, 1, 3, 0), (d_beside, at, 0, 1, 1), (d_beside, at, 1, 3, 1)]
+    notes += [(far_notes, NOTES, 0, 2, 0), (far_notes, NOTES, 1, 2, 1)]
+    fill_slots(offsets_ref, notes, *far_tables, far_slots)
+
+
 def early_kernel(offsets_ref, q_ref, *rest):
-    both, beside, beyond, y_own, y_beside, y_beyond = rest[:6]
-    late_scores = rest[6:8]
-    out_ref, score_ref, done_ref, cache_ref, sent_ref, *rest = rest[9:]
-    tokens, late_tokens, kept, slots, keeps, dests, coded, sem = rest
+    both, beside, beyond, y_own, y_beside, late, y_late, own, slots, late_scores = rest[:10]
+    out_ref, score_ref, done_ref, cache_ref, sent_ref, *rest = rest[11:]
+    tokens, late_tokens, kept, sem = rest
     done_ref[...] = jnp.zeros(done_ref.shape, jnp.float32)
     span = q_ref.shape[1]
     early = early_of(offsets_ref)
-    at = 2 * span
-    notes = [(both, at, 0, 0, 0), (beside, at, 0, 1, 0), (beside, at, 1, 3, 0)]
-    notes += [(beyond, at, 0, 2, 0), (y_own, at, 0, 0, 1), (y_beside, at, 0, 1, 1)]
-    notes += [(y_beside, at, 1, 3, 1), (y_beyond, at, 0, 2, 1)]
-    own = fill_slots(offsets_ref, notes, keeps, dests, coded, slots)
-    own = jnp.transpose(own.astype(jnp.float32)).astype(jnp.int32)
     pieces = [(both, 0, 0, 0), (beside, 0, 1, 0), (beside, span, 3, 0), (beyond, 0, 2, 0)]
-    pieces += [(y_own, 0, 0, 1), (y_beside, 0, 1, 1), (y_beside, span, 3, 1), (y_beyond, 0, 2, 1)]
+    pieces += [(beyond, span, 2, 1), (y_own, 0, 0, 1), (y_beside, 0, 1, 1), (y_beside, span, 3, 1)]
     sort_tokens(pieces, tokens, span)
-    sort_late([(beyond, span), (y_beyond, span)], late_tokens)
+    sort_late([(late, 0), (y_late, 0)], late_tokens)
     place_bands(slots.at[0], tokens, late_tokens, kept)
     column = lax.axis_index("kv")
     copy = pltpu.make_async_copy(kept, output_part(cache_ref, 0, kept.shape[0], column), sem)
     copy.start()
     place_bands(slots.at[1], tokens, late_tokens, sent_ref)
+    score_ref[1 - early] = late_scores[...]
     for head in range(score_ref.shape[1]):
         lanes = slice(head * WIDTH, (head + 1) * WIDTH)
         chosen = own[:, head : head + 1]
@@ -600,40 +621,29 @@
         rows = jnp.concatenate([cached, both[:span, lanes]], axis=0)
         mass = attend_columns(q_ref, head * GROUP * HEAD, rows, chosen, out_ref)
         score_ref[early, head : head + 1, :] = mass
-        score_ref[1 - early, head : head + 1, :] = late_scores[head][...]
     copy.wait()
 
 
-def far_index_kernel(offsets_ref, x_own, x_beside, x_beyond, d_own, d_beside, d_beyond, _, *rest):
-    slots_ref, keeps, dests, coded = rest
-    span = x_own.shape[0] - NOTES
-    at = 2 * span
-    notes = [(x_own, span, 0, 0, 0), (d_own, span, 0, 0, 1), (x_beside, at, 0, 1, 0)]
-    notes += [(x_beside, at, 1, 3, 0), (d_beside, at, 0, 1, 1), (d_beside, at, 1, 3, 1)]
-    notes += [(x_beyond, at, 0, 2, 0), (d_beyond, at, 0, 2, 1)]
-    fill_slots(offsets_ref, notes, keeps, dests, coded, slots_ref)
-
-
 def far_rows(flip, refs, far_ref, tokens, late_tokens):
-    x_own, x_beside, x_beyond, d_own, d_beside, d_beyond, slots = refs
-    span = x_own.shape[0] - NOTES
-    pieces = [(x_own, 0, 0, 0), (x_beside, 0, 1, 0), (x_beside, span, 3, 0), (x_beyond, 0, 2, 0)]
-    pieces += [(d_own, 0, 0, 1), (d_beside, 0, 1, 1), (d_beside, span, 3, 1), (d_beyond, 0, 2, 1)]
+    x_own, x_beside, x_end, d_own, d_beside, x_late, d_late, slots = refs
+    span = x_late.shape[0]
+    pieces = [(x_own, 0, 0, 0), (x_beside, 0, 1, 0), (x_beside, span, 3, 0), (x_end, 0, 2, 0)]
+    pieces += [(x_end, span, 2, 1), (d_own, 0, 0, 1), (d_beside, 0, 1, 1), (d_beside, span, 3, 1)]
     sort_tokens(pieces, tokens, span)
-    sort_late([(x_beyond, span), (d_beyond, span)], late_tokens)
+    sort_late([(x_late, 0), (d_late, 0)], late_tokens)
     place_bands(slots.at[flip], tokens, late_tokens, far_ref)
 
 
 def far_sent_kernel(*refs):
-    near_ref, sent_ref, tokens, late_tokens = refs[7:]
+    near_ref, sent_ref, tokens, late_tokens = refs[8:]
     rows = near_ref.shape[0]
     sent_ref[rows:, :] = near_ref[...]
-    far_rows(1, refs[:7], sent_ref.at[:rows], tokens, late_tokens)
+    far_rows(1, refs[:8], sent_ref.at[:rows], tokens, late_tokens)
 
 
 def far_kept_kernel(*refs):
-    cache_ref, far, tokens, late_tokens, sem = refs[8:]
-    far_rows(0, refs[:7], far, tokens, late_tokens)
+    cache_ref, far, tokens, late_tokens, sem = refs[9:]
+    far_rows(0, refs[:8], far, tokens, late_tokens)
     column = lax.axis_index("kv")
     copy = pltpu.make_async_copy(far, output_part(cache_ref, 0, far.shape[0], column ^ 2), sem)
     copy.start()
@@ -711,9 +721,17 @@
         cost_estimate=cost(10**9, 1),
     )(offsets, kv_rows, keep, jnp.transpose(dest))
 
-    below, above, far_level = along_z(both, 1), along_z(single, 3), along_z(single, 2)
-    y_own, x_own = across_y(both), across_x(single)
-    d_own = across_y(x_own)
+    below, above = along_z(both, 1), along_z(single, 3)
+    y_own, x_own, d_own = across_y(both), across_x(single), across_both(single)
+    going, going_notes = pl.pallas_call(
+        going_kernel,
+        out_shape=(piece(2 * span + 2 * NOTES), piece(2 * NOTES)),
+        in_specs=[vmem] * 4,
+        out_specs=(vmem, vmem),
+        compiler_params=params,
+        cost_estimate=cost(0, 10**6),
+    )(both, y_own, x_own, d_own)
+    beyond, far_notes = along_z(going, 2), along_z(going_notes, 2)
     beside, relay = pl.pallas_call(
         beside_kernel,
         out_shape=(piece(2 * span + NOTES), piece(span)),
@@ -721,70 +739,83 @@
         out_specs=(vmem,) * 2,
         compiler_params=params,
         cost_estimate=cost(0, 10**6),
-    )(below, above, both, x_own)
+    )(below, above, both, going)
     relayed = send(relay, "ctx", [(0, 2), (1, 3), (6, 4), (7, 5)])
     y_beside, x_beside = across_y(beside), across_x(beside)
-    d_beside = across_y(x_beside)
+    d_beside = across_both(beside)
 
     attention_shape = jax.ShapeDtypeStruct((prompts, span, qwidth), jnp.bfloat16)
-    half = qwidth // heads
-
-    def late_attention(head, *after):
+
+    def prompt_spec(late):
         def block(_, offsets_ref):
-            return (1 - early_of(offsets_ref), 0, head)
-
-        spec = pl.BlockSpec((1, span, half), block)
-        return pl.pallas_call(
-            functools.partial(late_kernel, head),
-            grid_spec=pltpu.PrefetchScalarGridSpec(
-                num_scalar_prefetch=1,
-                grid=(1,),
-                in_specs=[spec, vmem, vmem] + [anywhere] * len(after),
-                out_specs=(spec, vmem),
-            ),
-            out_shape=(attention_shape, jax.ShapeDtypeStruct((1, cache + span), jnp.float32)),
-            input_output_aliases={4: 0} if head else {},
-            compiler_params=params,
-            cost_estimate=cost(5 * 10**9, 10**7),
-        )(offsets, query, both, y_own, *after)
-
-    attention, late_first = late_attention(0, far_level)
-    beyond = pl.pallas_call(
-        beyond_kernel,
-        out_shape=piece(2 * span + NOTES),
-        in_specs=[vmem] * 3 + [anywhere] * 3,
+            early = early_of(offsets_ref)
+            return (1 - early if late else early, 0, 0)
+
+        return pl.BlockSpec((1, span, qwidth), block)
+
+    attention, late_scores = pl.pallas_call(
+        late_kernel,
+        grid_spec=pltpu.PrefetchScalarGridSpec(
+            num_scalar_prefetch=1,
+            grid=(1,),
+            in_specs=[prompt_spec(True), vmem, vmem],
+            out_specs=(prompt_spec(True), vmem),
+        ),
+        out_shape=(attention_shape, jax.ShapeDtypeStruct((heads, cache + span), jnp.float32)),
+        compiler_params=params,
+        cost_estimate=cost(10**6, 1),
+    )(offsets, query, both, y_own)
+    late = pl.pallas_call(
+        pick_late_kernel,
+        out_shape=piece(span),
+        in_specs=[vmem] * 2 + [anywhere],
         out_specs=vmem,
         compiler_params=params,
-        cost_estimate=cost(0, 10**6),
-    )(far_level, relay, relayed, y_beside, x_beside, late_first)
-    y_beyond, x_beyond = across_y(beyond), across_x(beyond)
-    attention, late_second = late_attention(1, attention, beyond)
-    d_beyond = across_x(y_beyond)
-
-    tokens = pltpu.VMEM((shards * span, width), jnp.bfloat16)
-    late_tokens = pltpu.VMEM((2 * span, width), jnp.bfloat16)
-    block_rows = pltpu.VMEM((rows, width), jnp.bfloat16)
-    cache_shape = jax.ShapeDtypeStruct((rows, columns * width), jnp.bfloat16)
+        cost_estimate=cost(0, 10**5),
+    )(relay, relayed, late_scores)
+    y_late, x_late, d_late = across_y(late), across_x(late), across_both(late)
+
     slots_shape = jax.ShapeDtypeStruct((2, rows, heads), jnp.int32)
     tables = [
         pltpu.VMEM((shards, 4 * heads, cache), jnp.int32),
         pltpu.VMEM((shards, prompts, cache), jnp.int32),
         pltpu.VMEM((shards, 8 * heads, cache), jnp.bfloat16),
     ]
-    early_spec = pl.BlockSpec(
-        (1, span, qwidth), lambda _, offsets_ref: (early_of(offsets_ref), 0, 0)
-    )
+    own_slots, near_slots, far_slots = pl.pallas_call(
+        index_kernel_in_planes,
+        out_shape=(
+            jax.ShapeDtypeStruct((cache, 4 * heads), jnp.int32),
+            slots_shape,
+            slots_shape,
+        ),
+        in_specs=[smem] + [vmem] * 9,
+        out_specs=(vmem,) * 3,
+        scratch_shapes=2 * tables,
+        compiler_params=params,
+        cost_estimate=cost(10**6, 1),
+    )(offsets, both, beside, y_own, y_beside, x_own, x_beside, d_own, d_beside, far_notes)
+    end = pl.pallas_call(
+        end_kernel,
+        out_shape=piece(2 * span),
+        in_specs=[vmem, anywhere],
+        out_specs=vmem,
+        compiler_params=params,
+        cost_estimate=cost(0, 10**5),
+    )(beyond, near_slots)
+    x_end = across_x(end)
+
+    tokens = pltpu.VMEM((shards * span, width), jnp.bfloat16)
+    late_tokens = pltpu.VMEM((2 * span, width), jnp.bfloat16)
+    block_rows = pltpu.VMEM((rows, width), jnp.bfloat16)
+    cache_shape = jax.ShapeDtypeStruct((rows, columns * width), jnp.bfloat16)
     attention, row_scores, early_done, owner_cache, near_sent = pl.pallas_call(
         early_kernel,
         grid_spec=pltpu.PrefetchScalarGridSpec(
             num_scalar_prefetch=1,
             grid=(1,),
-            in_specs=[early_spec] + [vmem] * 8 + [anywhere],
-            out_specs=(early_spec, vmem, vmem, hbm, vmem),
-            scratch_shapes=[tokens, late_tokens, block_rows]
-            + [pltpu.VMEM(slots_shape.shape, jnp.int32)]
-            + tables
-            + [pltpu.SemaphoreType.DMA],
+            in_specs=[prompt_spec(False)] + [vmem] * 10 + [anywhere],
+            out_specs=(prompt_spec(False), vmem, vmem, hbm, vmem),
+            scratch_shapes=[tokens, late_tokens, block_rows, pltpu.SemaphoreType.DMA],
         ),
         out_shape=(
             attention_shape,
@@ -793,7 +824,7 @@
             cache_shape,
             piece(rows),
         ),
-        input_output_aliases={10: 0},
+        input_output_aliases={12: 0},
         compiler_params=params,
         cost_estimate=cost(10**10, 10**7),
     )(
@@ -801,44 +832,37 @@
         query,
         both,
         beside,
-        beyond,
+        end,
         y_own,
         y_beside,
-        y_beyond,
-        late_first,
-        late_second,
+        late,
+        y_late,
+        own_slots,
+        near_slots,
+        late_scores,
         attention,
     )
-    far = (x_own, x_beside, x_beyond, d_own, d_beside, d_beyond)
-    far_slots = pl.pallas_call(
-        far_index_kernel,
-        out_shape=slots_shape,
-        in_specs=[smem] + [vmem] * 6 + [anywhere],
-        out_specs=vmem,
-        scratch_shapes=tables,
-        compiler_params=params,
-        cost_estimate=cost(10**6, 1),
-    )(offsets, *far, early_done)
+    far = (x_own, x_beside, x_end, d_own, d_beside, x_late, d_late, far_slots)
     sent = pl.pallas_call(
         far_sent_kernel,
         out_shape=piece(2 * rows),
-        in_specs=[vmem] * 8,
+        in_specs=[vmem] * 9,
         out_specs=vmem,
         scratch_shapes=[tokens, late_tokens],
         compiler_params=params,
         cost_estimate=cost(2 * 10**9, 4 * 10**6),
-    )(*far, far_slots, near_sent)
+    )(*far, near_sent)
     received = across_core(sent)
     owner_cache = pl.pallas_call(
         far_kept_kernel,
         out_shape=cache_shape,
-        in_specs=[vmem] * 7 + [hbm],
+        in_specs=[vmem] * 8 + [hbm],
         out_specs=hbm,
         scratch_shapes=[block_rows, tokens, late_tokens, pltpu.SemaphoreType.DMA],
-        input_output_aliases={7: 0},
+        input_output_aliases={8: 0},
         compiler_params=params,
         cost_estimate=cost(2 * 10**9, 4 * 10**6),
-    )(*far, far_slots, owner_cache)
+    )(*far, owner_cache)
     owner_cache = pl.pallas_call(
         last_kernel,
         out_shape=cache_shape,

time: 56.1 us -> 58.7 us (1.046)
  starting transfers between devices: 18.9 us -> 27.1 us
  waiting for transfers between devices: 14.7 us -> 10.7 us
  Pallas kernels: 19 us -> 17.8 us
    ppermute x14 -> x16, starting transfers between devices: 18.9 us -> 27.1 us  [send(): return lax.ppermute(value, axis, pairs)]
    ppermute x14 -> x16, waiting for transfers between devices: 14.7 us -> 10.7 us  [send(): return lax.ppermute(value, axis, pairs)]
    pallas_call x1, Pallas kernels: 8.33 us -> 6.96 us  [local_in_planes(): pl.pallas_call(early_kernel, grid_spec=pltpu.PrefetchScalarGridSpec(num_s...]
    pallas_call x4 -> x5, Pallas kernels: 4.83 us -> 5 us  [the longest x1 3.38 us: local_in_planes(): pl.pallas_call(index_kernel_in_planes, out_shape=(jax.ShapeDtypeStruct((c...]
  transfers between devices with their start and end apart: 14 -> 16, of which waited for: 6 -> 7; matrix products, arithmetic and copies ran while one was open for 0% -> 0% of each run, Pallas kernels for 23% -> 23%
where the time goes in v2:
time: 58.7 us; the launch traced here: 58.5 us
  starting transfers between devices  27.1 us (46%)
  Pallas kernels  17.8 us (30%)
  waiting for transfers between devices  10.7 us (18%)
  local copies, waits for them, and re-layouts  1.93 us (3%)
  between operations  0.94 us (2%)
    ppermute x16, starting transfers between devices, send(): return lax.ppermute(value, axis, pairs)  27.1 us
    ppermute x16, waiting for transfers between devices, send(): return lax.ppermute(value, axis, pairs)  10.7 us
    pallas_call x1, Pallas kernels, local_in_planes(): pl.pallas_call(early_kernel, grid_spec=pltpu.PrefetchScalarGridSpec(num_s...  6.96 us
    pallas_call x1, Pallas kernels, local_in_planes(): pl.pallas_call(index_kernel_in_planes, out_shape=(jax.ShapeDtypeStruct((c...  3.38 us
    pallas_call x1, Pallas kernels, local_in_planes(): pl.pallas_call(prepare_kernel, out_shape=(piece(2 * span + NOTES), piece(...  2.65 us
    unnamed x10, local copies, waits for them, and re-layouts  1.93 us
    pallas_call x1, Pallas kernels, local_in_planes(): pl.pallas_call(far_kept_kernel, out_shape=cache_shape, in_specs=[vmem] *...  1.46 us
    pallas_call x1, Pallas kernels, local_in_planes(): pl.pallas_call(late_kernel, grid_spec=pltpu.PrefetchScalarGridSpec(num_sc...  1.39 us
  transfers between devices with their start and end apart: 16, of which 7 were waited for; matrix products, arithmetic and copies ran while one was open for 0% of the time, Pallas kernels for 23%

profile of v2, /device:TPU:0, one launch (start us, length us, event | category | flops | bytes accessed | tf_op | source)
XLA Modules:
  0.0 58.5 jit_solution(4679066524524094036)
XLA Ops:
  0.7 2.7 %shard_map.76 = (bf16[272,512]{1,0:T(8,128)(2,1)}, bf16[144,512]{1,0:T(8,128)(2,1)}) custom-call(s32[2]{0:T(128)} %offsets_ref.7, bf16[2,128,512]{2,1,0:T(8,128)(2,1)} %kv_ref.1, s32[2,1,2,512]{3,2,1,0:T(2,128)} %keep_ref.1, s32[1,1024]{1,0:T(1,128)} %bitcast.1), custom_call_target="tpu_custom_call" | custom-call | flops 1000000000 | bytes 1 | tf_op jit(solution)/shard_map/pallas_call | solution.py:710
  3.3 3.0 %collective-permute-start.2 = (bf16[272,512]{1,0:T(8,128)(2,1)}, bf16[272,512]{1,0:T(8,128)(2,1)S(1)}, u32[]{:S(2)}, u32[]{:S(2)}) collective-permute-start(bf16[272,512]{1,0:T(8,128)(2,1)} %get-tuple-element.18.both.refs_0_.both_ref.rest_0_), channel_id=1, source_target_pairs={{0,4},{4,0},{8,12},{12,8},{16,20},{20,16},{24,28},{28,24},{1,5},{5... | collective-permute-start | bytes 835592 | tf_op jit(solution)/shard_map/ppermute | solution.py:671
  6.3 1.6 %collective-permute-start = (bf16[272,512]{1,0:T(8,128)(2,1)}, bf16[272,512]{1,0:T(8,128)(2,1)S(1)}, u32[]{:S(2)}, u32[]{:S(2)}) collective-permute-start(bf16[272,512]{1,0:T(8,128)(2,1)} %get-tuple-element.18.both.refs_0_.both_ref.rest_0_), channel_id=1, source_target_pairs={{0,8},{4,12},{8,16},{12,20},{16,24},{20,28},{24,0},{28,4},{1,9},{5... | collective-permute-start | bytes 835592 | tf_op jit(solution)/shard_map/ppermute | solution.py:671
  7.9 1.5 %collective-permute-start.3 = (bf16[144,512]{1,0:T(8,128)(2,1)}, bf16[144,512]{1,0:T(8,128)(2,1)S(1)}, u32[]{:S(2)}, u32[]{:S(2)}) collective-permute-start(bf16[144,512]{1,0:T(8,128)(2,1)} %get-tuple-element.19), channel_id=1, source_target_pairs={{0,2},{1,3},{2,0},{3,1},{4,6},{5,7},{6,4},{7,5},{8,10},{9,11},{10,... | collective-permute-start | bytes 442376 | tf_op jit(solution)/shard_map/ppermute | solution.py:671
  9.4 0.5 collective-permute-start.4
  9.9 2.0 %collective-permute-start.1 = (bf16[144,512]{1,0:T(8,128)(2,1)}, bf16[144,512]{1,0:T(8,128)(2,1)S(1)}, u32[]{:S(2)}, u32[]{:S(2)}) collective-permute-start(bf16[144,512]{1,0:T(8,128)(2,1)} %get-tuple-element.19), channel_id=1, source_target_pairs={{0,24},{4,28},{8,0},{12,4},{16,8},{20,12},{24,16},{28,20},{1,25},{... | collective-permute-start | bytes 442376 | tf_op jit(solution)/shard_map/ppermute | solution.py:671
  11.9 2.8 %collective-permute-done.3.x_own.refs_4_.refs_0_ = bf16[144,512]{1,0:T(8,128)(2,1)S(1)} collective-permute-done((bf16[144,512]{1,0:T(8,128)(2,1)}, bf16[144,512]{1,0:T(8,128)(2,1)S(1)}, u32[]{:S(2)}, u32[]{:S(2)}) %collective-permute-start.3) | collective-permute-done | bytes 147488 | tf_op jit(solution)/shard_map/ppermute | solution.py:671
  14.7 1.6 %collective-permute-done.4.d_own.refs_6_.refs_3_ = bf16[144,512]{1,0:T(8,128)(2,1)S(1)} collective-permute-done((bf16[144,512]{1,0:T(8,128)(2,1)}, bf16[144,512]{1,0:T(8,128)(2,1)S(1)}, u32[]{:S(2)}, u32[]{:S(2)}) %collective-permute-start.4) | collective-permute-done | bytes 147488 | tf_op jit(solution)/shard_map/ppermute | solution.py:671
  16.4 1.0 %copy-done = bf16[272,512]{1,0:T(8,128)(2,1)S(1)} copy-done((bf16[272,512]{1,0:T(8,128)(2,1)S(1)}, bf16[272,512]{1,0:T(8,128)(2,1)}, u32[]{:S(2)}) %copy-start) | copy-done | bytes 278552
  17.4 2.9 %collective-permute-start.5 = (bf16[288,512]{1,0:T(8,128)(2,1)S(1)}, bf16[288,512]{1,0:T(8,128)(2,1)S(1)}, u32[]{:S(2)}, u32[]{:S(2)}) collective-permute-start(bf16[288,512]{1,0:T(8,128)(2,1)S(1)} %get-tuple-element.20._), channel_id=1, source_target_pairs={{0,16},{4,20},{8,24},{12,28},{16,0},{20,4},{24,8},{28,12},{1,17},{... | collective-permute-start | bytes 884744 | tf_op jit(solution)/shard_map/ppermute | solution.py:671
  20.3 3.5 %collective-permute-start.10 = (bf16[128,512]{1,0:T(8,128)(2,1)S(1)}, bf16[128,512]{1,0:T(8,128)(2,1)S(1)}, u32[]{:S(2)}, u32[]{:S(2)}) collective-permute-start(bf16[128,512]{1,0:T(8,128)(2,1)S(1)} %get-tuple-element.24.relay), channel_id=1, source_target_pairs={{0,8},{4,12},{24,16},{28,20},{1,9},{5,13},{25,17},{29,21},{2,10},{... | collective-permute-start | bytes 393224 | tf_op jit(solution)/shard_map/ppermute | solution.py:671
  23.8 1.6 %collective-permute-start.7 = (bf16[272,512]{1,0:T(8,128)(2,1)S(1)}, bf16[272,512]{1,0:T(8,128)(2,1)S(1)}, u32[]{:S(2)}, u32[]{:S(2)}) collective-permute-start(bf16[272,512]{1,0:T(8,128)(2,1)S(1)} %get-tuple-element.21.refs_1_.rest_1_), channel_id=1, source_target_pairs={{0,2},{1,3},{2,0},{3,1},{4,6},{5,7},{6,4},{7,5},{8,10},{9,11},{10,... | collective-permute-start | bytes 835592 | tf_op jit(solution)/shard_map/ppermute | solution.py:671
  25.3 1.5 %collective-permute-start.8 = (bf16[272,512]{1,0:T(8,128)(2,1)S(1)}, bf16[272,512]{1,0:T(8,128)(2,1)S(1)}, u32[]{:S(2)}, u32[]{:S(2)}) collective-permute-start(bf16[272,512]{1,0:T(8,128)(2,1)S(1)} %get-tuple-element.21.refs_1_.rest_1_), channel_id=1, source_target_pairs={{0,6},{1,7},{2,4},{3,5},{4,2},{5,3},{6,0},{7,1},{8,14},{9,15},{10,... | collective-permute-start | bytes 835592 | tf_op jit(solution)/shard_map/ppermute | solution.py:671
  26.8 0.5 collective-permute-start.6
  27.3 0.9 %collective-permute-done.10.relayed = bf16[128,512]{1,0:T(8,128)(2,1)S(1)} collective-permute-done((bf16[128,512]{1,0:T(8,128)(2,1)S(1)}, bf16[128,512]{1,0:T(8,128)(2,1)S(1)}, u32[]{:S(2)}, u32[]{:S(2)}) %collective-permute-start.10) | collective-permute-done | bytes 131104 | tf_op jit(solution)/shard_map/ppermute | solution.py:671
  28.2 2.6 %collective-permute-start.9 = (bf16[32,512]{1,0:T(8,128)(2,1)S(1)}, bf16[32,512]{1,0:T(8,128)(2,1)S(1)}, u32[]{:S(2)}, u32[]{:S(2)}) collective-permute-start(bf16[32,512]{1,0:T(8,128)(2,1)S(1)} %get-tuple-element.22), channel_id=1, source_target_pairs={{0,16},{4,20},{8,24},{12,28},{16,0},{20,4},{24,8},{28,12},{1,17},{... | collective-permute-start | bytes 98312 | tf_op jit(solution)/shard_map/ppermute | solution.py:671
  30.8 1.0 %copy-done.1 = bf16[272,512]{1,0:T(8,128)(2,1)S(1)} copy-done((bf16[272,512]{1,0:T(8,128)(2,1)S(1)}, bf16[272,512]{1,0:T(8,128)(2,1)}, u32[]{:S(2)}) %copy-start.1) | copy-done | bytes 278552
  31.8 1.4 %shard_map.81 = (bf16[2,128,2048]{2,1,0:T(8,128)(2,1)}, f32[2,640]{1,0:T(2,128)S(1)}) custom-call(s32[2]{0:T(128)S(1)} %copy-done.4, bf16[2,128,2048]{2,1,0:T(8,128)(2,1)S(1)} %copy-done.3, bf16[272,512]{1,0:T(8,128)(2,1)S(1)} %copy-done.1, bf16[272,512]{1,0:T(8,128)(2,1)S(1)} %collective-permute-done.2.y_own.refs_2_.beside_ref.rest_3_), custom_call_target="tpu_custom_call" | custom-call | flops 1000000 | bytes 1 | tf_op jit(solution)/shard_map/pallas_call | solution.py:756
  33.1 0.2 shard_map.82.rest_5_
  33.3 0.2 collective-permute-done.9.refs_8_
  33.5 1.4 %collective-permute-start.11 = (bf16[128,512]{1,0:T(8,128)(2,1)S(1)}, bf16[128,512]{1,0:T(8,128)(2,1)S(1)}, u32[]{:S(2)}, u32[]{:S(2)}) collective-permute-start(bf16[128,512]{1,0:T(8,128)(2,1)S(1)} %shard_map.82.rest_5_), channel_id=1, source_target_pairs={{0,4},{4,0},{8,12},{12,8},{16,20},{20,16},{24,28},{28,24},{1,5},{5... | collective-permute-start | bytes 393224 | tf_op jit(solution)/shard_map/ppermute | solution.py:671
  34.9 1.5 %collective-permute-start.13 = (bf16[128,512]{1,0:T(8,128)(2,1)S(1)}, bf16[128,512]{1,0:T(8,128)(2,1)S(1)}, u32[]{:S(2)}, u32[]{:S(2)}) collective-permute-start(bf16[128,512]{1,0:T(8,128)(2,1)S(1)} %shard_map.82.rest_5_), channel_id=1, source_target_pairs={{0,2},{1,3},{2,0},{3,1},{4,6},{5,7},{6,4},{7,5},{8,10},{9,11},{10,... | collective-permute-start | bytes 393224 | tf_op jit(solution)/shard_map/ppermute | solution.py:671
  36.4 3.0 %collective-permute-done.8.refs_7_.refs_4_ = bf16[272,512]{1,0:T(8,128)(2,1)S(1)} collective-permute-done((bf16[272,512]{1,0:T(8,128)(2,1)S(1)}, bf16[272,512]{1,0:T(8,128)(2,1)S(1)}, u32[]{:S(2)}, u32[]{:S(2)}) %collective-permute-start.8) | collective-permute-done | bytes 278560 | tf_op jit(solution)/shard_map/ppermute | solution.py:671
  39.5 1.5 %collective-permute-start.14 = (bf16[128,512]{1,0:T(8,128)(2,1)S(1)}, bf16[128,512]{1,0:T(8,128)(2,1)S(1)}, u32[]{:S(2)}, u32[]{:S(2)}) collective-permute-start(bf16[128,512]{1,0:T(8,128)(2,1)S(1)} %shard_map.82.rest_5_), channel_id=1, source_target_pairs={{0,6},{1,7},{2,4},{3,5},{4,2},{5,3},{6,0},{7,1},{8,14},{9,15},{10,... | collective-permute-start | bytes 393224 | tf_op jit(solution)/shard_map/ppermute | solution.py:671
  41.0 0.9 %collective-permute-done.6.refs_3_.rest_4_ = bf16[272,512]{1,0:T(8,128)(2,1)S(1)} collective-permute-done((bf16[272,512]{1,0:T(8,128)(2,1)S(1)}, bf16[272,512]{1,0:T(8,128)(2,1)S(1)}, u32[]{:S(2)}, u32[]{:S(2)}) %collective-permute-start.6) | collective-permute-done | bytes 278560 | tf_op jit(solution)/shard_map/ppermute | solution.py:671
  41.9 3.4 %shard_map.79 = (s32[512,8]{1,0:T(8,128)S(1)}, s32[2,512,2]{2,1,0:T(8,128)S(1)}, s32[2,512,2]{2,1,0:T(8,128)S(1)}) custom-call(s32[2]{0:T(128)S(1)} %copy-done.4, bf16[272,512]{1,0:T(8,128)(2,1)S(1)} %copy-done.2, bf16[272,512]{1,0:T(8,128)(2,1)S(1)} %get-tuple-element.21.refs_1_.rest_1_, ...), custom_call_target="tpu_custom_call" | custom-call | flops 1000000 | bytes 1 | tf_op jit(solution)/shard_map/pallas_call | solution.py:784
  45.3 1.6 %collective-permute-start.12 = (bf16[256,512]{1,0:T(8,128)(2,1)S(1)}, bf16[256,512]{1,0:T(8,128)(2,1)S(1)}, u32[]{:S(2)}, u32[]{:S(2)}) collective-permute-start(bf16[256,512]{1,0:T(8,128)(2,1)S(1)} %shard_map.80.rest_2_), channel_id=1, source_target_pairs={{0,2},{1,3},{2,0},{3,1},{4,6},{5,7},{6,4},{7,5},{8,10},{9,11},{10,... | collective-permute-start | bytes 786440 | tf_op jit(solution)/shard_map/ppermute | solution.py:671
  46.9 7.0 %shard_map.83 = (bf16[2,128,2048]{2,1,0:T(8,128)(2,1)}, f32[2,2,640]{2,1,0:T(2,128)}, f32[8,128]{1,0:T(8,128)}, bf16[512,2048]{1,0:T(8,128)(2,1)}, bf16[512,512]{1,0:T(8,128)(2,1)S(1)}) custom-call(s32[2]{0:T(128)S(1)} %copy-done.4, bf16[2,128,2048]{2,1,0:T(8,128)(2,1)S(1)} %copy-done.3, ...), custom_call_target="tpu_custom_call", output_to_operand_aliasing={{0}: (12, {})} | custom-call | flops 10000000000 | bytes 10000000 | tf_op jit(solution)/shard_map/pallas_call | solution.py:811
  53.9 0.7 %shard_map.84 = bf16[1024,512]{1,0:T(8,128)(2,1)S(1)} custom-call(bf16[144,512]{1,0:T(8,128)(2,1)S(1)} %collective-permute-done.3.x_own.refs_4_.refs_0_, bf16[272,512]{1,0:T(8,128)(2,1)S(1)} %collective-permute-done.7.refs_5_.refs_1_, bf16[256,512]{1,0:T(8,128)(2,1)S(1)} %collective-permute-done.12.refs_2_, ...), custom_call_target="tpu_custom_call" | custom-call | flops 2000000000 | bytes 4000000 | tf_op jit(solution)/shard_map/pallas_call | solution.py:846
  54.7 1.5 %shard_map.85._ = bf16[512,2048]{1,0:T(8,128)(2,1)} custom-call(bf16[144,512]{1,0:T(8,128)(2,1)S(1)} %collective-permute-done.3.x_own.refs_4_.refs_0_, bf16[272,512]{1,0:T(8,128)(2,1)S(1)} %collective-permute-done.7.refs_5_.refs_1_, bf16[256,512]{1,0:T(8,128)(2,1)S(1)} %collective-permute-done.12.refs_2_, ...), custom_call_target="tpu_custom_call", output_to_operand_aliasing={{}: (8, {})} | custom-call | flops 2000000000 | bytes 4000000 | tf_op jit(solution)/shard_map/pallas_call | solution.py:856
  56.2 1.2 %collective-permute-done.15.sent_ref = bf16[1024,512]{1,0:T(8,128)(2,1)S(1)} collective-permute-done((bf16[1024,512]{1,0:T(8,128)(2,1)S(1)}, bf16[1024,512]{1,0:T(8,128)(2,1)S(1)}, u32[]{:S(2)}, u32[]{:S(2)}) %collective-permute-start.15) | collective-permute-done | bytes 1048608 | tf_op jit(solution)/shard_map/ppermute | solution.py:671
  57.3 1.0 %shard_map.86 = bf16[512,2048]{1,0:T(8,128)(2,1)} custom-call(bf16[1024,512]{1,0:T(8,128)(2,1)S(1)} %collective-permute-done.15.sent_ref, bf16[512,2048]{1,0:T(8,128)(2,1)} %shard_map.85._), custom_call_target="tpu_custom_call", output_to_operand_aliasing={{}: (1, {})} | custom-call | bytes 1000000 | tf_op jit(solution)/shard_map/pallas_call | solution.py:866
  (21 shorter events, 0.2 us)
Async XLA Ops:
  0.6 30.2 %copy-start.3 = (bf16[2,128,2048]{2,1,0:T(8,128)(2,1)S(1)}, bf16[2,128,2048]{2,1,0:T(8,128)(2,1)}, u32[]{:S(2)}) copy-start(bf16[2,128,2048]{2,1,0:T(8,128)(2,1)} %q_ref.3) | copy-start | bytes 3145732
  0.6 30.2 %copy-start.4 = (s32[2]{0:T(128)S(1)}, s32[2]{0:T(128)}, u32[]{:S(2)}) copy-start(s32[2]{0:T(128)} %offsets_ref.7) | copy-start | bytes 28
  3.3 13.1 %collective-permute-start.2 = (bf16[272,512]{1,0:T(8,128)(2,1)}, bf16[272,512]{1,0:T(8,128)(2,1)S(1)}, u32[]{:S(2)}, u32[]{:S(2)}) collective-permute-start(bf16[272,512]{1,0:T(8,128)(2,1)} %get-tuple-element.18.both.refs_0_.both_ref.rest_0_), channel_id=1, source_target_pairs={{0,4},{4,0},{8,12},{12,8},{16,20},{20,16},{24,28},{28,24},{1,5},{5... | collective-permute-start | bytes 835592 | tf_op jit(solution)/shard_map/ppermute | solution.py:671
  6.3 13.9 %collective-permute-start = (bf16[272,512]{1,0:T(8,128)(2,1)}, bf16[272,512]{1,0:T(8,128)(2,1)S(1)}, u32[]{:S(2)}, u32[]{:S(2)}) collective-permute-start(bf16[272,512]{1,0:T(8,128)(2,1)} %get-tuple-element.18.both.refs_0_.both_ref.rest_0_), channel_id=1, source_target_pairs={{0,8},{4,12},{8,16},{12,20},{16,24},{20,28},{24,0},{28,4},{1,9},{5... | collective-permute-start | bytes 835592 | tf_op jit(solution)/shard_map/ppermute | solution.py:671
  7.9 6.8 %collective-permute-start.3 = (bf16[144,512]{1,0:T(8,128)(2,1)}, bf16[144,512]{1,0:T(8,128)(2,1)S(1)}, u32[]{:S(2)}, u32[]{:S(2)}) collective-permute-start(bf16[144,512]{1,0:T(8,128)(2,1)} %get-tuple-element.19), channel_id=1, source_target_pairs={{0,2},{1,3},{2,0},{3,1},{4,6},{5,7},{6,4},{7,5},{8,10},{9,11},{10,... | collective-permute-start | bytes 442376 | tf_op jit(solution)/shard_map/ppermute | solution.py:671
  9.4 7.0 %collective-permute-start.4 = (bf16[144,512]{1,0:T(8,128)(2,1)}, bf16[144,512]{1,0:T(8,128)(2,1)S(1)}, u32[]{:S(2)}, u32[]{:S(2)}) collective-permute-start(bf16[144,512]{1,0:T(8,128)(2,1)} %get-tuple-element.19), channel_id=1, source_target_pairs={{0,6},{1,7},{2,4},{3,5},{4,2},{5,3},{6,0},{7,1},{8,14},{9,15},{10,... | collective-permute-start | bytes 442376 | tf_op jit(solution)/shard_map/ppermute | solution.py:671
  9.9 10.3 %collective-permute-start.1 = (bf16[144,512]{1,0:T(8,128)(2,1)}, bf16[144,512]{1,0:T(8,128)(2,1)S(1)}, u32[]{:S(2)}, u32[]{:S(2)}) collective-permute-start(bf16[144,512]{1,0:T(8,128)(2,1)} %get-tuple-element.19), channel_id=1, source_target_pairs={{0,24},{4,28},{8,0},{12,4},{16,8},{20,12},{24,16},{28,20},{1,25},{... | collective-permute-start | bytes 442376 | tf_op jit(solution)/shard_map/ppermute | solution.py:671
  16.4 1.0 %copy-start = (bf16[272,512]{1,0:T(8,128)(2,1)S(1)}, bf16[272,512]{1,0:T(8,128)(2,1)}, u32[]{:S(2)}) copy-start(bf16[272,512]{1,0:T(8,128)(2,1)} %get-tuple-element.18.both.refs_0_.both_ref.rest_0_) | copy-start | bytes 835588
  17.3 24.6 %copy-start.2 = (bf16[272,512]{1,0:T(8,128)(2,1)S(1)}, bf16[272,512]{1,0:T(8,128)(2,1)}, u32[]{:S(2)}) copy-start(bf16[272,512]{1,0:T(8,128)(2,1)} %get-tuple-element.18.both.refs_0_.both_ref.rest_0_) | copy-start | bytes 835588
  17.4 27.9 %collective-permute-start.5 = (bf16[288,512]{1,0:T(8,128)(2,1)S(1)}, bf16[288,512]{1,0:T(8,128)(2,1)S(1)}, u32[]{:S(2)}, u32[]{:S(2)}) collective-permute-start(bf16[288,512]{1,0:T(8,128)(2,1)S(1)} %get-tuple-element.20._), channel_id=1, source_target_pairs={{0,16},{4,20},{8,24},{12,28},{16,0},{20,4},{24,8},{28,12},{1,17},{... | collective-permute-start | bytes 884744 | tf_op jit(solution)/shard_map/ppermute | solution.py:671
  20.3 8.0 %collective-permute-start.10 = (bf16[128,512]{1,0:T(8,128)(2,1)S(1)}, bf16[128,512]{1,0:T(8,128)(2,1)S(1)}, u32[]{:S(2)}, u32[]{:S(2)}) collective-permute-start(bf16[128,512]{1,0:T(8,128)(2,1)S(1)} %get-tuple-element.24.relay), channel_id=1, source_target_pairs={{0,8},{4,12},{24,16},{28,20},{1,9},{5,13},{25,17},{29,21},{2,10},{... | collective-permute-start | bytes 393224 | tf_op jit(solution)/shard_map/ppermute | solution.py:671
  23.8 11.2 %collective-permute-start.7 = (bf16[272,512]{1,0:T(8,128)(2,1)S(1)}, bf16[272,512]{1,0:T(8,128)(2,1)S(1)}, u32[]{:S(2)}, u32[]{:S(2)}) collective-permute-start(bf16[272,512]{1,0:T(8,128)(2,1)S(1)} %get-tuple-element.21.refs_1_.rest_1_), channel_id=1, source_target_pairs={{0,2},{1,3},{2,0},{3,1},{4,6},{5,7},{6,4},{7,5},{8,10},{9,11},{10,... | collective-permute-start | bytes 835592 | tf_op jit(solution)/shard_map/ppermute | solution.py:671
  25.3 14.1 %collective-permute-start.8 = (bf16[272,512]{1,0:T(8,128)(2,1)S(1)}, bf16[272,512]{1,0:T(8,128)(2,1)S(1)}, u32[]{:S(2)}, u32[]{:S(2)}) collective-permute-start(bf16[272,512]{1,0:T(8,128)(2,1)S(1)} %get-tuple-element.21.refs_1_.rest_1_), channel_id=1, source_target_pairs={{0,6},{1,7},{2,4},{3,5},{4,2},{5,3},{6,0},{7,1},{8,14},{9,15},{10,... | collective-permute-start | bytes 835592 | tf_op jit(solution)/shard_map/ppermute | solution.py:671
  26.8 15.1 %collective-permute-start.6 = (bf16[272,512]{1,0:T(8,128)(2,1)S(1)}, bf16[272,512]{1,0:T(8,128)(2,1)S(1)}, u32[]{:S(2)}, u32[]{:S(2)}) collective-permute-start(bf16[272,512]{1,0:T(8,128)(2,1)S(1)} %get-tuple-element.21.refs_1_.rest_1_), channel_id=1, source_target_pairs={{0,4},{4,0},{8,12},{12,8},{16,20},{20,16},{24,28},{28,24},{1,5},{5... | collective-permute-start | bytes 835592 | tf_op jit(solution)/shard_map/ppermute | solution.py:671
  28.2 5.3 %collective-permute-start.9 = (bf16[32,512]{1,0:T(8,128)(2,1)S(1)}, bf16[32,512]{1,0:T(8,128)(2,1)S(1)}, u32[]{:S(2)}, u32[]{:S(2)}) collective-permute-start(bf16[32,512]{1,0:T(8,128)(2,1)S(1)} %get-tuple-element.22), channel_id=1, source_target_pairs={{0,16},{4,20},{8,24},{12,28},{16,0},{20,4},{24,8},{28,12},{1,17},{... | collective-permute-start | bytes 98312 | tf_op jit(solution)/shard_map/ppermute | solution.py:671
  30.8 1.0 %copy-start.1 = (bf16[272,512]{1,0:T(8,128)(2,1)S(1)}, bf16[272,512]{1,0:T(8,128)(2,1)}, u32[]{:S(2)}) copy-start(bf16[272,512]{1,0:T(8,128)(2,1)} %get-tuple-element.18.both.refs_0_.both_ref.rest_0_) | copy-start | bytes 835588
  33.5 13.3 %collective-permute-start.11 = (bf16[128,512]{1,0:T(8,128)(2,1)S(1)}, bf16[128,512]{1,0:T(8,128)(2,1)S(1)}, u32[]{:S(2)}, u32[]{:S(2)}) collective-permute-start(bf16[128,512]{1,0:T(8,128)(2,1)S(1)} %shard_map.82.rest_5_), channel_id=1, source_target_pairs={{0,4},{4,0},{8,12},{12,8},{16,20},{20,16},{24,28},{28,24},{1,5},{5... | collective-permute-start | bytes 393224 | tf_op jit(solution)/shard_map/ppermute | solution.py:671
  34.9 18.9 %collective-permute-start.13 = (bf16[128,512]{1,0:T(8,128)(2,1)S(1)}, bf16[128,512]{1,0:T(8,128)(2,1)S(1)}, u32[]{:S(2)}, u32[]{:S(2)}) collective-permute-start(bf16[128,512]{1,0:T(8,128)(2,1)S(1)} %shard_map.82.rest_5_), channel_id=1, source_target_pairs={{0,2},{1,3},{2,0},{3,1},{4,6},{5,7},{6,4},{7,5},{8,10},{9,11},{10,... | collective-permute-start | bytes 393224 | tf_op jit(solution)/shard_map/ppermute | solution.py:671
  39.5 14.4 %collective-permute-start.14 = (bf16[128,512]{1,0:T(8,128)(2,1)S(1)}, bf16[128,512]{1,0:T(8,128)(2,1)S(1)}, u32[]{:S(2)}, u32[]{:S(2)}) collective-permute-start(bf16[128,512]{1,0:T(8,128)(2,1)S(1)} %shard_map.82.rest_5_), channel_id=1, source_target_pairs={{0,6},{1,7},{2,4},{3,5},{4,2},{5,3},{6,0},{7,1},{8,14},{9,15},{10,... | collective-permute-start | bytes 393224 | tf_op jit(solution)/shard_map/ppermute | solution.py:671
  45.3 8.6 %collective-permute-start.12 = (bf16[256,512]{1,0:T(8,128)(2,1)S(1)}, bf16[256,512]{1,0:T(8,128)(2,1)S(1)}, u32[]{:S(2)}, u32[]{:S(2)}) collective-permute-start(bf16[256,512]{1,0:T(8,128)(2,1)S(1)} %shard_map.80.rest_2_), channel_id=1, source_target_pairs={{0,2},{1,3},{2,0},{3,1},{4,6},{5,7},{6,4},{7,5},{8,10},{9,11},{10,... | collective-permute-start | bytes 786440 | tf_op jit(solution)/shard_map/ppermute | solution.py:671
  54.6 2.7 %collective-permute-start.15 = (bf16[1024,512]{1,0:T(8,128)(2,1)S(1)}, bf16[1024,512]{1,0:T(8,128)(2,1)S(1)}, u32[]{:S(2)}, u32[]{:S(2)}) collective-permute-start(bf16[1024,512]{1,0:T(8,128)(2,1)S(1)} %shard_map.84), channel_id=1, source_target_pairs={{0,1},{1,0},{2,3},{3,2},{4,5},{5,4},{6,7},{7,6},{8,9},{9,8},{10,11... | collective-permute-start | bytes 3145736 | tf_op jit(solution)/shard_map/ppermute | solution.py:671

commit v3 on v0

--- a/solution.py
+++ b/solution.py
@@ -369,17 +369,20 @@
         relay_ref[...] = both[span : 2 * span, :]
 
 
-def join_second_kernel(beyond, relay, relayed, *rest):
-    out_ref, late_ref = rest[-2:]
-    span = relay.shape[0]
+def pick_late_kernel(relay, relayed, _, out_ref):
     level = lax.axis_index("ctx") // 2
-    out_ref[: 2 * span, :] = beyond[: 2 * span, :]
     for ref, chosen in ((relay, (level == 0) | (level == 3)), (relayed, (level == 1) | (level == 2))):
 
         @pl.when(chosen)
         def _(ref=ref):
-            out_ref[2 * span :, :] = ref[...]
-            late_ref[...] = ref[...]
+            out_ref[...] = ref[...]
+
+
+def end_kernel(beyond, late, *rest):
+    out_ref = rest[-1]
+    span = late.shape[0]
+    out_ref[: 2 * span, :] = beyond[: 2 * span, :]
+    out_ref[2 * span :, :] = late[...]
 
 
 def place_of(turn, flip, shards):
@@ -790,15 +793,24 @@
         cost_estimate=cost(10**6, 1),
     )(offsets, query, both, y_own)
 
-    end, late = pl.pallas_call(
-        join_second_kernel,
-        out_shape=(piece(3 * span), piece(span)),
-        in_specs=[vmem] * 3 + [anywhere] * 3,
-        out_specs=(vmem, vmem),
-        compiler_params=params,
-        cost_estimate=cost(10**6, 1),
-    )(beyond, relay, relayed, y_beside, x_beside, late_done)
-    d_late, y_late, x_end = across_both(late), across_y(late), across_x(end)
+    late = pl.pallas_call(
+        pick_late_kernel,
+        out_shape=piece(span),
+        in_specs=[vmem] * 2 + [anywhere],
+        out_specs=vmem,
+        compiler_params=params,
+        cost_estimate=cost(0, 1),
+    )(relay, relayed, late_done)
+    y_late, d_late = across_y(late), across_both(late)
+    end = pl.pallas_call(
+        end_kernel,
+        out_shape=piece(3 * span),
+        in_specs=[vmem] * 2 + [anywhere] * 2,
+        out_specs=vmem,
+        compiler_params=params,
+        cost_estimate=cost(0, 1),
+    )(beyond, late, y_beside, x_beside)
+    x_end = across_x(end)
 
     tokens = pltpu.VMEM((shards * span, width), jnp.bfloat16)
     late_tokens = pltpu.VMEM((2 * span, width), jnp.bfloat16)

time: 51.7 us -> 49.2 us (0.952)
  waiting for transfers between devices: 9.27 us -> 6.65 us
    ppermute x14, waiting for transfers between devices: 9.27 us -> 6.65 us  [send(): return lax.ppermute(value, axis, pairs)]
  transfers between devices with their start and end apart: 14 -> 14, of which waited for: 9 -> 5; matrix products, arithmetic and copies ran while one was open for 0% -> 0% of each run, Pallas kernels for 26% -> 28%
where the time goes in v3:
time: 49.2 us; the launch traced here: 48.9 us
  starting transfers between devices  22.5 us (46%)
  Pallas kernels  17.9 us (36%)
  waiting for transfers between devices  6.65 us (14%)
  local copies, waits for them, and re-layouts  0.97 us (2%)
  between operations  0.95 us (2%)
    ppermute x14, starting transfers between devices, send(): return lax.ppermute(value, axis, pairs)  22.5 us
    pallas_call x1, Pallas kernels, local_in_planes(): pl.pallas_call(early_kernel, grid_spec=pltpu.PrefetchScalarGridSpec(num_s...  8.28 us
    ppermute x14, waiting for transfers between devices, send(): return lax.ppermute(value, axis, pairs)  6.65 us
    pallas_call x1, Pallas kernels, local_in_planes(): pl.pallas_call(prepare_kernel, out_shape=(piece(2 * span + NOTES), piece(...  2.65 us
    pallas_call x1, Pallas kernels, local_in_planes(): pl.pallas_call(far_index_kernel, out_shape=slots_shape, in_specs=[smem] +...  2.04 us
    pallas_call x1, Pallas kernels, local_in_planes(): pl.pallas_call(far_kept_kernel, out_shape=cache_shape, in_specs=[vmem] *...  1.53 us
    pallas_call x1, Pallas kernels, local_in_planes(): pl.pallas_call(late_kernel, grid_spec=pltpu.PrefetchScalarGridSpec(num_sc...  1.39 us
  transfers between devices with their start and end apart: 14, of which 5 were waited for; matrix products, arithmetic and copies ran while one was open for 0% of the time, Pallas kernels for 28%

profile of v3, /device:TPU:0, one launch (start us, length us, event | category | flops | bytes accessed | tf_op | source)
XLA Modules:
  0.0 48.9 jit_solution(10993783874575935183)
XLA Ops:
  0.7 2.7 %shard_map.76 = (bf16[272,512]{1,0:T(8,128)(2,1)}, bf16[144,512]{1,0:T(8,128)(2,1)}) custom-call(s32[2]{0:T(128)} %offsets_ref.7, bf16[2,128,512]{2,1,0:T(8,128)(2,1)} %kv_ref.1, s32[2,1,2,512]{3,2,1,0:T(2,128)} %keep_ref.1, s32[1,1024]{1,0:T(1,128)} %bitcast.1), custom_call_target="tpu_custom_call" | custom-call | flops 1000000000 | bytes 1 | tf_op jit(solution)/shard_map/pallas_call | solution.py:733
  3.3 3.0 %collective-permute-start.2 = (bf16[272,512]{1,0:T(8,128)(2,1)}, bf16[272,512]{1,0:T(8,128)(2,1)S(1)}, u32[]{:S(2)}, u32[]{:S(2)}) collective-permute-start(bf16[272,512]{1,0:T(8,128)(2,1)} %get-tuple-element.17.both.both_ref.rest_0_), channel_id=1, source_target_pairs={{0,4},{4,0},{8,12},{12,8},{16,20},{20,16},{24,28},{28,24},{1,5},{5... | collective-permute-start | bytes 835592 | tf_op jit(solution)/shard_map/ppermute | solution.py:694
  6.3 1.6 %collective-permute-start = (bf16[272,512]{1,0:T(8,128)(2,1)}, bf16[272,512]{1,0:T(8,128)(2,1)S(1)}, u32[]{:S(2)}, u32[]{:S(2)}) collective-permute-start(bf16[272,512]{1,0:T(8,128)(2,1)} %get-tuple-element.17.both.both_ref.rest_0_), channel_id=1, source_target_pairs={{0,8},{4,12},{8,16},{12,20},{16,24},{20,28},{24,0},{28,4},{1,9},{5... | collective-permute-start | bytes 835592 | tf_op jit(solution)/shard_map/ppermute | solution.py:694
  7.9 1.4 %collective-permute-start.4 = (bf16[144,512]{1,0:T(8,128)(2,1)}, bf16[144,512]{1,0:T(8,128)(2,1)S(1)}, u32[]{:S(2)}, u32[]{:S(2)}) collective-permute-start(bf16[144,512]{1,0:T(8,128)(2,1)} %get-tuple-element.18), channel_id=1, source_target_pairs={{0,6},{1,7},{2,4},{3,5},{4,2},{5,3},{6,0},{7,1},{8,14},{9,15},{10,... | collective-permute-start | bytes 442376 | tf_op jit(solution)/shard_map/ppermute | solution.py:694
  9.4 0.5 %collective-permute-start.3 = (bf16[144,512]{1,0:T(8,128)(2,1)}, bf16[144,512]{1,0:T(8,128)(2,1)S(1)}, u32[]{:S(2)}, u32[]{:S(2)}) collective-permute-start(bf16[144,512]{1,0:T(8,128)(2,1)} %get-tuple-element.18), channel_id=1, source_target_pairs={{0,2},{1,3},{2,0},{3,1},{4,6},{5,7},{6,4},{7,5},{8,10},{9,11},{10,... | collective-permute-start | bytes 442376 | tf_op jit(solution)/shard_map/ppermute | solution.py:694
  9.9 2.0 %collective-permute-start.1 = (bf16[144,512]{1,0:T(8,128)(2,1)}, bf16[144,512]{1,0:T(8,128)(2,1)S(1)}, u32[]{:S(2)}, u32[]{:S(2)}) collective-permute-start(bf16[144,512]{1,0:T(8,128)(2,1)} %get-tuple-element.18), channel_id=1, source_target_pairs={{0,24},{4,28},{8,0},{12,4},{16,8},{20,12},{24,16},{28,20},{1,25},{... | collective-permute-start | bytes 442376 | tf_op jit(solution)/shard_map/ppermute | solution.py:694
  11.9 3.8 %collective-permute-done.4.d_own.refs_3_ = bf16[144,512]{1,0:T(8,128)(2,1)S(1)} collective-permute-done((bf16[144,512]{1,0:T(8,128)(2,1)}, bf16[144,512]{1,0:T(8,128)(2,1)S(1)}, u32[]{:S(2)}, u32[]{:S(2)}) %collective-permute-start.4) | collective-permute-done | bytes 147488 | tf_op jit(solution)/shard_map/ppermute | solution.py:694
  15.7 0.6 %collective-permute-done.3.x_own.refs_0_ = bf16[144,512]{1,0:T(8,128)(2,1)S(1)} collective-permute-done((bf16[144,512]{1,0:T(8,128)(2,1)}, bf16[144,512]{1,0:T(8,128)(2,1)S(1)}, u32[]{:S(2)}, u32[]{:S(2)}) %collective-permute-start.3) | collective-permute-done | bytes 147488 | tf_op jit(solution)/shard_map/ppermute | solution.py:694
  16.3 0.1 collective-permute-done.2.y_own.beside_ref.rest_3_
  16.4 1.0 %copy-done = bf16[272,512]{1,0:T(8,128)(2,1)S(1)} copy-done((bf16[272,512]{1,0:T(8,128)(2,1)S(1)}, bf16[272,512]{1,0:T(8,128)(2,1)}, u32[]{:S(2)}) %copy-start) | copy-done | bytes 278552
  17.4 2.9 %collective-permute-start.5 = (bf16[288,512]{1,0:T(8,128)(2,1)S(1)}, bf16[288,512]{1,0:T(8,128)(2,1)S(1)}, u32[]{:S(2)}, u32[]{:S(2)}) collective-permute-start(bf16[288,512]{1,0:T(8,128)(2,1)S(1)} %shard_map.77._), channel_id=1, source_target_pairs={{0,16},{4,20},{8,24},{12,28},{16,0},{20,4},{24,8},{28,12},{1,17},{... | collective-permute-start | bytes 884744 | tf_op jit(solution)/shard_map/ppermute | solution.py:694
  20.3 1.6 %collective-permute-start.8 = (bf16[272,512]{1,0:T(8,128)(2,1)S(1)}, bf16[272,512]{1,0:T(8,128)(2,1)S(1)}, u32[]{:S(2)}, u32[]{:S(2)}) collective-permute-start(bf16[272,512]{1,0:T(8,128)(2,1)S(1)} %get-tuple-element.19.rest_1_), channel_id=1, source_target_pairs={{0,2},{1,3},{2,0},{3,1},{4,6},{5,7},{6,4},{7,5},{8,10},{9,11},{10,... | collective-permute-start | bytes 835592 | tf_op jit(solution)/shard_map/ppermute | solution.py:694
  21.8 1.5 %collective-permute-start.6 = (bf16[272,512]{1,0:T(8,128)(2,1)S(1)}, bf16[272,512]{1,0:T(8,128)(2,1)S(1)}, u32[]{:S(2)}, u32[]{:S(2)}) collective-permute-start(bf16[272,512]{1,0:T(8,128)(2,1)S(1)} %get-tuple-element.19.rest_1_), channel_id=1, source_target_pairs={{0,4},{4,0},{8,12},{12,8},{16,20},{20,16},{24,28},{28,24},{1,5},{5... | collective-permute-start | bytes 835592 | tf_op jit(solution)/shard_map/ppermute | solution.py:694
  23.4 3.5 %collective-permute-start.7 = (bf16[128,512]{1,0:T(8,128)(2,1)S(1)}, bf16[128,512]{1,0:T(8,128)(2,1)S(1)}, u32[]{:S(2)}, u32[]{:S(2)}) collective-permute-start(bf16[128,512]{1,0:T(8,128)(2,1)S(1)} %get-tuple-element.20.relay), channel_id=1, source_target_pairs={{0,8},{4,12},{24,16},{28,20},{1,9},{5,13},{25,17},{29,21},{2,10},{... | collective-permute-start | bytes 393224 | tf_op jit(solution)/shard_map/ppermute | solution.py:694
  26.9 1.4 %shard_map.79 = (bf16[2,128,2048]{2,1,0:T(8,128)(2,1)}, f32[2,2,640]{2,1,0:T(2,128)}, f32[8,128]{1,0:T(8,128)S(1)}) custom-call(s32[2]{0:T(128)S(1)} %copy-done.3, bf16[2,128,2048]{2,1,0:T(8,128)(2,1)S(1)} %copy-done.2, bf16[272,512]{1,0:T(8,128)(2,1)S(1)} %copy-done.1, bf16[272,512]{1,0:T(8,128)(2,1)S(1)} %collective-permute-done.2.y_own.beside_ref.rest_3_), custom_call_target="tpu_custom_call" | custom-call | flops 1000000 | bytes 1 | tf_op jit(solution)/shard_map/pallas_call | solution.py:783
  28.3 1.1 %collective-permute-done.7.relayed = bf16[128,512]{1,0:T(8,128)(2,1)S(1)} collective-permute-done((bf16[128,512]{1,0:T(8,128)(2,1)S(1)}, bf16[128,512]{1,0:T(8,128)(2,1)S(1)}, u32[]{:S(2)}, u32[]{:S(2)}) %collective-permute-start.7) | collective-permute-done | bytes 131104 | tf_op jit(solution)/shard_map/ppermute | solution.py:694
  29.3 0.2 shard_map.80.rest_5_.late.refs_6_
  29.5 0.7 %collective-permute-start.12 = (bf16[128,512]{1,0:T(8,128)(2,1)S(1)}, bf16[128,512]{1,0:T(8,128)(2,1)S(1)}, u32[]{:S(2)}, u32[]{:S(2)}) collective-permute-start(bf16[128,512]{1,0:T(8,128)(2,1)S(1)} %shard_map.80.rest_5_.late.refs_6_), channel_id=1, source_target_pairs={{0,4},{4,0},{8,12},{12,8},{16,20},{20,16},{24,28},{28,24},{1,5},{5... | collective-permute-start | bytes 393224 | tf_op jit(solution)/shard_map/ppermute | solution.py:694
  30.3 1.3 %collective-permute-start.11 = (bf16[128,512]{1,0:T(8,128)(2,1)S(1)}, bf16[128,512]{1,0:T(8,128)(2,1)S(1)}, u32[]{:S(2)}, u32[]{:S(2)}) collective-permute-start(bf16[128,512]{1,0:T(8,128)(2,1)S(1)} %shard_map.80.rest_5_.late.refs_6_), channel_id=1, source_target_pairs={{0,6},{1,7},{2,4},{3,5},{4,2},{5,3},{6,0},{7,1},{8,14},{9,15},{10,... | collective-permute-start | bytes 393224 | tf_op jit(solution)/shard_map/ppermute | solution.py:694
  31.6 1.6 %collective-permute-start.10 = (bf16[272,512]{1,0:T(8,128)(2,1)S(1)}, bf16[272,512]{1,0:T(8,128)(2,1)S(1)}, u32[]{:S(2)}, u32[]{:S(2)}) collective-permute-start(bf16[272,512]{1,0:T(8,128)(2,1)S(1)} %collective-permute-done.8.rest_1_.x_beside.refs_1_), channel_id=1, source_target_pairs={{0,4},{4,0},{8,12},{12,8},{16,20},{20,16},{24,28},{28,24},{1,5},{5... | collective-permute-start | bytes 835592 | tf_op jit(solution)/shard_map/ppermute | solution.py:694
  33.2 0.0 collective-permute-done.6.rest_4_.rest_0_
  33.2 0.0 collective-permute-done.5.rest_2_.beyond
  33.3 0.7 %collective-permute-start.9 = (bf16[384,512]{1,0:T(8,128)(2,1)S(1)}, bf16[384,512]{1,0:T(8,128)(2,1)S(1)}, u32[]{:S(2)}, u32[]{:S(2)}) collective-permute-start(bf16[384,512]{1,0:T(8,128)(2,1)S(1)} %shard_map.82), channel_id=1, source_target_pairs={{0,2},{1,3},{2,0},{3,1},{4,6},{5,7},{6,4},{7,5},{8,10},{9,11},{10,... | collective-permute-start | bytes 1179656 | tf_op jit(solution)/shard_map/ppermute | solution.py:694
  34.0 8.3 %shard_map.81 = (bf16[2,128,2048]{2,1,0:T(8,128)(2,1)}, f32[2,2,640]{2,1,0:T(2,128)}, f32[8,128]{1,0:T(8,128)S(1)}, bf16[512,2048]{1,0:T(8,128)(2,1)}, bf16[384,...) custom-call(s32[2]{0:T(128)S(1)} %copy-done.3, ...), custom_call_target="tpu_custom_call", output_to_operand_aliasing={{0}: (8, {}), {1}: (9, {})} | custom-call | flops 10000000000 | bytes 10000000 | tf_op jit(solution)/shard_map/pallas_call | solution.py:825
  42.2 0.0 collective-permute-done.10.d_beside.refs_4_
  42.3 2.0 %shard_map.83.refs_10_ = s32[2,512,2]{2,1,0:T(8,128)S(1)} custom-call(s32[2]{0:T(128)S(1)} %copy-done.3, bf16[144,512]{1,0:T(8,128)(2,1)S(1)} %collective-permute-done.3.x_own.refs_0_, bf16[272,512]{1,0:T(8,128)(2,1)S(1)} %collective-permute-done.8.rest_1_.x_beside.refs_1_, bf16[144,512]{1,0:T(8,128)(2,1)S(1)} %collective-permute-done.4.d_own.refs_3_, ...), custom_call_target="tpu_custom_call" | custom-call | flops 1000000 | bytes 1 | tf_op jit(solution)/shard_map/pallas_call | solution.py:852
  44.3 0.0 collective-permute-done.11.refs_5_
  44.3 0.7 %shard_map.84 = bf16[1024,512]{1,0:T(8,128)(2,1)S(1)} custom-call(bf16[144,512]{1,0:T(8,128)(2,1)S(1)} %collective-permute-done.3.x_own.refs_0_, bf16[272,512]{1,0:T(8,128)(2,1)S(1)} %collective-permute-done.8.rest_1_.x_beside.refs_1_, bf16[384,512]{1,0:T(8,128)(2,1)S(1)} %collective-permute-done.9.refs_2_, ...), custom_call_target="tpu_custom_call" | custom-call | flops 2000000000 | bytes 4000000 | tf_op jit(solution)/shard_map/pallas_call | solution.py:863
  45.1 0.1 collective-permute-start.13
  45.2 1.5 %shard_map.85._ = bf16[512,2048]{1,0:T(8,128)(2,1)} custom-call(bf16[144,512]{1,0:T(8,128)(2,1)S(1)} %collective-permute-done.3.x_own.refs_0_, bf16[272,512]{1,0:T(8,128)(2,1)S(1)} %collective-permute-done.8.rest_1_.x_beside.refs_1_, bf16[384,512]{1,0:T(8,128)(2,1)S(1)} %collective-permute-done.9.refs_2_, ...), custom_call_target="tpu_custom_call", output_to_operand_aliasing={{}: (11, {})} | custom-call | flops 2000000000 | bytes 4000000 | tf_op jit(solution)/shard_map/pallas_call | solution.py:873
  46.7 1.1 %collective-permute-done.13.sent_ref = bf16[1024,512]{1,0:T(8,128)(2,1)S(1)} collective-permute-done((bf16[1024,512]{1,0:T(8,128)(2,1)S(1)}, bf16[1024,512]{1,0:T(8,128)(2,1)S(1)}, u32[]{:S(2)}, u32[]{:S(2)}) %collective-permute-start.13) | collective-permute-done | bytes 1048608 | tf_op jit(solution)/shard_map/ppermute | solution.py:694
  47.8 1.0 %shard_map.86 = bf16[512,2048]{1,0:T(8,128)(2,1)} custom-call(bf16[1024,512]{1,0:T(8,128)(2,1)S(1)} %collective-permute-done.13.sent_ref, bf16[512,2048]{1,0:T(8,128)(2,1)} %shard_map.85._), custom_call_target="tpu_custom_call", output_to_operand_aliasing={{}: (1, {})} | custom-call | bytes 1000000 | tf_op jit(solution)/shard_map/pallas_call | solution.py:890
  (15 shorter events, 0.1 us)
Async XLA Ops:
  0.6 26.2 %copy-start.2 = (bf16[2,128,2048]{2,1,0:T(8,128)(2,1)S(1)}, bf16[2,128,2048]{2,1,0:T(8,128)(2,1)}, u32[]{:S(2)}) copy-start(bf16[2,128,2048]{2,1,0:T(8,128)(2,1)} %q_ref.3) | copy-start | bytes 3145732
  0.6 26.2 %copy-start.3 = (s32[2]{0:T(128)S(1)}, s32[2]{0:T(128)}, u32[]{:S(2)}) copy-start(s32[2]{0:T(128)} %offsets_ref.7) | copy-start | bytes 28
  3.3 13.1 %collective-permute-start.2 = (bf16[272,512]{1,0:T(8,128)(2,1)}, bf16[272,512]{1,0:T(8,128)(2,1)S(1)}, u32[]{:S(2)}, u32[]{:S(2)}) collective-permute-start(bf16[272,512]{1,0:T(8,128)(2,1)} %get-tuple-element.17.both.both_ref.rest_0_), channel_id=1, source_target_pairs={{0,4},{4,0},{8,12},{12,8},{16,20},{20,16},{24,28},{28,24},{1,5},{5... | collective-permute-start | bytes 835592 | tf_op jit(solution)/shard_map/ppermute | solution.py:694
  6.3 13.9 %collective-permute-start = (bf16[272,512]{1,0:T(8,128)(2,1)}, bf16[272,512]{1,0:T(8,128)(2,1)S(1)}, u32[]{:S(2)}, u32[]{:S(2)}) collective-permute-start(bf16[272,512]{1,0:T(8,128)(2,1)} %get-tuple-element.17.both.both_ref.rest_0_), channel_id=1, source_target_pairs={{0,8},{4,12},{8,16},{12,20},{16,24},{20,28},{24,0},{28,4},{1,9},{5... | collective-permute-start | bytes 835592 | tf_op jit(solution)/shard_map/ppermute | solution.py:694
  7.9 7.8 %collective-permute-start.4 = (bf16[144,512]{1,0:T(8,128)(2,1)}, bf16[144,512]{1,0:T(8,128)(2,1)S(1)}, u32[]{:S(2)}, u32[]{:S(2)}) collective-permute-start(bf16[144,512]{1,0:T(8,128)(2,1)} %get-tuple-element.18), channel_id=1, source_target_pairs={{0,6},{1,7},{2,4},{3,5},{4,2},{5,3},{6,0},{7,1},{8,14},{9,15},{10,... | collective-permute-start | bytes 442376 | tf_op jit(solution)/shard_map/ppermute | solution.py:694
  9.4 7.0 %collective-permute-start.3 = (bf16[144,512]{1,0:T(8,128)(2,1)}, bf16[144,512]{1,0:T(8,128)(2,1)S(1)}, u32[]{:S(2)}, u32[]{:S(2)}) collective-permute-start(bf16[144,512]{1,0:T(8,128)(2,1)} %get-tuple-element.18), channel_id=1, source_target_pairs={{0,2},{1,3},{2,0},{3,1},{4,6},{5,7},{6,4},{7,5},{8,10},{9,11},{10,... | collective-permute-start | bytes 442376 | tf_op jit(solution)/shard_map/ppermute | solution.py:694
  9.9 10.3 %collective-permute-start.1 = (bf16[144,512]{1,0:T(8,128)(2,1)}, bf16[144,512]{1,0:T(8,128)(2,1)S(1)}, u32[]{:S(2)}, u32[]{:S(2)}) collective-permute-start(bf16[144,512]{1,0:T(8,128)(2,1)} %get-tuple-element.18), channel_id=1, source_target_pairs={{0,24},{4,28},{8,0},{12,4},{16,8},{20,12},{24,16},{28,20},{1,25},{... | collective-permute-start | bytes 442376 | tf_op jit(solution)/shard_map/ppermute | solution.py:694
  16.4 1.0 %copy-start = (bf16[272,512]{1,0:T(8,128)(2,1)S(1)}, bf16[272,512]{1,0:T(8,128)(2,1)}, u32[]{:S(2)}) copy-start(bf16[272,512]{1,0:T(8,128)(2,1)} %get-tuple-element.17.both.both_ref.rest_0_) | copy-start | bytes 835588
  17.3 9.5 %copy-start.1 = (bf16[272,512]{1,0:T(8,128)(2,1)S(1)}, bf16[272,512]{1,0:T(8,128)(2,1)}, u32[]{:S(2)}) copy-start(bf16[272,512]{1,0:T(8,128)(2,1)} %get-tuple-element.17.both.both_ref.rest_0_) | copy-start | bytes 835588
  17.4 15.9 %collective-permute-start.5 = (bf16[288,512]{1,0:T(8,128)(2,1)S(1)}, bf16[288,512]{1,0:T(8,128)(2,1)S(1)}, u32[]{:S(2)}, u32[]{:S(2)}) collective-permute-start(bf16[288,512]{1,0:T(8,128)(2,1)S(1)} %shard_map.77._), channel_id=1, source_target_pairs={{0,16},{4,20},{8,24},{12,28},{16,0},{20,4},{24,8},{28,12},{1,17},{... | collective-permute-start | bytes 884744 | tf_op jit(solution)/shard_map/ppermute | solution.py:694
  20.3 11.3 %collective-permute-start.8 = (bf16[272,512]{1,0:T(8,128)(2,1)S(1)}, bf16[272,512]{1,0:T(8,128)(2,1)S(1)}, u32[]{:S(2)}, u32[]{:S(2)}) collective-permute-start(bf16[272,512]{1,0:T(8,128)(2,1)S(1)} %get-tuple-element.19.rest_1_), channel_id=1, source_target_pairs={{0,2},{1,3},{2,0},{3,1},{4,6},{5,7},{6,4},{7,5},{8,10},{9,11},{10,... | collective-permute-start | bytes 835592 | tf_op jit(solution)/shard_map/ppermute | solution.py:694
  21.8 11.4 %collective-permute-start.6 = (bf16[272,512]{1,0:T(8,128)(2,1)S(1)}, bf16[272,512]{1,0:T(8,128)(2,1)S(1)}, u32[]{:S(2)}, u32[]{:S(2)}) collective-permute-start(bf16[272,512]{1,0:T(8,128)(2,1)S(1)} %get-tuple-element.19.rest_1_), channel_id=1, source_target_pairs={{0,4},{4,0},{8,12},{12,8},{16,20},{20,16},{24,28},{28,24},{1,5},{5... | collective-permute-start | bytes 835592 | tf_op jit(solution)/shard_map/ppermute | solution.py:694
  23.4 6.0 %collective-permute-start.7 = (bf16[128,512]{1,0:T(8,128)(2,1)S(1)}, bf16[128,512]{1,0:T(8,128)(2,1)S(1)}, u32[]{:S(2)}, u32[]{:S(2)}) collective-permute-start(bf16[128,512]{1,0:T(8,128)(2,1)S(1)} %get-tuple-element.20.relay), channel_id=1, source_target_pairs={{0,8},{4,12},{24,16},{28,20},{1,9},{5,13},{25,17},{29,21},{2,10},{... | collective-permute-start | bytes 393224 | tf_op jit(solution)/shard_map/ppermute | solution.py:694
  29.5 14.8 %collective-permute-start.12 = (bf16[128,512]{1,0:T(8,128)(2,1)S(1)}, bf16[128,512]{1,0:T(8,128)(2,1)S(1)}, u32[]{:S(2)}, u32[]{:S(2)}) collective-permute-start(bf16[128,512]{1,0:T(8,128)(2,1)S(1)} %shard_map.80.rest_5_.late.refs_6_), channel_id=1, source_target_pairs={{0,4},{4,0},{8,12},{12,8},{16,20},{20,16},{24,28},{28,24},{1,5},{5... | collective-permute-start | bytes 393224 | tf_op jit(solution)/shard_map/ppermute | solution.py:694
  30.3 14.1 %collective-permute-start.11 = (bf16[128,512]{1,0:T(8,128)(2,1)S(1)}, bf16[128,512]{1,0:T(8,128)(2,1)S(1)}, u32[]{:S(2)}, u32[]{:S(2)}) collective-permute-start(bf16[128,512]{1,0:T(8,128)(2,1)S(1)} %shard_map.80.rest_5_.late.refs_6_), channel_id=1, source_target_pairs={{0,6},{1,7},{2,4},{3,5},{4,2},{5,3},{6,0},{7,1},{8,14},{9,15},{10,... | collective-permute-start | bytes 393224 | tf_op jit(solution)/shard_map/ppermute | solution.py:694
  31.6 10.7 %collective-permute-start.10 = (bf16[272,512]{1,0:T(8,128)(2,1)S(1)}, bf16[272,512]{1,0:T(8,128)(2,1)S(1)}, u32[]{:S(2)}, u32[]{:S(2)}) collective-permute-start(bf16[272,512]{1,0:T(8,128)(2,1)S(1)} %collective-permute-done.8.rest_1_.x_beside.refs_1_), channel_id=1, source_target_pairs={{0,4},{4,0},{8,12},{12,8},{16,20},{20,16},{24,28},{28,24},{1,5},{5... | collective-permute-start | bytes 835592 | tf_op jit(solution)/shard_map/ppermute | solution.py:694
  33.3 11.1 %collective-permute-start.9 = (bf16[384,512]{1,0:T(8,128)(2,1)S(1)}, bf16[384,512]{1,0:T(8,128)(2,1)S(1)}, u32[]{:S(2)}, u32[]{:S(2)}) collective-permute-start(bf16[384,512]{1,0:T(8,128)(2,1)S(1)} %shard_map.82), channel_id=1, source_target_pairs={{0,2},{1,3},{2,0},{3,1},{4,6},{5,7},{6,4},{7,5},{8,10},{9,11},{10,... | collective-permute-start | bytes 1179656 | tf_op jit(solution)/shard_map/ppermute | solution.py:694
  45.1 2.7 %collective-permute-start.13 = (bf16[1024,512]{1,0:T(8,128)(2,1)S(1)}, bf16[1024,512]{1,0:T(8,128)(2,1)S(1)}, u32[]{:S(2)}, u32[]{:S(2)}) collective-permute-start(bf16[1024,512]{1,0:T(8,128)(2,1)S(1)} %shard_map.84), channel_id=1, source_target_pairs={{0,1},{1,0},{2,3},{3,2},{4,5},{5,4},{6,7},{7,6},{8,9},{9,8},{10,11... | collective-permute-start | bytes 3145736 | tf_op jit(solution)/shard_map/ppermute | solution.py:694

commit v4 on v3

--- a/solution.py
+++ b/solution.py
@@ -446,10 +446,9 @@
     return own
 
 
-def find_slots(early, dests, coded, owner, slots):
+def fill_picks(early, dests, owner, picks):
     shards, halves, cache = dests.shape
-    heads = coded.shape[1] // 8
-    cap = slots.shape[0] // shards
+    cap = picks.shape[1]
     upper = marks(
         lax.broadcasted_iota(jnp.int32, (LANES, LANES), 0)
         <= lax.broadcasted_iota(jnp.int32, (LANES, LANES), 1)
@@ -468,12 +467,22 @@
         ranks.append(jnp.concatenate(parts, axis=1))
     rank_early = jnp.where(early == 0, ranks[0], ranks[1])
     rank_late = jnp.where(early == 0, ranks[1], ranks[0])
+    for shard in range(shards):
+        picks[shard] = marks(rank_early[shard : shard + 1] == place)
+        if shard >= shards - 2:
+            picks[shard + 2] = marks(rank_late[shard : shard + 1] == place)
+
+
+def find_slots(picks, coded, slots):
+    shards, lists = coded.shape[0], coded.shape[1]
+    heads = lists // 8
+    cap = picks.shape[1]
     across = ((1,), (1,))
     for shard in range(shards):
-        found = dot(marks(rank_early[shard : shard + 1] == place), coded[shard], across)
+        found = dot(picks[shard], coded[shard], across)
         tokens = found[:, :heads] * 128.0 + found[:, 4 * heads : 5 * heads]
         if shard >= shards - 2:
-            found = dot(marks(rank_late[shard : shard + 1] == place), coded[shard], across)
+            found = dot(picks[shard + 2], coded[shard], across)
             tokens += found[:, heads : 2 * heads] * 128.0 + found[:, 5 * heads : 6 * heads]
         slots[shard * cap : (shard + 1) * cap, :] = tokens.astype(jnp.int32)
 
@@ -578,19 +587,21 @@
     ]
 
 
-def fill_slots(offsets_ref, notes, keeps, dests, coded, slots_ref):
-    me = lax.axis_index("ctx") * lax.axis_size("kv") + lax.axis_index("kv")
+def fill_slots(notes, keeps, dests, coded, picks_ref, slots_ref, early=None):
     sort_notes(notes, keeps, dests)
     own = follow_lists(keeps, coded, LANES)
+    me = lax.axis_index("ctx") * lax.axis_size("kv") + lax.axis_index("kv")
     for flip in range(2):
-        find_slots(early_of(offsets_ref), dests, coded, me ^ flip, slots_ref.at[flip])
+        if early is not None:
+            fill_picks(early, dests, me ^ flip, picks_ref.at[flip])
+        find_slots(picks_ref.at[flip], coded, slots_ref.at[flip])
     return own
 
 
 def early_kernel(offsets_ref, q_ref, *rest):
     both, beside, beyond, y_own, y_beside = rest[:5]
     out_ref, score_ref, done_ref, cache_ref, top_sent, low_ref, slots_ref = rest[8:15]
-    tokens, top, sem, keeps, dests, coded = rest[15:]
+    picks_ref, tokens, top, sem, keeps, dests, coded = rest[15:]
     done_ref[...] = jnp.zeros(done_ref.shape, jnp.float32)
     span = both.shape[0] // 2 - NOTES // 2
     column = lax.axis_index("kv")
@@ -598,7 +609,8 @@
     notes = [(both, at, 0, 0, 0), (beside, at, 0, 1, 0), (beside, at, 1, 3, 0)]
     notes += [(beyond, at, 0, 2, 0), (beyond, at, 1, 2, 1), (y_own, at, 0, 0, 1)]
     notes += [(y_beside, at, 0, 1, 1), (y_beside, at, 1, 3, 1)]
-    own = fill_slots(offsets_ref, notes, keeps, dests, coded, slots_ref)
+    early = early_of(offsets_ref)
+    own = fill_slots(notes, keeps, dests, coded, picks_ref, slots_ref, early)
     own = jnp.transpose(own.astype(jnp.float32)).astype(jnp.int32)
     pieces = [(both, 0, 0, 0), (beside, 0, 1, 0), (beside, span, 3, 0), (beyond, 0, 2, 0)]
     pieces += [(beyond, span, 2, 1), (y_own, 0, 0, 1), (y_beside, 0, 1, 1), (y_beside, span, 3, 1)]
@@ -619,14 +631,14 @@
     copy.wait()
 
 
-def far_index_kernel(offsets_ref, x_own, x_beside, d_own, d_beside, beyond, _, *rest):
+def far_index_kernel(x_own, x_beside, d_own, d_beside, beyond, picks, _, *rest):
     slots_ref, keeps, dests, coded = rest
     span = x_own.shape[0] - NOTES
     at = 2 * span
     notes = [(x_own, span, 0, 0, 0), (d_own, span, 0, 0, 1), (x_beside, at, 0, 1, 0)]
     notes += [(x_beside, at, 1, 3, 0), (d_beside, at, 0, 1, 1), (d_beside, at, 1, 3, 1)]
     notes += [(beyond, at + NOTES, 0, 2, 0), (beyond, at + NOTES, 1, 2, 1)]
-    fill_slots(offsets_ref, notes, keeps, dests, coded, slots_ref)
+    fill_slots(notes, keeps, dests, coded, picks, slots_ref)
 
 
 def far_rows(flip, refs, far_ref, low, tokens, near_late, far_late):
@@ -822,13 +834,13 @@
         pltpu.VMEM((shards, prompts, cache), jnp.int32),
         pltpu.VMEM((shards, 8 * heads, cache), jnp.bfloat16),
     ]
-    attention, row_scores, early_done, owner_cache, top, low, near_slots = pl.pallas_call(
+    (attention, row_scores, early_done, owner_cache, top, low, near_slots, picks) = pl.pallas_call(
         early_kernel,
         grid_spec=pltpu.PrefetchScalarGridSpec(
             num_scalar_prefetch=1,
             grid=(1,),
             in_specs=[prompt_specs(False)[0]] + [vmem] * 5 + [anywhere] * 3,
-            out_specs=prompt_specs(False) + (vmem, hbm, vmem, vmem, vmem),
+            out_specs=prompt_specs(False) + (vmem, hbm, vmem, vmem, vmem, vmem),
             scratch_shapes=[
                 tokens,
                 pltpu.VMEM((rows - band, width), jnp.bfloat16),
@@ -844,6 +856,7 @@
             piece(rows - band),
             jax.ShapeDtypeStruct((2, band, width), jnp.bfloat16),
             slots_shape,
+            jax.ShapeDtypeStruct((2, shards + 2, rows // shards, cache), jnp.bfloat16),
         ),
         input_output_aliases={8: 0, 9: 1},
         compiler_params=params,
@@ -852,12 +865,12 @@
     far_slots = pl.pallas_call(
         far_index_kernel,
         out_shape=slots_shape,
-        in_specs=[smem] + [vmem] * 5 + [anywhere],
+        in_specs=[vmem] * 6 + [anywhere],
         out_specs=vmem,
         scratch_shapes=tables,
         compiler_params=params,
         cost_estimate=cost(10**6, 1),
-    )(offsets, x_own, x_beside, d_own, d_beside, beyond, early_done)
+    )(x_own, x_beside, d_own, d_beside, beyond, picks, early_done)
     far = (x_own, x_beside, x_end, d_own, d_beside, d_late, late, y_late, low)
     far += (near_slots, far_slots)
     sent = pl.pallas_call(

time: 49.2 us -> 48.5 us (0.986)
  Pallas kernels: 17.9 us -> 17.2 us
    pallas_call x1, Pallas kernels: 2.04 us -> 1.24 us  [local_in_planes(): pl.pallas_call(far_index_kernel, out_shape=slots_shape, in_specs=[vmem] *...]
  transfers between devices with their start and end apart: 14 -> 14, of which waited for: 5 -> 5; matrix products, arithmetic and copies ran while one was open for 0% -> 0% of each run, Pallas kernels for 28% -> 27%
where the time goes in v4:
time: 48.5 us; the launch traced here: 48.2 us
  starting transfers between devices  22.1 us (46%)
  Pallas kernels  17.2 us (35%)
  waiting for transfers between devices  7.05 us (15%)
  local copies, waits for them, and re-layouts  0.97 us (2%)
  between operations  0.95 us (2%)
    ppermute x14, starting transfers between devices, send(): return lax.ppermute(value, axis, pairs)  22.1 us
    pallas_call x1, Pallas kernels, local_in_planes(): pl.pallas_call(early_kernel, grid_spec=pltpu.PrefetchScalarGridSpec(num_s...  8.38 us
    ppermute x14, waiting for transfers between devices, send(): return lax.ppermute(value, axis, pairs)  7.05 us
    pallas_call x1, Pallas kernels, local_in_planes(): pl.pallas_call(prepare_kernel, out_shape=(piece(2 * span + NOTES), piece(...  2.65 us
    pallas_call x1, Pallas kernels, local_in_planes(): pl.pallas_call(far_kept_kernel, out_shape=cache_shape, in_specs=[vmem] *...  1.54 us
    pallas_call x1, Pallas kernels, local_in_planes(): pl.pallas_call(late_kernel, grid_spec=pltpu.PrefetchScalarGridSpec(num_sc...  1.39 us
    pallas_call x1, Pallas kernels, local_in_planes(): pl.pallas_call(far_index_kernel, out_shape=slots_shape, in_specs=[vmem] *...  1.24 us
    pallas_call x1, Pallas kernels, local_in_planes(): pl.pallas_call(last_kernel, out_shape=cache_shape, in_specs=[anywhere, hb...  0.98 us
  transfers between devices with their start and end apart: 14, of which 5 were waited for; matrix products, arithmetic and copies ran while one was open for 0% of the time, Pallas kernels for 27%

profile of v4, /device:TPU:0, one launch (start us, length us, event | category | flops | bytes accessed | tf_op | source)
XLA Modules:
  0.0 48.2 jit_solution(13393911641863358286)
XLA Ops:
  0.7 2.7 %shard_map.76 = (bf16[272,512]{1,0:T(8,128)(2,1)}, bf16[144,512]{1,0:T(8,128)(2,1)}) custom-call(s32[2]{0:T(128)} %offsets_ref.5, bf16[2,128,512]{2,1,0:T(8,128)(2,1)} %kv_ref.1, s32[2,1,2,512]{3,2,1,0:T(2,128)} %keep_ref.1, s32[1,1024]{1,0:T(1,128)} %bitcast.1), custom_call_target="tpu_custom_call" | custom-call | flops 1000000000 | bytes 1 | tf_op jit(solution)/shard_map/pallas_call | solution.py:745
  3.3 3.0 %collective-permute-start.2 = (bf16[272,512]{1,0:T(8,128)(2,1)}, bf16[272,512]{1,0:T(8,128)(2,1)S(1)}, u32[]{:S(2)}, u32[]{:S(2)}) collective-permute-start(bf16[272,512]{1,0:T(8,128)(2,1)} %get-tuple-element.18.both.both_ref.rest_0_), channel_id=1, source_target_pairs={{0,4},{4,0},{8,12},{12,8},{16,20},{20,16},{24,28},{28,24},{1,5},{5... | collective-permute-start | bytes 835592 | tf_op jit(solution)/shard_map/ppermute | solution.py:706
  6.3 1.6 %collective-permute-start = (bf16[272,512]{1,0:T(8,128)(2,1)}, bf16[272,512]{1,0:T(8,128)(2,1)S(1)}, u32[]{:S(2)}, u32[]{:S(2)}) collective-permute-start(bf16[272,512]{1,0:T(8,128)(2,1)} %get-tuple-element.18.both.both_ref.rest_0_), channel_id=1, source_target_pairs={{0,8},{4,12},{8,16},{12,20},{16,24},{20,28},{24,0},{28,4},{1,9},{5... | collective-permute-start | bytes 835592 | tf_op jit(solution)/shard_map/ppermute | solution.py:706
  7.9 1.5 %collective-permute-start.3 = (bf16[144,512]{1,0:T(8,128)(2,1)}, bf16[144,512]{1,0:T(8,128)(2,1)S(1)}, u32[]{:S(2)}, u32[]{:S(2)}) collective-permute-start(bf16[144,512]{1,0:T(8,128)(2,1)} %get-tuple-element.19), channel_id=1, source_target_pairs={{0,2},{1,3},{2,0},{3,1},{4,6},{5,7},{6,4},{7,5},{8,10},{9,11},{10,... | collective-permute-start | bytes 442376 | tf_op jit(solution)/shard_map/ppermute | solution.py:706
  9.4 0.5 collective-permute-start.4
  9.9 2.0 %collective-permute-start.1 = (bf16[144,512]{1,0:T(8,128)(2,1)}, bf16[144,512]{1,0:T(8,128)(2,1)S(1)}, u32[]{:S(2)}, u32[]{:S(2)}) collective-permute-start(bf16[144,512]{1,0:T(8,128)(2,1)} %get-tuple-element.19), channel_id=1, source_target_pairs={{0,24},{4,28},{8,0},{12,4},{16,8},{20,12},{24,16},{28,20},{1,25},{... | collective-permute-start | bytes 442376 | tf_op jit(solution)/shard_map/ppermute | solution.py:706
  11.9 2.8 %collective-permute-done.3.x_own.refs_0_ = bf16[144,512]{1,0:T(8,128)(2,1)S(1)} collective-permute-done((bf16[144,512]{1,0:T(8,128)(2,1)}, bf16[144,512]{1,0:T(8,128)(2,1)S(1)}, u32[]{:S(2)}, u32[]{:S(2)}) %collective-permute-start.3) | collective-permute-done | bytes 147488 | tf_op jit(solution)/shard_map/ppermute | solution.py:706
  14.7 1.6 %collective-permute-done.4.d_own.refs_3_ = bf16[144,512]{1,0:T(8,128)(2,1)S(1)} collective-permute-done((bf16[144,512]{1,0:T(8,128)(2,1)}, bf16[144,512]{1,0:T(8,128)(2,1)S(1)}, u32[]{:S(2)}, u32[]{:S(2)}) %collective-permute-start.4) | collective-permute-done | bytes 147488 | tf_op jit(solution)/shard_map/ppermute | solution.py:706
  16.4 0.0 collective-permute-done.2.y_own.beside_ref.rest_3_
  16.4 1.0 %copy-done = bf16[272,512]{1,0:T(8,128)(2,1)S(1)} copy-done((bf16[272,512]{1,0:T(8,128)(2,1)S(1)}, bf16[272,512]{1,0:T(8,128)(2,1)}, u32[]{:S(2)}) %copy-start) | copy-done | bytes 278552
  17.4 2.9 %collective-permute-start.5 = (bf16[288,512]{1,0:T(8,128)(2,1)S(1)}, bf16[288,512]{1,0:T(8,128)(2,1)S(1)}, u32[]{:S(2)}, u32[]{:S(2)}) collective-permute-start(bf16[288,512]{1,0:T(8,128)(2,1)S(1)} %shard_map.77._), channel_id=1, source_target_pairs={{0,16},{4,20},{8,24},{12,28},{16,0},{20,4},{24,8},{28,12},{1,17},{... | collective-permute-start | bytes 884744 | tf_op jit(solution)/shard_map/ppermute | solution.py:706
  20.2 0.0 collective-permute-done.1.above
  20.3 1.6 %collective-permute-start.8 = (bf16[272,512]{1,0:T(8,128)(2,1)S(1)}, bf16[272,512]{1,0:T(8,128)(2,1)S(1)}, u32[]{:S(2)}, u32[]{:S(2)}) collective-permute-start(bf16[272,512]{1,0:T(8,128)(2,1)S(1)} %get-tuple-element.20.rest_1_), channel_id=1, source_target_pairs={{0,2},{1,3},{2,0},{3,1},{4,6},{5,7},{6,4},{7,5},{8,10},{9,11},{10,... | collective-permute-start | bytes 835592 | tf_op jit(solution)/shard_map/ppermute | solution.py:706
  21.8 1.5 %collective-permute-start.6 = (bf16[272,512]{1,0:T(8,128)(2,1)S(1)}, bf16[272,512]{1,0:T(8,128)(2,1)S(1)}, u32[]{:S(2)}, u32[]{:S(2)}) collective-permute-start(bf16[272,512]{1,0:T(8,128)(2,1)S(1)} %get-tuple-element.20.rest_1_), channel_id=1, source_target_pairs={{0,4},{4,0},{8,12},{12,8},{16,20},{20,16},{24,28},{28,24},{1,5},{5... | collective-permute-start | bytes 835592 | tf_op jit(solution)/shard_map/ppermute | solution.py:706
  23.4 3.5 %collective-permute-start.7 = (bf16[128,512]{1,0:T(8,128)(2,1)S(1)}, bf16[128,512]{1,0:T(8,128)(2,1)S(1)}, u32[]{:S(2)}, u32[]{:S(2)}) collective-permute-start(bf16[128,512]{1,0:T(8,128)(2,1)S(1)} %get-tuple-element.21.relay), channel_id=1, source_target_pairs={{0,8},{4,12},{24,16},{28,20},{1,9},{5,13},{25,17},{29,21},{2,10},{... | collective-permute-start | bytes 393224 | tf_op jit(solution)/shard_map/ppermute | solution.py:706
  26.9 1.4 %shard_map.79 = (bf16[2,128,2048]{2,1,0:T(8,128)(2,1)}, f32[2,2,640]{2,1,0:T(2,128)}, f32[8,128]{1,0:T(8,128)S(1)}) custom-call(s32[2]{0:T(128)S(1)} %copy-done.3, bf16[2,128,2048]{2,1,0:T(8,128)(2,1)S(1)} %copy-done.2, bf16[272,512]{1,0:T(8,128)(2,1)S(1)} %copy-done.1, bf16[272,512]{1,0:T(8,128)(2,1)S(1)} %collective-permute-done.2.y_own.beside_ref.rest_3_), custom_call_target="tpu_custom_call" | custom-call | flops 1000000 | bytes 1 | tf_op jit(solution)/shard_map/pallas_call | solution.py:795
  28.3 1.1 %collective-permute-done.7.relayed = bf16[128,512]{1,0:T(8,128)(2,1)S(1)} collective-permute-done((bf16[128,512]{1,0:T(8,128)(2,1)S(1)}, bf16[128,512]{1,0:T(8,128)(2,1)S(1)}, u32[]{:S(2)}, u32[]{:S(2)}) %collective-permute-start.7) | collective-permute-done | bytes 131104 | tf_op jit(solution)/shard_map/ppermute | solution.py:706
  29.3 0.2 shard_map.80.rest_5_.late.refs_6_
  29.5 0.5 %collective-permute-start.11 = (bf16[128,512]{1,0:T(8,128)(2,1)S(1)}, bf16[128,512]{1,0:T(8,128)(2,1)S(1)}, u32[]{:S(2)}, u32[]{:S(2)}) collective-permute-start(bf16[128,512]{1,0:T(8,128)(2,1)S(1)} %shard_map.80.rest_5_.late.refs_6_), channel_id=1, source_target_pairs={{0,6},{1,7},{2,4},{3,5},{4,2},{5,3},{6,0},{7,1},{8,14},{9,15},{10,... | collective-permute-start | bytes 393224 | tf_op jit(solution)/shard_map/ppermute | solution.py:706
  30.1 1.5 %collective-permute-start.12 = (bf16[128,512]{1,0:T(8,128)(2,1)S(1)}, bf16[128,512]{1,0:T(8,128)(2,1)S(1)}, u32[]{:S(2)}, u32[]{:S(2)}) collective-permute-start(bf16[128,512]{1,0:T(8,128)(2,1)S(1)} %shard_map.80.rest_5_.late.refs_6_), channel_id=1, source_target_pairs={{0,4},{4,0},{8,12},{12,8},{16,20},{20,16},{24,28},{28,24},{1,5},{5... | collective-permute-start | bytes 393224 | tf_op jit(solution)/shard_map/ppermute | solution.py:706
  31.6 0.0 collective-permute-done.8.rest_1_.x_beside.refs_1_
  31.6 0.5 %collective-permute-start.10 = (bf16[272,512]{1,0:T(8,128)(2,1)S(1)}, bf16[272,512]{1,0:T(8,128)(2,1)S(1)}, u32[]{:S(2)}, u32[]{:S(2)}) collective-permute-start(bf16[272,512]{1,0:T(8,128)(2,1)S(1)} %collective-permute-done.8.rest_1_.x_beside.refs_1_), channel_id=1, source_target_pairs={{0,4},{4,0},{8,12},{12,8},{16,20},{20,16},{24,28},{28,24},{1,5},{5... | collective-permute-start | bytes 835592 | tf_op jit(solution)/shard_map/ppermute | solution.py:706
  32.1 0.0 collective-permute-done.6.rest_4_.rest_0_
  32.1 0.4 collective-permute-done.5.rest_2_.beyond
  32.5 1.4 %collective-permute-start.9 = (bf16[384,512]{1,0:T(8,128)(2,1)S(1)}, bf16[384,512]{1,0:T(8,128)(2,1)S(1)}, u32[]{:S(2)}, u32[]{:S(2)}) collective-permute-start(bf16[384,512]{1,0:T(8,128)(2,1)S(1)} %shard_map.82), channel_id=1, source_target_pairs={{0,2},{1,3},{2,0},{3,1},{4,6},{5,7},{6,4},{7,5},{8,10},{9,11},{10,... | collective-permute-start | bytes 1179656 | tf_op jit(solution)/shard_map/ppermute | solution.py:706
  34.0 8.4 %shard_map.81 = (bf16[2,128,2048]{2,1,0:T(8,128)(2,1)}, f32[2,2,640]{2,1,0:T(2,128)}, f32[8,128]{1,0:T(8,128)S(1)}, bf16[512,2048]{1,0:T(8,128)(2,1)}, bf16[384,...) custom-call(s32[2]{0:T(128)S(1)} %copy-done.3, ...), custom_call_target="tpu_custom_call", output_to_operand_aliasing={{0}: (8, {}), {1}: (9, {})} | custom-call | flops 10000000000 | bytes 10000000 | tf_op jit(solution)/shard_map/pallas_call | solution.py:837
  42.3 1.2 %shard_map.83.refs_10_ = s32[2,512,2]{2,1,0:T(8,128)S(1)} custom-call(bf16[144,512]{1,0:T(8,128)(2,1)S(1)} %collective-permute-done.3.x_own.refs_0_, bf16[272,512]{1,0:T(8,128)(2,1)S(1)} %collective-permute-done.8.rest_1_.x_beside.refs_1_, bf16[144,512]{1,0:T(8,128)(2,1)S(1)} %collective-permute-done.4.d_own.refs_3_, ...), custom_call_target="tpu_custom_call" | custom-call | flops 1000000 | bytes 1 | tf_op jit(solution)/shard_map/pallas_call | solution.py:865
  43.6 0.7 %shard_map.84 = bf16[1024,512]{1,0:T(8,128)(2,1)S(1)} custom-call(bf16[144,512]{1,0:T(8,128)(2,1)S(1)} %collective-permute-done.3.x_own.refs_0_, bf16[272,512]{1,0:T(8,128)(2,1)S(1)} %collective-permute-done.8.rest_1_.x_beside.refs_1_, bf16[384,512]{1,0:T(8,128)(2,1)S(1)} %collective-permute-done.9.refs_2_, ...), custom_call_target="tpu_custom_call" | custom-call | flops 2000000000 | bytes 4000000 | tf_op jit(solution)/shard_map/pallas_call | solution.py:876
  44.4 0.1 collective-permute-start.13
  44.4 1.5 %shard_map.85._ = bf16[512,2048]{1,0:T(8,128)(2,1)} custom-call(bf16[144,512]{1,0:T(8,128)(2,1)S(1)} %collective-permute-done.3.x_own.refs_0_, bf16[272,512]{1,0:T(8,128)(2,1)S(1)} %collective-permute-done.8.rest_1_.x_beside.refs_1_, bf16[384,512]{1,0:T(8,128)(2,1)S(1)} %collective-permute-done.9.refs_2_, ...), custom_call_target="tpu_custom_call", output_to_operand_aliasing={{}: (11, {})} | custom-call | flops 2000000000 | bytes 4000000 | tf_op jit(solution)/shard_map/pallas_call | solution.py:886
  46.0 1.1 %collective-permute-done.13.sent_ref = bf16[1024,512]{1,0:T(8,128)(2,1)S(1)} collective-permute-done((bf16[1024,512]{1,0:T(8,128)(2,1)S(1)}, bf16[1024,512]{1,0:T(8,128)(2,1)S(1)}, u32[]{:S(2)}, u32[]{:S(2)}) %collective-permute-start.13) | collective-permute-done | bytes 1048608 | tf_op jit(solution)/shard_map/ppermute | solution.py:706
  47.1 1.0 %shard_map.86 = bf16[512,2048]{1,0:T(8,128)(2,1)} custom-call(bf16[1024,512]{1,0:T(8,128)(2,1)S(1)} %collective-permute-done.13.sent_ref, bf16[512,2048]{1,0:T(8,128)(2,1)} %shard_map.85._), custom_call_target="tpu_custom_call", output_to_operand_aliasing={{}: (1, {})} | custom-call | bytes 1000000 | tf_op jit(solution)/shard_map/pallas_call | solution.py:903
  (15 shorter events, 0.1 us)
Async XLA Ops:
  0.6 26.2 %copy-start.2 = (bf16[2,128,2048]{2,1,0:T(8,128)(2,1)S(1)}, bf16[2,128,2048]{2,1,0:T(8,128)(2,1)}, u32[]{:S(2)}) copy-start(bf16[2,128,2048]{2,1,0:T(8,128)(2,1)} %q_ref.3) | copy-start | bytes 3145732
  0.6 26.2 %copy-start.3 = (s32[2]{0:T(128)S(1)}, s32[2]{0:T(128)}, u32[]{:S(2)}) copy-start(s32[2]{0:T(128)} %offsets_ref.5) | copy-start | bytes 28
  3.3 13.1 %collective-permute-start.2 = (bf16[272,512]{1,0:T(8,128)(2,1)}, bf16[272,512]{1,0:T(8,128)(2,1)S(1)}, u32[]{:S(2)}, u32[]{:S(2)}) collective-permute-start(bf16[272,512]{1,0:T(8,128)(2,1)} %get-tuple-element.18.both.both_ref.rest_0_), channel_id=1, source_target_pairs={{0,4},{4,0},{8,12},{12,8},{16,20},{20,16},{24,28},{28,24},{1,5},{5... | collective-permute-start | bytes 835592 | tf_op jit(solution)/shard_map/ppermute | solution.py:706
  6.3 13.9 %collective-permute-start = (bf16[272,512]{1,0:T(8,128)(2,1)}, bf16[272,512]{1,0:T(8,128)(2,1)S(1)}, u32[]{:S(2)}, u32[]{:S(2)}) collective-permute-start(bf16[272,512]{1,0:T(8,128)(2,1)} %get-tuple-element.18.both.both_ref.rest_0_), channel_id=1, source_target_pairs={{0,8},{4,12},{8,16},{12,20},{16,24},{20,28},{24,0},{28,4},{1,9},{5... | collective-permute-start | bytes 835592 | tf_op jit(solution)/shard_map/ppermute | solution.py:706
  7.9 6.8 %collective-permute-start.3 = (bf16[144,512]{1,0:T(8,128)(2,1)}, bf16[144,512]{1,0:T(8,128)(2,1)S(1)}, u32[]{:S(2)}, u32[]{:S(2)}) collective-permute-start(bf16[144,512]{1,0:T(8,128)(2,1)} %get-tuple-element.19), channel_id=1, source_target_pairs={{0,2},{1,3},{2,0},{3,1},{4,6},{5,7},{6,4},{7,5},{8,10},{9,11},{10,... | collective-permute-start | bytes 442376 | tf_op jit(solution)/shard_map/ppermute | solution.py:706
  9.4 7.0 %collective-permute-start.4 = (bf16[144,512]{1,0:T(8,128)(2,1)}, bf16[144,512]{1,0:T(8,128)(2,1)S(1)}, u32[]{:S(2)}, u32[]{:S(2)}) collective-permute-start(bf16[144,512]{1,0:T(8,128)(2,1)} %get-tuple-element.19), channel_id=1, source_target_pairs={{0,6},{1,7},{2,4},{3,5},{4,2},{5,3},{6,0},{7,1},{8,14},{9,15},{10,... | collective-permute-start | bytes 442376 | tf_op jit(solution)/shard_map/ppermute | solution.py:706
  9.9 10.3 %collective-permute-start.1 = (bf16[144,512]{1,0:T(8,128)(2,1)}, bf16[144,512]{1,0:T(8,128)(2,1)S(1)}, u32[]{:S(2)}, u32[]{:S(2)}) collective-permute-start(bf16[144,512]{1,0:T(8,128)(2,1)} %get-tuple-element.19), channel_id=1, source_target_pairs={{0,24},{4,28},{8,0},{12,4},{16,8},{20,12},{24,16},{28,20},{1,25},{... | collective-permute-start | bytes 442376 | tf_op jit(solution)/shard_map/ppermute | solution.py:706
  16.4 1.0 %copy-start = (bf16[272,512]{1,0:T(8,128)(2,1)S(1)}, bf16[272,512]{1,0:T(8,128)(2,1)}, u32[]{:S(2)}) copy-start(bf16[272,512]{1,0:T(8,128)(2,1)} %get-tuple-element.18.both.both_ref.rest_0_) | copy-start | bytes 835588
  17.3 9.5 %copy-start.1 = (bf16[272,512]{1,0:T(8,128)(2,1)S(1)}, bf16[272,512]{1,0:T(8,128)(2,1)}, u32[]{:S(2)}) copy-start(bf16[272,512]{1,0:T(8,128)(2,1)} %get-tuple-element.18.both.both_ref.rest_0_) | copy-start | bytes 835588
  17.4 15.1 %collective-permute-start.5 = (bf16[288,512]{1,0:T(8,128)(2,1)S(1)}, bf16[288,512]{1,0:T(8,128)(2,1)S(1)}, u32[]{:S(2)}, u32[]{:S(2)}) collective-permute-start(bf16[288,512]{1,0:T(8,128)(2,1)S(1)} %shard_map.77._), channel_id=1, source_target_pairs={{0,16},{4,20},{8,24},{12,28},{16,0},{20,4},{24,8},{28,12},{1,17},{... | collective-permute-start | bytes 884744 | tf_op jit(solution)/shard_map/ppermute | solution.py:706
  20.3 11.3 %collective-permute-start.8 = (bf16[272,512]{1,0:T(8,128)(2,1)S(1)}, bf16[272,512]{1,0:T(8,128)(2,1)S(1)}, u32[]{:S(2)}, u32[]{:S(2)}) collective-permute-start(bf16[272,512]{1,0:T(8,128)(2,1)S(1)} %get-tuple-element.20.rest_1_), channel_id=1, source_target_pairs={{0,2},{1,3},{2,0},{3,1},{4,6},{5,7},{6,4},{7,5},{8,10},{9,11},{10,... | collective-permute-start | bytes 835592 | tf_op jit(solution)/shard_map/ppermute | solution.py:706
  21.8 10.3 %collective-permute-start.6 = (bf16[272,512]{1,0:T(8,128)(2,1)S(1)}, bf16[272,512]{1,0:T(8,128)(2,1)S(1)}, u32[]{:S(2)}, u32[]{:S(2)}) collective-permute-start(bf16[272,512]{1,0:T(8,128)(2,1)S(1)} %get-tuple-element.20.rest_1_), channel_id=1, source_target_pairs={{0,4},{4,0},{8,12},{12,8},{16,20},{20,16},{24,28},{28,24},{1,5},{5... | collective-permute-start | bytes 835592 | tf_op jit(solution)/shard_map/ppermute | solution.py:706
  23.4 6.0 %collective-permute-start.7 = (bf16[128,512]{1,0:T(8,128)(2,1)S(1)}, bf16[128,512]{1,0:T(8,128)(2,1)S(1)}, u32[]{:S(2)}, u32[]{:S(2)}) collective-permute-start(bf16[128,512]{1,0:T(8,128)(2,1)S(1)} %get-tuple-element.21.relay), channel_id=1, source_target_pairs={{0,8},{4,12},{24,16},{28,20},{1,9},{5,13},{25,17},{29,21},{2,10},{... | collective-permute-start | bytes 393224 | tf_op jit(solution)/shard_map/ppermute | solution.py:706
  29.5 14.1 %collective-permute-start.11 = (bf16[128,512]{1,0:T(8,128)(2,1)S(1)}, bf16[128,512]{1,0:T(8,128)(2,1)S(1)}, u32[]{:S(2)}, u32[]{:S(2)}) collective-permute-start(bf16[128,512]{1,0:T(8,128)(2,1)S(1)} %shard_map.80.rest_5_.late.refs_6_), channel_id=1, source_target_pairs={{0,6},{1,7},{2,4},{3,5},{4,2},{5,3},{6,0},{7,1},{8,14},{9,15},{10,... | collective-permute-start | bytes 393224 | tf_op jit(solution)/shard_map/ppermute | solution.py:706
  30.1 13.5 %collective-permute-start.12 = (bf16[128,512]{1,0:T(8,128)(2,1)S(1)}, bf16[128,512]{1,0:T(8,128)(2,1)S(1)}, u32[]{:S(2)}, u32[]{:S(2)}) collective-permute-start(bf16[128,512]{1,0:T(8,128)(2,1)S(1)} %shard_map.80.rest_5_.late.refs_6_), channel_id=1, source_target_pairs={{0,4},{4,0},{8,12},{12,8},{16,20},{20,16},{24,28},{28,24},{1,5},{5... | collective-permute-start | bytes 393224 | tf_op jit(solution)/shard_map/ppermute | solution.py:706
  31.6 10.7 %collective-permute-start.10 = (bf16[272,512]{1,0:T(8,128)(2,1)S(1)}, bf16[272,512]{1,0:T(8,128)(2,1)S(1)}, u32[]{:S(2)}, u32[]{:S(2)}) collective-permute-start(bf16[272,512]{1,0:T(8,128)(2,1)S(1)} %collective-permute-done.8.rest_1_.x_beside.refs_1_), channel_id=1, source_target_pairs={{0,4},{4,0},{8,12},{12,8},{16,20},{20,16},{24,28},{28,24},{1,5},{5... | collective-permute-start | bytes 835592 | tf_op jit(solution)/shard_map/ppermute | solution.py:706
  32.5 11.1 %collective-permute-start.9 = (bf16[384,512]{1,0:T(8,128)(2,1)S(1)}, bf16[384,512]{1,0:T(8,128)(2,1)S(1)}, u32[]{:S(2)}, u32[]{:S(2)}) collective-permute-start(bf16[384,512]{1,0:T(8,128)(2,1)S(1)} %shard_map.82), channel_id=1, source_target_pairs={{0,2},{1,3},{2,0},{3,1},{4,6},{5,7},{6,4},{7,5},{8,10},{9,11},{10,... | collective-permute-start | bytes 1179656 | tf_op jit(solution)/shard_map/ppermute | solution.py:706
  44.4 2.7 %collective-permute-start.13 = (bf16[1024,512]{1,0:T(8,128)(2,1)S(1)}, bf16[1024,512]{1,0:T(8,128)(2,1)S(1)}, u32[]{:S(2)}, u32[]{:S(2)}) collective-permute-start(bf16[1024,512]{1,0:T(8,128)(2,1)S(1)} %shard_map.84), channel_id=1, source_target_pairs={{0,1},{1,0},{2,3},{3,2},{4,5},{5,4},{6,7},{7,6},{8,9},{9,8},{10,11... | collective-permute-start | bytes 3145736 | tf_op jit(solution)/shard_map/ppermute | solution.py:706

commit v5 on v4

--- a/solution.py
+++ b/solution.py
@@ -536,10 +536,9 @@
             axis=0,
         )
         scores = dot(keys, jnp.concatenate([query, ones], axis=1), ((1,), (1,)))
-        near = scores[cache:] + bias
-        scores = jnp.concatenate([scores[:cache], near], axis=0) * scale
+        scores = jnp.concatenate([scores[:cache], scores[cache:] + bias], axis=0)
         peak = jnp.max(scores, axis=0, keepdims=True)
-        expo = jnp.exp2(scores - peak)
+        expo = jnp.exp2((scores - peak) * scale)
         weights = expo * (1.0 / jnp.sum(expo, axis=0, keepdims=True))
         both = weights[:, :span] + weights[:, span:]
         mass = both if mass is None else mass + both

time: 48.5 us -> 48.4 us (level)
  no operation moved by 1% of the time
where the time goes in v5:
time: 48.4 us; the launch traced here: 48.2 us
  starting transfers between devices  22.1 us (46%)
  Pallas kernels  17.1 us (35%)
  waiting for transfers between devices  7.05 us (15%)
  local copies, waits for them, and re-layouts  0.97 us (2%)
  between operations  0.95 us (2%)
    ppermute x14, starting transfers between devices, send(): return lax.ppermute(value, axis, pairs)  22.1 us
    pallas_call x1, Pallas kernels, local_in_planes(): pl.pallas_call(early_kernel, grid_spec=pltpu.PrefetchScalarGridSpec(num_s...  8.34 us
    ppermute x14, waiting for transfers between devices, send(): return lax.ppermute(value, axis, pairs)  7.05 us
    pallas_call x1, Pallas kernels, local_in_planes(): pl.pallas_call(prepare_kernel, out_shape=(piece(2 * span + NOTES), piece(...  2.65 us
    pallas_call x1, Pallas kernels, local_in_planes(): pl.pallas_call(far_kept_kernel, out_shape=cache_shape, in_specs=[vmem] *...  1.54 us
    pallas_call x1, Pallas kernels, local_in_planes(): pl.pallas_call(late_kernel, grid_spec=pltpu.PrefetchScalarGridSpec(num_sc...  1.39 us
    pallas_call x1, Pallas kernels, local_in_planes(): pl.pallas_call(far_index_kernel, out_shape=slots_shape, in_specs=[vmem] *...  1.24 us
    pallas_call x1, Pallas kernels, local_in_planes(): pl.pallas_call(last_kernel, out_shape=cache_shape, in_specs=[anywhere, hb...  0.98 us
  transfers between devices with their start and end apart: 14, of which 5 were waited for; matrix products, arithmetic and copies ran while one was open for 0% of the time, Pallas kernels for 27%

profile of v5, /device:TPU:0, one launch (start us, length us, event | category | flops | bytes accessed | tf_op | source)
XLA Modules:
  0.0 48.2 jit_solution(18352645256872574282)
XLA Ops:
  0.7 2.7 %shard_map.76 = (bf16[272,512]{1,0:T(8,128)(2,1)}, bf16[144,512]{1,0:T(8,128)(2,1)}) custom-call(s32[2]{0:T(128)} %offsets_ref.5, bf16[2,128,512]{2,1,0:T(8,128)(2,1)} %kv_ref.1, s32[2,1,2,512]{3,2,1,0:T(2,128)} %keep_ref.1, s32[1,1024]{1,0:T(1,128)} %bitcast.1), custom_call_target="tpu_custom_call" | custom-call | flops 1000000000 | bytes 1 | tf_op jit(solution)/shard_map/pallas_call | solution.py:744
  3.3 3.0 %collective-permute-start.2 = (bf16[272,512]{1,0:T(8,128)(2,1)}, bf16[272,512]{1,0:T(8,128)(2,1)S(1)}, u32[]{:S(2)}, u32[]{:S(2)}) collective-permute-start(bf16[272,512]{1,0:T(8,128)(2,1)} %get-tuple-element.18.both.both_ref.rest_0_), channel_id=1, source_target_pairs={{0,4},{4,0},{8,12},{12,8},{16,20},{20,16},{24,28},{28,24},{1,5},{5... | collective-permute-start | bytes 835592 | tf_op jit(solution)/shard_map/ppermute | solution.py:705
  6.3 1.6 %collective-permute-start = (bf16[272,512]{1,0:T(8,128)(2,1)}, bf16[272,512]{1,0:T(8,128)(2,1)S(1)}, u32[]{:S(2)}, u32[]{:S(2)}) collective-permute-start(bf16[272,512]{1,0:T(8,128)(2,1)} %get-tuple-element.18.both.both_ref.rest_0_), channel_id=1, source_target_pairs={{0,8},{4,12},{8,16},{12,20},{16,24},{20,28},{24,0},{28,4},{1,9},{5... | collective-permute-start | bytes 835592 | tf_op jit(solution)/shard_map/ppermute | solution.py:705
  7.9 1.5 %collective-permute-start.3 = (bf16[144,512]{1,0:T(8,128)(2,1)}, bf16[144,512]{1,0:T(8,128)(2,1)S(1)}, u32[]{:S(2)}, u32[]{:S(2)}) collective-permute-start(bf16[144,512]{1,0:T(8,128)(2,1)} %get-tuple-element.19), channel_id=1, source_target_pairs={{0,2},{1,3},{2,0},{3,1},{4,6},{5,7},{6,4},{7,5},{8,10},{9,11},{10,... | collective-permute-start | bytes 442376 | tf_op jit(solution)/shard_map/ppermute | solution.py:705
  9.4 0.5 collective-permute-start.4
  9.9 2.0 %collective-permute-start.1 = (bf16[144,512]{1,0:T(8,128)(2,1)}, bf16[144,512]{1,0:T(8,128)(2,1)S(1)}, u32[]{:S(2)}, u32[]{:S(2)}) collective-permute-start(bf16[144,512]{1,0:T(8,128)(2,1)} %get-tuple-element.19), channel_id=1, source_target_pairs={{0,24},{4,28},{8,0},{12,4},{16,8},{20,12},{24,16},{28,20},{1,25},{... | collective-permute-start | bytes 442376 | tf_op jit(solution)/shard_map/ppermute | solution.py:705
  11.9 2.8 %collective-permute-done.3.x_own.refs_0_ = bf16[144,512]{1,0:T(8,128)(2,1)S(1)} collective-permute-done((bf16[144,512]{1,0:T(8,128)(2,1)}, bf16[144,512]{1,0:T(8,128)(2,1)S(1)}, u32[]{:S(2)}, u32[]{:S(2)}) %collective-permute-start.3) | collective-permute-done | bytes 147488 | tf_op jit(solution)/shard_map/ppermute | solution.py:705
  14.7 1.6 %collective-permute-done.4.d_own.refs_3_ = bf16[144,512]{1,0:T(8,128)(2,1)S(1)} collective-permute-done((bf16[144,512]{1,0:T(8,128)(2,1)}, bf16[144,512]{1,0:T(8,128)(2,1)S(1)}, u32[]{:S(2)}, u32[]{:S(2)}) %collective-permute-start.4) | collective-permute-done | bytes 147488 | tf_op jit(solution)/shard_map/ppermute | solution.py:705
  16.4 1.0 %copy-done = bf16[272,512]{1,0:T(8,128)(2,1)S(1)} copy-done((bf16[272,512]{1,0:T(8,128)(2,1)S(1)}, bf16[272,512]{1,0:T(8,128)(2,1)}, u32[]{:S(2)}) %copy-start) | copy-done | bytes 278552
  17.4 2.9 %collective-permute-start.5 = (bf16[288,512]{1,0:T(8,128)(2,1)S(1)}, bf16[288,512]{1,0:T(8,128)(2,1)S(1)}, u32[]{:S(2)}, u32[]{:S(2)}) collective-permute-start(bf16[288,512]{1,0:T(8,128)(2,1)S(1)} %shard_map.77._), channel_id=1, source_target_pairs={{0,16},{4,20},{8,24},{12,28},{16,0},{20,4},{24,8},{28,12},{1,17},{... | collective-permute-start | bytes 884744 | tf_op jit(solution)/shard_map/ppermute | solution.py:705
  20.2 0.0 collective-permute-done.1.above
  20.2 0.0 collective-permute-done.below
  20.3 1.6 %collective-permute-start.8 = (bf16[272,512]{1,0:T(8,128)(2,1)S(1)}, bf16[272,512]{1,0:T(8,128)(2,1)S(1)}, u32[]{:S(2)}, u32[]{:S(2)}) collective-permute-start(bf16[272,512]{1,0:T(8,128)(2,1)S(1)} %get-tuple-element.20.rest_1_), channel_id=1, source_target_pairs={{0,2},{1,3},{2,0},{3,1},{4,6},{5,7},{6,4},{7,5},{8,10},{9,11},{10,... | collective-permute-start | bytes 835592 | tf_op jit(solution)/shard_map/ppermute | solution.py:705
  21.8 1.5 %collective-permute-start.6 = (bf16[272,512]{1,0:T(8,128)(2,1)S(1)}, bf16[272,512]{1,0:T(8,128)(2,1)S(1)}, u32[]{:S(2)}, u32[]{:S(2)}) collective-permute-start(bf16[272,512]{1,0:T(8,128)(2,1)S(1)} %get-tuple-element.20.rest_1_), channel_id=1, source_target_pairs={{0,4},{4,0},{8,12},{12,8},{16,20},{20,16},{24,28},{28,24},{1,5},{5... | collective-permute-start | bytes 835592 | tf_op jit(solution)/shard_map/ppermute | solution.py:705
  23.4 3.5 %collective-permute-start.7 = (bf16[128,512]{1,0:T(8,128)(2,1)S(1)}, bf16[128,512]{1,0:T(8,128)(2,1)S(1)}, u32[]{:S(2)}, u32[]{:S(2)}) collective-permute-start(bf16[128,512]{1,0:T(8,128)(2,1)S(1)} %get-tuple-element.21.relay), channel_id=1, source_target_pairs={{0,8},{4,12},{24,16},{28,20},{1,9},{5,13},{25,17},{29,21},{2,10},{... | collective-permute-start | bytes 393224 | tf_op jit(solution)/shard_map/ppermute | solution.py:705
  26.9 1.4 %shard_map.79 = (bf16[2,128,2048]{2,1,0:T(8,128)(2,1)}, f32[2,2,640]{2,1,0:T(2,128)}, f32[8,128]{1,0:T(8,128)S(1)}) custom-call(s32[2]{0:T(128)S(1)} %copy-done.3, bf16[2,128,2048]{2,1,0:T(8,128)(2,1)S(1)} %copy-done.2, bf16[272,512]{1,0:T(8,128)(2,1)S(1)} %copy-done.1, bf16[272,512]{1,0:T(8,128)(2,1)S(1)} %collective-permute-done.2.y_own.beside_ref.rest_3_), custom_call_target="tpu_custom_call" | custom-call | flops 1000000 | bytes 1 | tf_op jit(solution)/shard_map/pallas_call | solution.py:794
  28.3 1.1 %collective-permute-done.7.relayed = bf16[128,512]{1,0:T(8,128)(2,1)S(1)} collective-permute-done((bf16[128,512]{1,0:T(8,128)(2,1)S(1)}, bf16[128,512]{1,0:T(8,128)(2,1)S(1)}, u32[]{:S(2)}, u32[]{:S(2)}) %collective-permute-start.7) | collective-permute-done | bytes 131104 | tf_op jit(solution)/shard_map/ppermute | solution.py:705
  29.3 0.2 shard_map.80.rest_5_.late.refs_6_
  29.5 0.5 %collective-permute-start.11 = (bf16[128,512]{1,0:T(8,128)(2,1)S(1)}, bf16[128,512]{1,0:T(8,128)(2,1)S(1)}, u32[]{:S(2)}, u32[]{:S(2)}) collective-permute-start(bf16[128,512]{1,0:T(8,128)(2,1)S(1)} %shard_map.80.rest_5_.late.refs_6_), channel_id=1, source_target_pairs={{0,6},{1,7},{2,4},{3,5},{4,2},{5,3},{6,0},{7,1},{8,14},{9,15},{10,... | collective-permute-start | bytes 393224 | tf_op jit(solution)/shard_map/ppermute | solution.py:705
  30.1 1.5 %collective-permute-start.12 = (bf16[128,512]{1,0:T(8,128)(2,1)S(1)}, bf16[128,512]{1,0:T(8,128)(2,1)S(1)}, u32[]{:S(2)}, u32[]{:S(2)}) collective-permute-start(bf16[128,512]{1,0:T(8,128)(2,1)S(1)} %shard_map.80.rest_5_.late.refs_6_), channel_id=1, source_target_pairs={{0,4},{4,0},{8,12},{12,8},{16,20},{20,16},{24,28},{28,24},{1,5},{5... | collective-permute-start | bytes 393224 | tf_op jit(solution)/shard_map/ppermute | solution.py:705
  31.6 0.0 collective-permute-done.8.rest_1_.x_beside.refs_1_
  31.6 0.5 %collective-permute-start.10 = (bf16[272,512]{1,0:T(8,128)(2,1)S(1)}, bf16[272,512]{1,0:T(8,128)(2,1)S(1)}, u32[]{:S(2)}, u32[]{:S(2)}) collective-permute-start(bf16[272,512]{1,0:T(8,128)(2,1)S(1)} %collective-permute-done.8.rest_1_.x_beside.refs_1_), channel_id=1, source_target_pairs={{0,4},{4,0},{8,12},{12,8},{16,20},{20,16},{24,28},{28,24},{1,5},{5... | collective-permute-start | bytes 835592 | tf_op jit(solution)/shard_map/ppermute | solution.py:705
  32.1 0.4 collective-permute-done.5.rest_2_.beyond
  32.5 1.4 %collective-permute-start.9 = (bf16[384,512]{1,0:T(8,128)(2,1)S(1)}, bf16[384,512]{1,0:T(8,128)(2,1)S(1)}, u32[]{:S(2)}, u32[]{:S(2)}) collective-permute-start(bf16[384,512]{1,0:T(8,128)(2,1)S(1)} %shard_map.82), channel_id=1, source_target_pairs={{0,2},{1,3},{2,0},{3,1},{4,6},{5,7},{6,4},{7,5},{8,10},{9,11},{10,... | collective-permute-start | bytes 1179656 | tf_op jit(solution)/shard_map/ppermute | solution.py:705
  34.0 8.3 %shard_map.81 = (bf16[2,128,2048]{2,1,0:T(8,128)(2,1)}, f32[2,2,640]{2,1,0:T(2,128)}, f32[8,128]{1,0:T(8,128)S(1)}, bf16[512,2048]{1,0:T(8,128)(2,1)}, bf16[384,...) custom-call(s32[2]{0:T(128)S(1)} %copy-done.3, ...), custom_call_target="tpu_custom_call", output_to_operand_aliasing={{0}: (8, {}), {1}: (9, {})} | custom-call | flops 10000000000 | bytes 10000000 | tf_op jit(solution)/shard_map/pallas_call | solution.py:836
  42.3 0.0 collective-permute-done.10.d_beside.refs_4_
  42.3 1.2 %shard_map.83.refs_10_ = s32[2,512,2]{2,1,0:T(8,128)S(1)} custom-call(bf16[144,512]{1,0:T(8,128)(2,1)S(1)} %collective-permute-done.3.x_own.refs_0_, bf16[272,512]{1,0:T(8,128)(2,1)S(1)} %collective-permute-done.8.rest_1_.x_beside.refs_1_, bf16[144,512]{1,0:T(8,128)(2,1)S(1)} %collective-permute-done.4.d_own.refs_3_, ...), custom_call_target="tpu_custom_call" | custom-call | flops 1000000 | bytes 1 | tf_op jit(solution)/shard_map/pallas_call | solution.py:864
  43.6 0.7 %shard_map.84 = bf16[1024,512]{1,0:T(8,128)(2,1)S(1)} custom-call(bf16[144,512]{1,0:T(8,128)(2,1)S(1)} %collective-permute-done.3.x_own.refs_0_, bf16[272,512]{1,0:T(8,128)(2,1)S(1)} %collective-permute-done.8.rest_1_.x_beside.refs_1_, bf16[384,512]{1,0:T(8,128)(2,1)S(1)} %collective-permute-done.9.refs_2_, ...), custom_call_target="tpu_custom_call" | custom-call | flops 2000000000 | bytes 4000000 | tf_op jit(solution)/shard_map/pallas_call | solution.py:875
  44.3 0.1 collective-permute-start.13
  44.4 1.5 %shard_map.85._ = bf16[512,2048]{1,0:T(8,128)(2,1)} custom-call(bf16[144,512]{1,0:T(8,128)(2,1)S(1)} %collective-permute-done.3.x_own.refs_0_, bf16[272,512]{1,0:T(8,128)(2,1)S(1)} %collective-permute-done.8.rest_1_.x_beside.refs_1_, bf16[384,512]{1,0:T(8,128)(2,1)S(1)} %collective-permute-done.9.refs_2_, ...), custom_call_target="tpu_custom_call", output_to_operand_aliasing={{}: (11, {})} | custom-call | flops 2000000000 | bytes 4000000 | tf_op jit(solution)/shard_map/pallas_call | solution.py:885
  46.0 1.1 %collective-permute-done.13.sent_ref = bf16[1024,512]{1,0:T(8,128)(2,1)S(1)} collective-permute-done((bf16[1024,512]{1,0:T(8,128)(2,1)S(1)}, bf16[1024,512]{1,0:T(8,128)(2,1)S(1)}, u32[]{:S(2)}, u32[]{:S(2)}) %collective-permute-start.13) | collective-permute-done | bytes 1048608 | tf_op jit(solution)/shard_map/ppermute | solution.py:705
  47.1 1.0 %shard_map.86 = bf16[512,2048]{1,0:T(8,128)(2,1)} custom-call(bf16[1024,512]{1,0:T(8,128)(2,1)S(1)} %collective-permute-done.13.sent_ref, bf16[512,2048]{1,0:T(8,128)(2,1)} %shard_map.85._), custom_call_target="tpu_custom_call", output_to_operand_aliasing={{}: (1, {})} | custom-call | bytes 1000000 | tf_op jit(solution)/shard_map/pallas_call | solution.py:902
  (15 shorter events, 0.1 us)
Async XLA Ops:
  0.6 26.2 %copy-start.2 = (bf16[2,128,2048]{2,1,0:T(8,128)(2,1)S(1)}, bf16[2,128,2048]{2,1,0:T(8,128)(2,1)}, u32[]{:S(2)}) copy-start(bf16[2,128,2048]{2,1,0:T(8,128)(2,1)} %q_ref.3) | copy-start | bytes 3145732
  0.6 26.2 %copy-start.3 = (s32[2]{0:T(128)S(1)}, s32[2]{0:T(128)}, u32[]{:S(2)}) copy-start(s32[2]{0:T(128)} %offsets_ref.5) | copy-start | bytes 28
  3.3 13.1 %collective-permute-start.2 = (bf16[272,512]{1,0:T(8,128)(2,1)}, bf16[272,512]{1,0:T(8,128)(2,1)S(1)}, u32[]{:S(2)}, u32[]{:S(2)}) collective-permute-start(bf16[272,512]{1,0:T(8,128)(2,1)} %get-tuple-element.18.both.both_ref.rest_0_), channel_id=1, source_target_pairs={{0,4},{4,0},{8,12},{12,8},{16,20},{20,16},{24,28},{28,24},{1,5},{5... | collective-permute-start | bytes 835592 | tf_op jit(solution)/shard_map/ppermute | solution.py:705
  6.3 13.9 %collective-permute-start = (bf16[272,512]{1,0:T(8,128)(2,1)}, bf16[272,512]{1,0:T(8,128)(2,1)S(1)}, u32[]{:S(2)}, u32[]{:S(2)}) collective-permute-start(bf16[272,512]{1,0:T(8,128)(2,1)} %get-tuple-element.18.both.both_ref.rest_0_), channel_id=1, source_target_pairs={{0,8},{4,12},{8,16},{12,20},{16,24},{20,28},{24,0},{28,4},{1,9},{5... | collective-permute-start | bytes 835592 | tf_op jit(solution)/shard_map/ppermute | solution.py:705
  7.9 6.8 %collective-permute-start.3 = (bf16[144,512]{1,0:T(8,128)(2,1)}, bf16[144,512]{1,0:T(8,128)(2,1)S(1)}, u32[]{:S(2)}, u32[]{:S(2)}) collective-permute-start(bf16[144,512]{1,0:T(8,128)(2,1)} %get-tuple-element.19), channel_id=1, source_target_pairs={{0,2},{1,3},{2,0},{3,1},{4,6},{5,7},{6,4},{7,5},{8,10},{9,11},{10,... | collective-permute-start | bytes 442376 | tf_op jit(solution)/shard_map/ppermute | solution.py:705
  9.4 7.0 %collective-permute-start.4 = (bf16[144,512]{1,0:T(8,128)(2,1)}, bf16[144,512]{1,0:T(8,128)(2,1)S(1)}, u32[]{:S(2)}, u32[]{:S(2)}) collective-permute-start(bf16[144,512]{1,0:T(8,128)(2,1)} %get-tuple-element.19), channel_id=1, source_target_pairs={{0,6},{1,7},{2,4},{3,5},{4,2},{5,3},{6,0},{7,1},{8,14},{9,15},{10,... | collective-permute-start | bytes 442376 | tf_op jit(solution)/shard_map/ppermute | solution.py:705
  9.9 10.3 %collective-permute-start.1 = (bf16[144,512]{1,0:T(8,128)(2,1)}, bf16[144,512]{1,0:T(8,128)(2,1)S(1)}, u32[]{:S(2)}, u32[]{:S(2)}) collective-permute-start(bf16[144,512]{1,0:T(8,128)(2,1)} %get-tuple-element.19), channel_id=1, source_target_pairs={{0,24},{4,28},{8,0},{12,4},{16,8},{20,12},{24,16},{28,20},{1,25},{... | collective-permute-start | bytes 442376 | tf_op jit(solution)/shard_map/ppermute | solution.py:705
  16.4 1.0 %copy-start = (bf16[272,512]{1,0:T(8,128)(2,1)S(1)}, bf16[272,512]{1,0:T(8,128)(2,1)}, u32[]{:S(2)}) copy-start(bf16[272,512]{1,0:T(8,128)(2,1)} %get-tuple-element.18.both.both_ref.rest_0_) | copy-start | bytes 835588
  17.3 9.5 %copy-start.1 = (bf16[272,512]{1,0:T(8,128)(2,1)S(1)}, bf16[272,512]{1,0:T(8,128)(2,1)}, u32[]{:S(2)}) copy-start(bf16[272,512]{1,0:T(8,128)(2,1)} %get-tuple-element.18.both.both_ref.rest_0_) | copy-start | bytes 835588
  17.4 15.1 %collective-permute-start.5 = (bf16[288,512]{1,0:T(8,128)(2,1)S(1)}, bf16[288,512]{1,0:T(8,128)(2,1)S(1)}, u32[]{:S(2)}, u32[]{:S(2)}) collective-permute-start(bf16[288,512]{1,0:T(8,128)(2,1)S(1)} %shard_map.77._), channel_id=1, source_target_pairs={{0,16},{4,20},{8,24},{12,28},{16,0},{20,4},{24,8},{28,12},{1,17},{... | collective-permute-start | bytes 884744 | tf_op jit(solution)/shard_map/ppermute | solution.py:705
  20.3 11.3 %collective-permute-start.8 = (bf16[272,512]{1,0:T(8,128)(2,1)S(1)}, bf16[272,512]{1,0:T(8,128)(2,1)S(1)}, u32[]{:S(2)}, u32[]{:S(2)}) collective-permute-start(bf16[272,512]{1,0:T(8,128)(2,1)S(1)} %get-tuple-element.20.rest_1_), channel_id=1, source_target_pairs={{0,2},{1,3},{2,0},{3,1},{4,6},{5,7},{6,4},{7,5},{8,10},{9,11},{10,... | collective-permute-start | bytes 835592 | tf_op jit(solution)/shard_map/ppermute | solution.py:705
  21.8 10.3 %collective-permute-start.6 = (bf16[272,512]{1,0:T(8,128)(2,1)S(1)}, bf16[272,512]{1,0:T(8,128)(2,1)S(1)}, u32[]{:S(2)}, u32[]{:S(2)}) collective-permute-start(bf16[272,512]{1,0:T(8,128)(2,1)S(1)} %get-tuple-element.20.rest_1_), channel_id=1, source_target_pairs={{0,4},{4,0},{8,12},{12,8},{16,20},{20,16},{24,28},{28,24},{1,5},{5... | collective-permute-start | bytes 835592 | tf_op jit(solution)/shard_map/ppermute | solution.py:705
  23.4 6.0 %collective-permute-start.7 = (bf16[128,512]{1,0:T(8,128)(2,1)S(1)}, bf16[128,512]{1,0:T(8,128)(2,1)S(1)}, u32[]{:S(2)}, u32[]{:S(2)}) collective-permute-start(bf16[128,512]{1,0:T(8,128)(2,1)S(1)} %get-tuple-element.21.relay), channel_id=1, source_target_pairs={{0,8},{4,12},{24,16},{28,20},{1,9},{5,13},{25,17},{29,21},{2,10},{... | collective-permute-start | bytes 393224 | tf_op jit(solution)/shard_map/ppermute | solution.py:705
  29.5 14.0 %collective-permute-start.11 = (bf16[128,512]{1,0:T(8,128)(2,1)S(1)}, bf16[128,512]{1,0:T(8,128)(2,1)S(1)}, u32[]{:S(2)}, u32[]{:S(2)}) collective-permute-start(bf16[128,512]{1,0:T(8,128)(2,1)S(1)} %shard_map.80.rest_5_.late.refs_6_), channel_id=1, source_target_pairs={{0,6},{1,7},{2,4},{3,5},{4,2},{5,3},{6,0},{7,1},{8,14},{9,15},{10,... | collective-permute-start | bytes 393224 | tf_op jit(solution)/shard_map/ppermute | solution.py:705
  30.1 13.5 %collective-permute-start.12 = (bf16[128,512]{1,0:T(8,128)(2,1)S(1)}, bf16[128,512]{1,0:T(8,128)(2,1)S(1)}, u32[]{:S(2)}, u32[]{:S(2)}) collective-permute-start(bf16[128,512]{1,0:T(8,128)(2,1)S(1)} %shard_map.80.rest_5_.late.refs_6_), channel_id=1, source_target_pairs={{0,4},{4,0},{8,12},{12,8},{16,20},{20,16},{24,28},{28,24},{1,5},{5... | collective-permute-start | bytes 393224 | tf_op jit(solution)/shard_map/ppermute | solution.py:705
  31.6 10.7 %collective-permute-start.10 = (bf16[272,512]{1,0:T(8,128)(2,1)S(1)}, bf16[272,512]{1,0:T(8,128)(2,1)S(1)}, u32[]{:S(2)}, u32[]{:S(2)}) collective-permute-start(bf16[272,512]{1,0:T(8,128)(2,1)S(1)} %collective-permute-done.8.rest_1_.x_beside.refs_1_), channel_id=1, source_target_pairs={{0,4},{4,0},{8,12},{12,8},{16,20},{20,16},{24,28},{28,24},{1,5},{5... | collective-permute-start | bytes 835592 | tf_op jit(solution)/shard_map/ppermute | solution.py:705
  32.5 11.1 %collective-permute-start.9 = (bf16[384,512]{1,0:T(8,128)(2,1)S(1)}, bf16[384,512]{1,0:T(8,128)(2,1)S(1)}, u32[]{:S(2)}, u32[]{:S(2)}) collective-permute-start(bf16[384,512]{1,0:T(8,128)(2,1)S(1)} %shard_map.82), channel_id=1, source_target_pairs={{0,2},{1,3},{2,0},{3,1},{4,6},{5,7},{6,4},{7,5},{8,10},{9,11},{10,... | collective-permute-start | bytes 1179656 | tf_op jit(solution)/shard_map/ppermute | solution.py:705
  44.3 2.7 %collective-permute-start.13 = (bf16[1024,512]{1,0:T(8,128)(2,1)S(1)}, bf16[1024,512]{1,0:T(8,128)(2,1)S(1)}, u32[]{:S(2)}, u32[]{:S(2)}) collective-permute-start(bf16[1024,512]{1,0:T(8,128)(2,1)S(1)} %shard_map.84), channel_id=1, source_target_pairs={{0,1},{1,0},{2,3},{3,2},{4,5},{5,4},{6,7},{7,6},{8,9},{9,8},{10,11... | collective-permute-start | bytes 3145736 | tf_op jit(solution)/shard_map/ppermute | solution.py:705
